TPU v7x, 32 devices: a whole 2x2x4 slice. The times are simulated.
32 devices in a mesh: ctx: 2 (over y), exp: 16 (over z, x, core).
Axes of the slice: x: 2, y: 2, z: 4, core: 2. Of those that a mesh axis runs over, the one named last changes fastest.
Arguments:
- hidden_in: bfloat16 [16, 256, 2048], P('exp', 'ctx'), may hold values from -3 to 3
- query: bfloat16 [16, 256, 4096], P('exp', 'ctx'), may hold values from -96 to 96
- keyval: bfloat16 [16, 256, 512], P('exp', 'ctx'), may hold values from -5 to 5
- out_proj: bfloat16 [4096, 2048], P('exp'), may hold values from -0.375 to 0.375
- norm_gain: bfloat16 [2048], replicated, may hold values from 0.099609375 to 1.8984375
- expert_ids: int32 [16, 256, 8], P('exp', 'ctx'), may hold values from 0 to 15, all different within a row; in each aligned block of 128 rows (0 to 127, 128 to 255, ..., all dimensions but the last counted through in order) at most 68 rows name the same one
- gate_weights: float32 [16, 256, 8], P('exp', 'ctx'), may hold values from 0.1 to 0.4
- w_gate: bfloat16 [16, 2048, 768], P('exp'), may hold values from -0.125 to 0.125
- w_up: bfloat16 [16, 2048, 768], P('exp'), may hold values from -0.125 to 0.125
- w_down: bfloat16 [16, 768, 2048], P('exp'), may hold values from -0.21875 to 0.21875
Outputs:
- layer_out: bfloat16 [16, 256, 2048], P('exp', 'ctx')
Inputs may be any that keep to these rules, and one draw needn't show every extreme that they name: `expert_ids`: in each aligned block of 128 tokens (the tokens of one device) no expert is named by more than 68 tokens, a bound that some block reaches; a token names 8 different experts.
All inputs are finite; a program needn't handle non-finite values.
Results may differ from a plain program's by a relative error of at most 0.014.
Values may be sent and summed in bfloat16 or wider, within the bound.
No kernel may reach another device: no remote copies, remote signals or barrier semaphores. Data moves between devices by JAX's collectives and lax.ppermute only.
A program may use at most 128 MiB of HBM per device.

v0:
```python
import functools

import jax
import jax.numpy as jnp
from jax import lax
from jax.experimental import pallas as pl
from jax.experimental.pallas import tpu as pltpu
from jax.sharding import PartitionSpec as P

D = 2048
QH = 32
KVH = 2
HD = 128
TOP = 8
LANES = 128
TERMS = 3


def chip_ring(n):
    chips = n // 2
    return list(range(0, chips, 2)) + list(range(1, chips, 2))[::-1]


def device_ring(n):
    return [2 * chip + core for chip in chip_ring(n) for core in range(2)]


def core_rings(n):
    return [[2 * chip + core for chip in chip_ring(n)] for core in range(2)]


def swap_cores(block):
    n = lax.axis_size("exp")
    return lax.ppermute(block, "exp", [(i, i ^ 1) for i in range(n)])


def round_ring(block, direction):
    n = lax.axis_size("exp")
    route = []
    for ring in core_rings(n):
        route += [(ring[i], ring[(i + direction) % len(ring)]) for i in range(len(ring))]
    return lax.ppermute(block, "exp", route)


def rotate(block, axis, distance):
    if distance == 0:
        return block
    n = lax.axis_size(axis)
    return lax.ppermute(block, axis, [(i, (i + distance) % n) for i in range(n)])


def attention_kernel(places, pos_ref, query_ref, *refs):
    *kv_refs, out_ref = refs
    n_ctx = len(kv_refs)
    position = pos_ref[0]
    rows = query_ref.shape[0]
    row = lax.broadcasted_iota(jnp.int32, (rows, rows), 0)
    col = lax.broadcasted_iota(jnp.int32, (rows, rows), 1)
    visible = [row >= col]
    for back in range(1, n_ctx):
        visible.append(jnp.full((rows, rows), position, jnp.int32) >= back)
    visible = jnp.concatenate(visible, axis=1)
    for kv_head in range(KVH):
        k_at = kv_head * HD
        v_at = (KVH + kv_head) * HD
        keys = jnp.concatenate([ref[:, k_at : k_at + HD] for ref in kv_refs], axis=0)
        values = jnp.concatenate([ref[:, v_at : v_at + HD] for ref in kv_refs], axis=0)
        for group in range(QH // KVH):
            head = kv_head * (QH // KVH) + group
            scores = lax.dot_general(
                query_ref[:, head * HD : (head + 1) * HD],
                keys,
                (((1,), (1,)), ((), ())),
                preferred_element_type=jnp.float32,
            ) * HD ** (-0.5)
            scores = jnp.where(visible, scores, -1e30)
            weights = jnp.exp(scores - jnp.max(scores, axis=1, keepdims=True))
            row_sum = jnp.sum(weights, axis=1, keepdims=True)
            mixed = jnp.dot(
                weights.astype(jnp.bfloat16), values, preferred_element_type=jnp.float32
            )
            core, at = places[head]
            slot = lax.rem(core + pos_ref[1], 2)
            out_ref[slot, :, at : at + HD] = (mixed / row_sum).astype(jnp.bfloat16)


def norm_kernel(experts_all, pos_ref, hidden_ref, *refs):
    *projected_refs, gain_ref, ids_ref, gates_ref, residual_ref, tokens_ref = refs
    n_ctx = len(projected_refs)
    wide = D // n_ctx
    square_sum = None
    for back, ref in enumerate(projected_refs):
        at = pl.ds(pl.multiple_of(lax.rem(pos_ref[0] + back, n_ctx) * wide, wide), wide)
        part = hidden_ref[:, at].astype(jnp.float32) + ref[...].astype(jnp.float32)
        residual_ref[:, at] = part
        squares = jnp.sum(part * part, axis=1, keepdims=True)
        square_sum = squares if square_sum is None else square_sum + squares
    scale_inv = lax.rsqrt(square_sum * (1.0 / D) + 1e-06)
    normed = residual_ref[...] * scale_inv * gain_ref[...].astype(jnp.float32)
    tokens_ref[:, :D] = normed.astype(jnp.bfloat16)
    shape = (tokens_ref.shape[0], tokens_ref.shape[1] - D)
    column = lax.broadcasted_iota(jnp.int32, shape, 1)
    expert = lax.rem(column, experts_all)
    gates = jnp.zeros(shape, jnp.float32)
    for k in range(TOP):
        gates = gates + jnp.where(ids_ref[:, k : k + 1] == expert, gates_ref[:, k : k + 1], 0.0)
    terms = jnp.zeros(shape, jnp.float32)
    for term in range(TERMS):
        rounded = gates.astype(jnp.bfloat16).astype(jnp.float32)
        terms = jnp.where(column // experts_all == term, rounded, terms)
        gates = gates - rounded
    tokens_ref[:, D:] = terms.astype(jnp.bfloat16)


def expert_kernel(experts_all, n_chip, offsets, parts, chained, where_ref, *refs):
    groups = len(offsets)
    gate_ref, up_ref, down_ref, *refs = refs
    block_refs, refs = refs[: 2 * groups * parts], refs[2 * groups * parts + chained :]
    out_hbm, result_ref, sems = refs
    blocks = jnp.concatenate([ref[...] for ref in block_refs], axis=0)
    terms = blocks[:, D:].astype(jnp.float32)
    column = lax.broadcasted_iota(jnp.int32, terms.shape, 1)
    mine = (lax.rem(column, experts_all) == where_ref[0]) & (column < TERMS * experts_all)
    gates = jnp.sum(jnp.where(mine, terms, 0.0), axis=1, keepdims=True)
    tokens = blocks[:, :D]
    gate_pre = jnp.dot(tokens, gate_ref[...], preferred_element_type=jnp.float32)
    up_pre = jnp.dot(tokens, up_ref[...], preferred_element_type=jnp.float32)
    activated = (gate_pre / (1.0 + jnp.exp(-gate_pre)) * up_pre).astype(jnp.bfloat16)
    expert_out = jnp.dot(activated, down_ref[...], preferred_element_type=jnp.float32)
    weighted = jnp.where(gates > 0.0, expert_out * gates, 0.0).astype(jnp.bfloat16)
    rows = blocks.shape[0] // (2 * groups)
    copies = []
    for g in range(groups):
        for other in range(2):
            core = lax.rem(where_ref[1] + other, 2)
            at = pl.ds(pl.multiple_of(core * rows, rows), rows)
            start = (2 * g + other) * rows
            result_ref[g, at, :] = weighted[start : start + rows]
        place = lax.rem(where_ref[2] + offsets[g], n_chip)
        at = pl.ds(pl.multiple_of(place * (2 * rows), 2 * rows), 2 * rows)
        copies.append(pltpu.make_async_copy(result_ref.at[g], out_hbm.at[at], sems.at[g]))
        copies[-1].start()
    for copy in copies:
        copy.wait()


def vmem():
    return pl.BlockSpec(memory_space=pltpu.VMEM)


def smem():
    return pl.BlockSpec(memory_space=pltpu.SMEM)


def attend(position, core, queries, blocks, n_exp, proj_rows):
    rows = queries.shape[0]
    rings = core_rings(n_exp)
    places = {}
    for head in range(QH):
        device, inside = divmod(head * HD, proj_rows)
        places[head] = (device % 2, rings[device % 2].index(device) * proj_rows + inside)
    return pl.pallas_call(
        functools.partial(attention_kernel, places),
        out_shape=jax.ShapeDtypeStruct((2, rows, QH * HD // 2), jnp.bfloat16),
        in_specs=[smem()] + [vmem()] * (1 + len(blocks)),
        out_specs=vmem(),
        compiler_params=pltpu.CompilerParams(vmem_limit_bytes=16 * 1024 * 1024),
        name="attention",
    )(jnp.stack([position, core]), queries, *blocks)


def run_expert(experts_all, n_chip, where, chips, earlier, weights):
    groups, parts = len(chips), len(chips[0][1])
    blocks = [block for _, own, other in chips for block in own + other]
    rows = sum(block.shape[0] for block in blocks) // (2 * groups)
    offsets = [offset for offset, _, _ in chips]
    anywhere = pl.BlockSpec(memory_space=pl.ANY)
    chained = [] if earlier is None else [earlier]
    ef = weights[0].shape[1]
    return pl.pallas_call(
        functools.partial(expert_kernel, experts_all, n_chip, offsets, parts, len(chained)),
        out_shape=jax.ShapeDtypeStruct((n_chip * 2 * rows, D), jnp.bfloat16),
        in_specs=[smem()] + [vmem()] * (3 + len(blocks)) + [anywhere] * len(chained),
        out_specs=anywhere,
        scratch_shapes=[
            pltpu.VMEM((groups, 2 * rows, D), jnp.bfloat16),
            pltpu.SemaphoreType.DMA((groups,)),
        ],
        input_output_aliases={4 + len(blocks): 0} if chained else {},
        compiler_params=pltpu.CompilerParams(vmem_limit_bytes=38 * 1024 * 1024),
        cost_estimate=pl.CostEstimate(
            flops=12 * groups * rows * D * ef,
            bytes_accessed=8 * groups * rows * D + 6 * D * ef,
            transcendentals=0,
        ),
        name="experts",
    )(where, *weights, *blocks, *chained)


def body(
    hidden_in, query, keyval, out_proj, norm_gain, expert_ids, gate_weights, w_gate, w_up, w_down
):
    n_ctx = lax.axis_size("ctx")
    n_exp = lax.axis_size("exp")
    position = lax.axis_index("ctx")
    rows = hidden_in.shape[1]
    proj_rows = out_proj.shape[0]
    wide = D // n_ctx
    columns = lax.all_gather(
        lax.dynamic_slice_in_dim(out_proj, position * wide, wide, axis=1),
        "exp",
        axis=0,
        tiled=True,
        axis_index_groups=core_rings(n_exp),
    )

    def times_columns(block):
        return jnp.dot(block, columns, preferred_element_type=jnp.float32)

    core = lax.axis_index("exp") % 2
    blocks = [keyval[0]] + [rotate(keyval[0], "ctx", back) for back in range(1, n_ctx)]
    attended = attend(position, core, query[0], blocks, n_exp, proj_rows)
    own_heads, other_heads = attended[0], attended[1]
    sibling_heads = swap_cores(other_heads)
    projected = []
    for back in range(n_ctx):
        heads = [rotate(own_heads, "ctx", back), rotate(sibling_heads, "ctx", back)]
        from_sibling = swap_cores(times_columns(heads[1]).astype(jnp.bfloat16))
        part = times_columns(heads[0]) + from_sibling.astype(jnp.float32)
        if back:
            part = rotate(part.astype(jnp.bfloat16), "ctx", -back)
        projected.append(part)

    local_experts = w_gate.shape[0]
    experts_all = n_exp * local_experts
    extra = -(-TERMS * experts_all // LANES) * LANES
    residual, tokens = pl.pallas_call(
        functools.partial(norm_kernel, experts_all),
        out_shape=(
            jax.ShapeDtypeStruct((rows, D), jnp.float32),
            jax.ShapeDtypeStruct((rows, D + extra), jnp.bfloat16),
        ),
        in_specs=[smem()] + [vmem()] * (4 + n_ctx),
        out_specs=(vmem(), vmem()),
        compiler_params=pltpu.CompilerParams(vmem_limit_bytes=16 * 1024 * 1024),
        name="norm",
    )(
        position.reshape(1),
        hidden_in[0],
        *projected,
        norm_gain.reshape(1, D),
        expert_ids[0],
        gate_weights[0],
    )

    n_chip = n_exp // 2
    chip = lax.axis_index("exp") // 2
    place = jnp.where(chip % 2 == 0, chip // 2, n_chip - 1 - chip // 2)

    def experts_on(chips, earlier):
        results = []
        for local in range(local_experts):
            where = jnp.stack([lax.axis_index("exp") * local_experts + local, core, place])
            weights = (w_gate[local], w_up[local], w_down[local])
            before = None if earlier is None else earlier[local]
            results.append(run_expert(experts_all, n_chip, where, chips, before, weights))
        return results

    def send_on(forward, backward, step):
        if step < n_chip // 2:
            return round_ring(forward, 1), round_ring(backward, -1)
        return round_ring(forward[: rows // 2], 1), round_ring(backward[rows // 2 :], -1)

    forward, backward = send_on(tokens, tokens, 1)
    weighted = experts_on([(0, [tokens], [swap_cores(tokens)])], None)
    forward, backward, weighted = lax.optimization_barrier((forward, backward, weighted))
    for step in range(1, n_chip // 2):
        chips = [
            (n_chip - step, [forward], [swap_cores(forward)]),
            (step, [backward], [swap_cores(backward)]),
        ]
        forward, backward = send_on(forward, backward, step + 1)
        weighted = experts_on(chips, weighted)
        forward, backward, weighted = lax.optimization_barrier((forward, backward, weighted))
    halves = [forward, backward]
    swapped = [swap_cores(half) for half in halves]
    weighted = experts_on([(n_chip // 2, halves, swapped)], weighted)
    partial = functools.reduce(jnp.add, weighted)
    expert_sum = lax.psum_scatter(
        partial,
        "exp",
        scatter_dimension=0,
        axis_index_groups=[device_ring(n_exp)],
        tiled=True,
    )
    result = (residual + expert_sum.astype(jnp.float32)).astype(jnp.bfloat16)
    return result[None]


def solution(mesh):
    in_specs = (
        P("exp", "ctx", None),
        P("exp", "ctx", None),
        P("exp", "ctx", None),
        P("exp", None),
        P(),
        P("exp", "ctx", None),
        P("exp", "ctx", None),
        P("exp", None, None),
        P("exp", None, None),
        P("exp", None, None),
    )
    out_specs = P("exp", "ctx", None)
    return jax.shard_map(body, mesh=mesh, in_specs=in_specs, out_specs=out_specs, check_vma=False)
```

profile of v0, /device:TPU:0, one launch (start us, length us, event | category | flops | bytes accessed | tf_op | source)
XLA Modules:
  0.0 203.5 jit_solution(5566896548956784288)
XLA Ops:
  6.6 1.2 copy-done
  7.8 0.8 constant_dynamic-slice_fusion
  8.7 3.0 %collective-permute-start = (bf16[128,512]{1,0:T(8,128)(2,1)}, bf16[128,512]{1,0:T(8,128)(2,1)S(1)}, u32[]{:S(2)}, u32[]{:S(2)}) collective-permute-start(bf16[128,512]{1,0:T(8,128)(2,1)} %bitcast.45), channel_id=1, source_target_pairs={{0,16},{16,0},{1,17},{17,1},{2,18},{18,2},{3,19},{19,3},{4,20},{20... | collective-permute-start | bytes 393224 | tf_op jit(solution)/shard_map/ppermute | solution.py:49
  11.8 3.6 %collective-permute-done.refs_1_ = bf16[128,512]{1,0:T(8,128)(2,1)S(1)} collective-permute-done((bf16[128,512]{1,0:T(8,128)(2,1)}, bf16[128,512]{1,0:T(8,128)(2,1)S(1)}, u32[]{:S(2)}, u32[]{:S(2)}) %collective-permute-start) | collective-permute-done | bytes 131104 | tf_op jit(solution)/shard_map/ppermute | solution.py:49
  15.4 1.2 copy-done.7
  16.6 0.9 copy-done.9
  17.5 2.6 %attention.1 = bf16[2,128,2048]{2,1,0:T(8,128)(2,1)S(1)} custom-call(s32[2]{0:T(128)S(1)} %pad_add_fusion.pos_ref, bf16[128,4096]{1,0:T(8,128)(2,1)S(1)} %bitcast.41, bf16[128,512]{1,0:T(8,128)(2,1)S(1)} %bitcast.46, bf16[128,512]{1,0:T(8,128)(2,1)S(1)} %collective-permute-done.refs_1_), custom_call_target="tpu_custom_call" | custom-call | tf_op jit(solution)/shard_map/attention/pallas_call | solution.py:162
  20.2 0.9 slice_bitcast_fusion.1
  21.1 1.9 collective-permute-done.1
  23.0 1.7 collective-permute-start.4
  25.3 12.6 %collective-permute-done.4 = bf16[128,2048]{1,0:T(8,128)(2,1)} collective-permute-done((bf16[128,2048]{1,0:T(8,128)(2,1)S(1)}, bf16[128,2048]{1,0:T(8,128)(2,1)}, u32[]{:S(2)}, u32[]{:S(2)}) %collective-permute-start.4) | collective-permute-done | bytes 524320 | tf_op jit(solution)/shard_map/ppermute | solution.py:49
  37.9 21.7 %all-gather.2.cloned.1.call-done = bf16[2048,1024]{1,0:T(8,128)(2,1)} async-done(((bf16[256,1024]{1,0:T(8,128)(2,1)}), bf16[2048,1024]{1,0:T(8,128)(2,1)}) %all-gather.2.cloned.1.call-update) | async-done | bytes 4194320 | tf_op jit(solution)/shard_map/all_gather | solution.py:209
  59.5 3.2 %convolution_convert_fusion = bf16[128,1024]{1,0:T(8,128)(2,1)S(1)} fusion(bf16[128,2048]{1,0:T(8,128)(2,1)} %collective-permute-done.4, bf16[2048,1024]{1,0:T(8,128)(2,1)} %all-gather.2.cloned.1.call-done), kind=kOutput, calls=%fused_computation.3 | convolution fusion | flops 537001984 | bytes 4980736 | tf_op jit(solution)/shard_map/dot_general | solution.py:218
  63.1 0.7 convolution_convert_fusion.1
  64.4 0.7 fusion
  65.1 1.5 collective-permute-start.6
  66.7 0.7 convolution_add_fusion.1.refs_0_
  67.4 6.1 %collective-permute-done.6.refs_1_ = bf16[128,1024]{1,0:T(8,128)(2,1)S(1)} collective-permute-done((bf16[128,1024]{1,0:T(8,128)(2,1)S(1)}, bf16[128,1024]{1,0:T(8,128)(2,1)S(1)}, u32[]{:S(2)}, u32[]{:S(2)}) %collective-permute-start.6) | collective-permute-done | bytes 262176 | tf_op jit(solution)/shard_map/ppermute | solution.py:49
  73.5 0.5 norm.1
  74.2 1.5 collective-permute-start.7
  75.7 0.6 collective-permute-start.8
  76.3 1.9 copy-done.1
  78.2 1.9 copy-done.3
  80.1 1.9 copy-done.5
  82.0 4.2 %experts.5.refs_7_ = bf16[2048,2048]{1,0:T(8,128)(2,1)} custom-call(s32[3]{0:T(128)S(1)} %pad_add_fusion.1.where_ref, bf16[2048,768]{1,0:T(8,128)(2,1)S(1)} %bitcast.26, bf16[2048,768]{1,0:T(8,128)(2,1)S(1)} %bitcast.31, bf16[768,2048]{1,0:T(8,128)(2,1)S(1)} %bitcast.36, bf16[128,2176]{1,0:T(8,128)(2,1)S(1)} %get-tuple-element.20.refs_3_, ...), custom_call_target="tpu_custom_call" | custom-call | flops 2415919104 | bytes 11534336 | tf_op jit(solution)/shard_map/experts/pallas_call | solution.py:180
  86.2 3.1 %collective-permute-done.7.refs_3_ = bf16[128,2176]{1,0:T(8,128)(2,1)} collective-permute-done((bf16[128,2176]{1,0:T(8,128)(2,1)S(1)}, bf16[128,2176]{1,0:T(8,128)(2,1)}, u32[]{:S(2)}, u32[]{:S(2)}) %collective-permute-start.7) | collective-permute-done | bytes 557088 | tf_op jit(solution)/shard_map/ppermute | solution.py:42
  89.3 1.2 collective-permute-done.8.refs_5_
  90.5 0.5 collective-permute-start.13
  91.0 1.5 collective-permute-start.10
  92.5 0.5 collective-permute-start.11
  93.0 0.4 collective-permute-done.13.refs_6_
  93.5 7.7 %experts.6.refs_7_ = bf16[2048,2048]{1,0:T(8,128)(2,1)} custom-call(s32[3]{0:T(128)S(1)} %pad_add_fusion.1.where_ref, bf16[2048,768]{1,0:T(8,128)(2,1)S(1)} %bitcast.27, bf16[2048,768]{1,0:T(8,128)(2,1)S(1)} %bitcast.32, bf16[768,2048]{1,0:T(8,128)(2,1)S(1)} %bitcast.37, ...), custom_call_target="tpu_custom_call", output_to_operand_aliasing={{}: (8, {})} | custom-call | flops 4831838208 | bytes 13631488 | tf_op jit(solution)/shard_map/experts/pallas_call | solution.py:180
  101.2 4.6 %collective-permute-done.10.refs_3_ = bf16[128,2176]{1,0:T(8,128)(2,1)S(1)} collective-permute-done((bf16[128,2176]{1,0:T(8,128)(2,1)}, bf16[128,2176]{1,0:T(8,128)(2,1)S(1)}, u32[]{:S(2)}, u32[]{:S(2)}) %collective-permute-start.10) | collective-permute-done | bytes 557088 | tf_op jit(solution)/shard_map/ppermute | solution.py:42
  105.7 1.2 collective-permute-done.11.refs_5_
  107.0 0.5 collective-permute-start.17
  107.5 1.5 collective-permute-start.14
  108.9 0.6 collective-permute-start.15
  109.7 6.9 %experts.7.refs_7_ = bf16[2048,2048]{1,0:T(8,128)(2,1)} custom-call(s32[3]{0:T(128)S(1)} %pad_add_fusion.1.where_ref, bf16[2048,768]{1,0:T(8,128)(2,1)S(1)} %bitcast.28, bf16[2048,768]{1,0:T(8,128)(2,1)S(1)} %bitcast.33, bf16[768,2048]{1,0:T(8,128)(2,1)S(1)} %bitcast.38, ...), custom_call_target="tpu_custom_call", output_to_operand_aliasing={{}: (8, {})} | custom-call | flops 4831838208 | bytes 13631488 | tf_op jit(solution)/shard_map/experts/pallas_call | solution.py:180
  116.6 5.4 %collective-permute-done.14.refs_3_ = bf16[128,2176]{1,0:T(8,128)(2,1)S(1)} collective-permute-done((bf16[128,2176]{1,0:T(8,128)(2,1)S(1)}, bf16[128,2176]{1,0:T(8,128)(2,1)S(1)}, u32[]{:S(2)}, u32[]{:S(2)}) %collective-permute-start.14) | collective-permute-done | bytes 557088 | tf_op jit(solution)/shard_map/ppermute | solution.py:42
  122.0 1.2 collective-permute-done.15.refs_5_
  123.2 0.5 collective-permute-start.21
  123.8 0.6 collective-permute-start.18
  124.4 1.4 collective-permute-start.19
  125.9 6.9 %experts.8.refs_7_ = bf16[2048,2048]{1,0:T(8,128)(2,1)} custom-call(s32[3]{0:T(128)S(1)} %pad_add_fusion.1.where_ref, bf16[2048,768]{1,0:T(8,128)(2,1)S(1)} %bitcast.29, bf16[2048,768]{1,0:T(8,128)(2,1)S(1)} %bitcast.34, bf16[768,2048]{1,0:T(8,128)(2,1)S(1)} %bitcast.39, ...), custom_call_target="tpu_custom_call", output_to_operand_aliasing={{}: (8, {})} | custom-call | flops 4831838208 | bytes 13631488 | tf_op jit(solution)/shard_map/experts/pallas_call | solution.py:180
  133.4 1.0 collective-permute-done.22.refs_5_
  134.9 4.2 %experts.9 = bf16[2048,2048]{1,0:T(8,128)(2,1)} custom-call(s32[3]{0:T(128)S(1)} %pad_add_fusion.1.where_ref, bf16[2048,768]{1,0:T(8,128)(2,1)S(1)} %bitcast.30, bf16[2048,768]{1,0:T(8,128)(2,1)S(1)} %bitcast.35, bf16[768,2048]{1,0:T(8,128)(2,1)S(1)} %bitcast.40, ...), custom_call_target="tpu_custom_call", output_to_operand_aliasing={{}: (8, {})} | custom-call | flops 2415919104 | bytes 11534336 | tf_op jit(solution)/shard_map/experts/pallas_call | solution.py:180
  139.1 55.6 %reduce-scatter.2.cloned.1.call-done = bf16[128,2048]{1,0:T(8,128)(2,1)} async-done(((bf16[2048,2048]{1,0:T(8,128)(2,1)}), bf16[128,2048]{1,0:T(8,128)(2,1)}) %reduce-scatter.2.cloned.1.call-update) | async-done | bytes 524304 | tf_op jit(solution)/shard_map/reduce_scatter | solution.py:289
  194.7 1.9 fusion.1
  (55 shorter events, 3.1 us)
Async XLA Ops:
  6.5 1.2 copy-start
  6.5 18.2 %copy-start.11 = (s32[1,128,8]{1,2,0:T(8,128)S(1)}, s32[1,128,8]{1,2,0:T(8,128)}, u32[]{:S(2)}) copy-start(s32[1,128,8]{1,2,0:T(8,128)} %param.15) | copy-start | bytes 12292
  6.5 18.3 %copy-start.12 = (f32[1,128,8]{1,2,0:T(8,128)S(1)}, f32[1,128,8]{1,2,0:T(8,128)}, u32[]{:S(2)}) copy-start(f32[1,128,8]{1,2,0:T(8,128)} %param.16) | copy-start | bytes 12292
  6.5 18.4 %copy-start.13 = (bf16[2048]{0:T(1024)(128)(2,1)S(1)}, bf16[2048]{0:T(1024)(128)(2,1)}, u32[]{:S(2)}) copy-start(bf16[2048]{0:T(1024)(128)(2,1)} %param.14) | copy-start | bytes 12292
  6.5 53.0 %all-gather.2.cloned.1.call-start = ((), (), s32[]{:S(2)}) async-start(), calls=%async_computation.1 | async-start | bytes 4718592 | tf_op jit(solution)/shard_map/all_gather | solution.py:209
  8.6 186.1 %reduce-scatter.2.cloned.1.call-start = ((), (), s32[]{:S(2)}) async-start(), calls=%async_computation.2 | async-start | bytes 8912896 | tf_op jit(solution)/shard_map/reduce_scatter | solution.py:289
  8.7 6.7 %collective-permute-start = (bf16[128,512]{1,0:T(8,128)(2,1)}, bf16[128,512]{1,0:T(8,128)(2,1)S(1)}, u32[]{:S(2)}, u32[]{:S(2)}) collective-permute-start(bf16[128,512]{1,0:T(8,128)(2,1)} %bitcast.45), channel_id=1, source_target_pairs={{0,16},{16,0},{1,17},{17,1},{2,18},{18,2},{3,19},{19,3},{4,20},{20... | collective-permute-start | bytes 393224 | tf_op jit(solution)/shard_map/ppermute | solution.py:49
  15.4 1.2 copy-start.7
  16.6 0.9 copy-start.9
  21.1 1.9 collective-permute-start.1
  23.0 14.9 %collective-permute-start.4 = (bf16[128,2048]{1,0:T(8,128)(2,1)S(1)}, bf16[128,2048]{1,0:T(8,128)(2,1)}, u32[]{:S(2)}, u32[]{:S(2)}) collective-permute-start(bf16[128,2048]{1,0:T(8,128)(2,1)S(1)} %collective-permute-done.1), channel_id=1, source_target_pairs={{0,16},{16,0},{1,17},{17,1},{2,18},{18,2},{3,19},{19,3},{4,20},{20... | collective-permute-start | bytes 1572872 | tf_op jit(solution)/shard_map/ppermute | solution.py:49
  25.0 39.2 %collective-permute-start.3 = (bf16[128,2048]{1,0:T(8,128)(2,1)}, bf16[128,2048]{1,0:T(8,128)(2,1)S(1)}, u32[]{:S(2)}, u32[]{:S(2)}) collective-permute-start(bf16[128,2048]{1,0:T(8,128)(2,1)} %get-tuple-element.33), channel_id=1, source_target_pairs={{0,16},{16,0},{1,17},{17,1},{2,18},{18,2},{3,19},{19,3},{4,20},{20... | collective-permute-start | bytes 1572872 | tf_op jit(solution)/shard_map/ppermute | solution.py:49
  59.5 3.6 %copy-start.10 = (bf16[2048,1024]{1,0:T(8,128)(2,1)S(1)}, bf16[2048,1024]{1,0:T(8,128)(2,1)}, u32[]{:S(2)}) copy-start(bf16[2048,1024]{1,0:T(8,128)(2,1)} %all-gather.2.cloned.1.call-done) | copy-start | bytes 12582916
  62.8 1.6 collective-permute-start.5
  63.9 9.6 %copy-start.8 = (bf16[1,128,2048]{2,1,0:T(8,128)(2,1)S(1)}, bf16[1,128,2048]{2,1,0:T(8,128)(2,1)}, u32[]{:S(2)}) copy-start(bf16[1,128,2048]{2,1,0:T(8,128)(2,1)} %param.10) | copy-start | bytes 1572868
  63.9 2.7 %collective-permute-start.2 = (bf16[128,1024]{1,0:T(8,128)(2,1)S(1)}, bf16[128,1024]{1,0:T(8,128)(2,1)S(1)}, u32[]{:S(2)}, u32[]{:S(2)}) collective-permute-start(bf16[128,1024]{1,0:T(8,128)(2,1)S(1)} %convolution_convert_fusion.1), channel_id=1, source_target_pairs={{0,1},{1,0},{2,3},{3,2},{4,5},{5,4},{6,7},{7,6},{8,9},{9,8},{10,11... | collective-permute-start | bytes 786440 | tf_op jit(solution)/shard_map/ppermute | solution.py:34
  65.1 8.4 %collective-permute-start.6 = (bf16[128,1024]{1,0:T(8,128)(2,1)S(1)}, bf16[128,1024]{1,0:T(8,128)(2,1)S(1)}, u32[]{:S(2)}, u32[]{:S(2)}) collective-permute-start(bf16[128,1024]{1,0:T(8,128)(2,1)S(1)} %fusion), channel_id=1, source_target_pairs={{0,16},{16,0},{1,17},{17,1},{2,18},{18,2},{3,19},{19,3},{4,20},{20... | collective-permute-start | bytes 786440 | tf_op jit(solution)/shard_map/ppermute | solution.py:49
  74.1 2.2 %collective-permute-start.9 = (bf16[128,2176]{1,0:T(8,128)(2,1)S(1)}, bf16[128,2176]{1,0:T(8,128)(2,1)S(1)}, u32[]{:S(2)}, u32[]{:S(2)}) collective-permute-start(bf16[128,2176]{1,0:T(8,128)(2,1)S(1)} %get-tuple-element.20.refs_3_), channel_id=1, source_target_pairs={{0,1},{1,0},{2,3},{3,2},{4,5},{5,4},{6,7},{7,6},{8,9},{9,8},{10,11... | collective-permute-start | bytes 1671176 | tf_op jit(solution)/shard_map/ppermute | solution.py:34
  74.2 15.1 %collective-permute-start.7 = (bf16[128,2176]{1,0:T(8,128)(2,1)S(1)}, bf16[128,2176]{1,0:T(8,128)(2,1)}, u32[]{:S(2)}, u32[]{:S(2)}) collective-permute-start(bf16[128,2176]{1,0:T(8,128)(2,1)S(1)} %get-tuple-element.20.refs_3_), channel_id=1, source_target_pairs={{0,4},{4,8},{8,12},{12,14},{14,10},{10,6},{6,2},{2,0},{1,5},{5,9},... | collective-permute-start | bytes 1671176 | tf_op jit(solution)/shard_map/ppermute | solution.py:42
  75.7 14.8 %collective-permute-start.8 = (bf16[128,2176]{1,0:T(8,128)(2,1)S(1)}, bf16[128,2176]{1,0:T(8,128)(2,1)}, u32[]{:S(2)}, u32[]{:S(2)}) collective-permute-start(bf16[128,2176]{1,0:T(8,128)(2,1)S(1)} %get-tuple-element.20.refs_3_), channel_id=1, source_target_pairs={{0,2},{4,0},{8,4},{12,8},{14,12},{10,14},{6,10},{2,6},{1,3},{5,1},... | collective-permute-start | bytes 1671176 | tf_op jit(solution)/shard_map/ppermute | solution.py:42
  76.3 1.9 copy-start.1
  78.2 1.9 copy-start.3
  80.1 1.9 copy-start.5
  82.0 11.5 %copy-start.2 = (bf16[1,2048,768]{2,1,0:T(8,128)(2,1)S(1)}, bf16[1,2048,768]{2,1,0:T(8,128)(2,1)}, u32[]{:S(2)}) copy-start(bf16[1,2048,768]{2,1,0:T(8,128)(2,1)} %param.17) | copy-start | bytes 9437188
  82.0 11.5 %copy-start.4 = (bf16[1,2048,768]{2,1,0:T(8,128)(2,1)S(1)}, bf16[1,2048,768]{2,1,0:T(8,128)(2,1)}, u32[]{:S(2)}) copy-start(bf16[1,2048,768]{2,1,0:T(8,128)(2,1)} %param.18) | copy-start | bytes 9437188
  82.0 11.5 %copy-start.6 = (bf16[1,768,2048]{2,1,0:T(8,128)(2,1)S(1)}, bf16[1,768,2048]{2,1,0:T(8,128)(2,1)}, u32[]{:S(2)}) copy-start(bf16[1,768,2048]{2,1,0:T(8,128)(2,1)} %param.19) | copy-start | bytes 9437188
  90.5 2.5 %collective-permute-start.12 = (bf16[128,2176]{1,0:T(8,128)(2,1)}, bf16[128,2176]{1,0:T(8,128)(2,1)S(1)}, u32[]{:S(2)}, u32[]{:S(2)}) collective-permute-start(bf16[128,2176]{1,0:T(8,128)(2,1)} %collective-permute-done.7.refs_3_), channel_id=1, source_target_pairs={{0,1},{1,0},{2,3},{3,2},{4,5},{5,4},{6,7},{7,6},{8,9},{9,8},{10,11... | collective-permute-start | bytes 1671176 | tf_op jit(solution)/shard_map/ppermute | solution.py:34
  90.5 3.0 %collective-permute-start.13 = (bf16[128,2176]{1,0:T(8,128)(2,1)}, bf16[128,2176]{1,0:T(8,128)(2,1)S(1)}, u32[]{:S(2)}, u32[]{:S(2)}) collective-permute-start(bf16[128,2176]{1,0:T(8,128)(2,1)} %collective-permute-done.8.refs_5_), channel_id=1, source_target_pairs={{0,1},{1,0},{2,3},{3,2},{4,5},{5,4},{6,7},{7,6},{8,9},{9,8},{10,11... | collective-permute-start | bytes 1671176 | tf_op jit(solution)/shard_map/ppermute | solution.py:34
  91.0 14.7 %collective-permute-start.10 = (bf16[128,2176]{1,0:T(8,128)(2,1)}, bf16[128,2176]{1,0:T(8,128)(2,1)S(1)}, u32[]{:S(2)}, u32[]{:S(2)}) collective-permute-start(bf16[128,2176]{1,0:T(8,128)(2,1)} %collective-permute-done.7.refs_3_), channel_id=1, source_target_pairs={{0,4},{4,8},{8,12},{12,14},{14,10},{10,6},{6,2},{2,0},{1,5},{5,9},... | collective-permute-start | bytes 1671176 | tf_op jit(solution)/shard_map/ppermute | solution.py:42
  92.5 14.5 %collective-permute-start.11 = (bf16[128,2176]{1,0:T(8,128)(2,1)}, bf16[128,2176]{1,0:T(8,128)(2,1)S(1)}, u32[]{:S(2)}, u32[]{:S(2)}) collective-permute-start(bf16[128,2176]{1,0:T(8,128)(2,1)} %collective-permute-done.8.refs_5_), channel_id=1, source_target_pairs={{0,2},{4,0},{8,4},{12,8},{14,12},{10,14},{6,10},{2,6},{1,3},{5,1},... | collective-permute-start | bytes 1671176 | tf_op jit(solution)/shard_map/ppermute | solution.py:42
  107.0 2.5 %collective-permute-start.16 = (bf16[128,2176]{1,0:T(8,128)(2,1)S(1)}, bf16[128,2176]{1,0:T(8,128)(2,1)S(1)}, u32[]{:S(2)}, u32[]{:S(2)}) collective-permute-start(bf16[128,2176]{1,0:T(8,128)(2,1)S(1)} %collective-permute-done.10.refs_3_), channel_id=1, source_target_pairs={{0,1},{1,0},{2,3},{3,2},{4,5},{5,4},{6,7},{7,6},{8,9},{9,8},{10,11... | collective-permute-start | bytes 1671176 | tf_op jit(solution)/shard_map/ppermute | solution.py:34
  107.0 2.8 %collective-permute-start.17 = (bf16[128,2176]{1,0:T(8,128)(2,1)S(1)}, bf16[128,2176]{1,0:T(8,128)(2,1)S(1)}, u32[]{:S(2)}, u32[]{:S(2)}) collective-permute-start(bf16[128,2176]{1,0:T(8,128)(2,1)S(1)} %collective-permute-done.11.refs_5_), channel_id=1, source_target_pairs={{0,1},{1,0},{2,3},{3,2},{4,5},{5,4},{6,7},{7,6},{8,9},{9,8},{10,11... | collective-permute-start | bytes 1671176 | tf_op jit(solution)/shard_map/ppermute | solution.py:34
  107.5 14.5 %collective-permute-start.14 = (bf16[128,2176]{1,0:T(8,128)(2,1)S(1)}, bf16[128,2176]{1,0:T(8,128)(2,1)S(1)}, u32[]{:S(2)}, u32[]{:S(2)}) collective-permute-start(bf16[128,2176]{1,0:T(8,128)(2,1)S(1)} %collective-permute-done.10.refs_3_), channel_id=1, source_target_pairs={{0,4},{4,8},{8,12},{12,14},{14,10},{10,6},{6,2},{2,0},{1,5},{5,9},... | collective-permute-start | bytes 1671176 | tf_op jit(solution)/shard_map/ppermute | solution.py:42
  108.9 14.3 %collective-permute-start.15 = (bf16[128,2176]{1,0:T(8,128)(2,1)S(1)}, bf16[128,2176]{1,0:T(8,128)(2,1)S(1)}, u32[]{:S(2)}, u32[]{:S(2)}) collective-permute-start(bf16[128,2176]{1,0:T(8,128)(2,1)S(1)} %collective-permute-done.11.refs_5_), channel_id=1, source_target_pairs={{0,2},{4,0},{8,4},{12,8},{14,12},{10,14},{6,10},{2,6},{1,3},{5,1},... | collective-permute-start | bytes 1671176 | tf_op jit(solution)/shard_map/ppermute | solution.py:42
  123.2 2.6 %collective-permute-start.20 = (bf16[128,2176]{1,0:T(8,128)(2,1)S(1)}, bf16[128,2176]{1,0:T(8,128)(2,1)S(1)}, u32[]{:S(2)}, u32[]{:S(2)}) collective-permute-start(bf16[128,2176]{1,0:T(8,128)(2,1)S(1)} %collective-permute-done.14.refs_3_), channel_id=1, source_target_pairs={{0,1},{1,0},{2,3},{3,2},{4,5},{5,4},{6,7},{7,6},{8,9},{9,8},{10,11... | collective-permute-start | bytes 1671176 | tf_op jit(solution)/shard_map/ppermute | solution.py:34
  123.2 2.8 %collective-permute-start.21 = (bf16[128,2176]{1,0:T(8,128)(2,1)S(1)}, bf16[128,2176]{1,0:T(8,128)(2,1)S(1)}, u32[]{:S(2)}, u32[]{:S(2)}) collective-permute-start(bf16[128,2176]{1,0:T(8,128)(2,1)S(1)} %collective-permute-done.15.refs_5_), channel_id=1, source_target_pairs={{0,1},{1,0},{2,3},{3,2},{4,5},{5,4},{6,7},{7,6},{8,9},{9,8},{10,11... | collective-permute-start | bytes 1671176 | tf_op jit(solution)/shard_map/ppermute | solution.py:34
  123.8 9.1 %collective-permute-start.18 = (bf16[64,2176]{1,0:T(8,128)(2,1)S(1)}, bf16[64,2176]{1,0:T(8,128)(2,1)S(1)}, u32[]{:S(2)}, u32[]{:S(2)}) collective-permute-start(bf16[64,2176]{1,0:T(8,128)(2,1)S(1)} %slice.14), channel_id=1, source_target_pairs={{0,4},{4,8},{8,12},{12,14},{14,10},{10,6},{6,2},{2,0},{1,5},{5,9},... | collective-permute-start | bytes 835592 | tf_op jit(solution)/shard_map/ppermute | solution.py:42
  124.4 8.5 %collective-permute-start.19 = (bf16[64,2176]{1,0:T(8,128)(2,1)S(1)}, bf16[64,2176]{1,0:T(8,128)(2,1)S(1)}, u32[]{:S(2)}, u32[]{:S(2)}) collective-permute-start(bf16[64,2176]{1,0:T(8,128)(2,1)S(1)} %slice.15), channel_id=1, source_target_pairs={{0,2},{4,0},{8,4},{12,8},{14,12},{10,14},{6,10},{2,6},{1,3},{5,1},... | collective-permute-start | bytes 835592 | tf_op jit(solution)/shard_map/ppermute | solution.py:42
  132.9 1.6 collective-permute-start.22
  133.1 1.8 collective-permute-start.23
Sparse Core Ops, SparseCore 0:
  8.9 50.5 all-gather.1
  139.2 55.4 reduce-scatter.1
where the time goes:
time: 204 us; the launch traced here: 203 us
  waiting for transfers between devices  121 us (59%)
  Pallas kernels  33.1 us (16%)
  starting transfers between devices  17.5 us (9%)
  between operations  13.6 us (7%)
  local copies, waits for them, and re-layouts  11.3 us (6%)
  matrix products  5.45 us (3%)
  other arithmetic  2.09 us (1%)
    reduce_scatter x1, waiting for transfers between devices, body(): lax.psum_scatter(partial, 'exp', scatter_dimension=0, axis_index_groups=[...  55.6 us
    pallas_call x5, Pallas kernels, run_expert(): pl.pallas_call(functools.partial(expert_kernel, experts_all, n_chip, offs...  29.9 us
    ppermute x4, waiting for transfers between devices, rotate(): lax.ppermute(block, axis, [(i, (i + distance) % n) for i in range(n)])  22.3 us
    all_gather x1, waiting for transfers between devices, body(): lax.all_gather(lax.dynamic_slice_in_dim(out_proj, position * wide, wide,...  21.7 us
    ppermute x8, waiting for transfers between devices, round_ring(): return lax.ppermute(block, 'exp', route)  16.6 us
    unnamed x30, local copies, waits for them, and re-layouts  9.51 us
    ppermute x8, starting transfers between devices, round_ring(): return lax.ppermute(block, 'exp', route)  8.21 us
    ppermute x4, starting transfers between devices, rotate(): lax.ppermute(block, axis, [(i, (i + distance) % n) for i in range(n)])  6.66 us
  transfers between devices with their start and end apart: 26, of which 18 were waited for; matrix products, arithmetic and copies ran while one was open for 3% of the time, Pallas kernels for 14%

commit v1 on v0

--- a/solution.py
+++ b/solution.py
@@ -112,15 +112,13 @@
     tokens_ref[:, D:] = terms.astype(jnp.bfloat16)
 
 
-def expert_kernel(experts_all, n_chip, offsets, parts, chained, where_ref, *refs):
-    groups = len(offsets)
+def expert_kernel(experts_all, groups, parts, expert_ref, *refs):
     gate_ref, up_ref, down_ref, *refs = refs
-    block_refs, refs = refs[: 2 * groups * parts], refs[2 * groups * parts + chained :]
-    out_hbm, result_ref, sems = refs
+    block_refs, out_refs = refs[: 2 * groups * parts], refs[2 * groups * parts :]
     blocks = jnp.concatenate([ref[...] for ref in block_refs], axis=0)
     terms = blocks[:, D:].astype(jnp.float32)
     column = lax.broadcasted_iota(jnp.int32, terms.shape, 1)
-    mine = (lax.rem(column, experts_all) == where_ref[0]) & (column < TERMS * experts_all)
+    mine = (lax.rem(column, experts_all) == expert_ref[0]) & (column < TERMS * experts_all)
     gates = jnp.sum(jnp.where(mine, terms, 0.0), axis=1, keepdims=True)
     tokens = blocks[:, :D]
     gate_pre = jnp.dot(tokens, gate_ref[...], preferred_element_type=jnp.float32)
@@ -128,20 +126,9 @@
     activated = (gate_pre / (1.0 + jnp.exp(-gate_pre)) * up_pre).astype(jnp.bfloat16)
     expert_out = jnp.dot(activated, down_ref[...], preferred_element_type=jnp.float32)
     weighted = jnp.where(gates > 0.0, expert_out * gates, 0.0).astype(jnp.bfloat16)
-    rows = blocks.shape[0] // (2 * groups)
-    copies = []
-    for g in range(groups):
-        for other in range(2):
-            core = lax.rem(where_ref[1] + other, 2)
-            at = pl.ds(pl.multiple_of(core * rows, rows), rows)
-            start = (2 * g + other) * rows
-            result_ref[g, at, :] = weighted[start : start + rows]
-        place = lax.rem(where_ref[2] + offsets[g], n_chip)
-        at = pl.ds(pl.multiple_of(place * (2 * rows), 2 * rows), 2 * rows)
-        copies.append(pltpu.make_async_copy(result_ref.at[g], out_hbm.at[at], sems.at[g]))
-        copies[-1].start()
-    for copy in copies:
-        copy.wait()
+    rows = out_refs[0].shape[0]
+    for i, ref in enumerate(out_refs):
+        ref[...] = weighted[i * rows : (i + 1) * rows]
 
 
 def vmem():
@@ -169,24 +156,16 @@
     )(jnp.stack([position, core]), queries, *blocks)
 
 
-def run_expert(experts_all, n_chip, where, chips, earlier, weights):
-    groups, parts = len(chips), len(chips[0][1])
-    blocks = [block for _, own, other in chips for block in own + other]
+def run_expert(experts_all, expert, chips, weights):
+    groups, parts = len(chips), len(chips[0][0])
+    blocks = [block for own, other in chips for block in own + other]
     rows = sum(block.shape[0] for block in blocks) // (2 * groups)
-    offsets = [offset for offset, _, _ in chips]
-    anywhere = pl.BlockSpec(memory_space=pl.ANY)
-    chained = [] if earlier is None else [earlier]
     ef = weights[0].shape[1]
-    return pl.pallas_call(
-        functools.partial(expert_kernel, experts_all, n_chip, offsets, parts, len(chained)),
-        out_shape=jax.ShapeDtypeStruct((n_chip * 2 * rows, D), jnp.bfloat16),
-        in_specs=[smem()] + [vmem()] * (3 + len(blocks)) + [anywhere] * len(chained),
-        out_specs=anywhere,
-        scratch_shapes=[
-            pltpu.VMEM((groups, 2 * rows, D), jnp.bfloat16),
-            pltpu.SemaphoreType.DMA((groups,)),
-        ],
-        input_output_aliases={4 + len(blocks): 0} if chained else {},
+    results = pl.pallas_call(
+        functools.partial(expert_kernel, experts_all, groups, parts),
+        out_shape=[jax.ShapeDtypeStruct((rows, D), jnp.bfloat16)] * (2 * groups),
+        in_specs=[smem()] + [vmem()] * (3 + len(blocks)),
+        out_specs=[vmem()] * (2 * groups),
         compiler_params=pltpu.CompilerParams(vmem_limit_bytes=38 * 1024 * 1024),
         cost_estimate=pl.CostEstimate(
             flops=12 * groups * rows * D * ef,
@@ -194,7 +173,8 @@
             transcendentals=0,
         ),
         name="experts",
-    )(where, *weights, *blocks, *chained)
+    )(expert.reshape(1), *weights, *blocks)
+    return [(results[2 * g], results[2 * g + 1]) for g in range(groups)]
 
 
 def body(
@@ -254,47 +234,75 @@
     )
 
     n_chip = n_exp // 2
-    chip = lax.axis_index("exp") // 2
-    place = jnp.where(chip % 2 == 0, chip // 2, n_chip - 1 - chip // 2)
-
-    def experts_on(chips, earlier):
-        results = []
+    far = n_chip // 2
+    half_rows = rows // 2
+    sums = {}
+
+    def experts_on(chips):
+        offsets = [offset for offset, _, _ in chips]
+        total = None
         for local in range(local_experts):
-            where = jnp.stack([lax.axis_index("exp") * local_experts + local, core, place])
+            expert = lax.axis_index("exp") * local_experts + local
             weights = (w_gate[local], w_up[local], w_down[local])
-            before = None if earlier is None else earlier[local]
-            results.append(run_expert(experts_all, n_chip, where, chips, before, weights))
-        return results
+            pairs = run_expert(
+                experts_all, expert, [(own, other) for _, own, other in chips], weights
+            )
+            total = pairs if total is None else jax.tree.map(jnp.add, total, pairs)
+        for offset, (own, other) in zip(offsets, total):
+            sums[offset] = [own, swap_cores(other)]
+        return total
 
     def send_on(forward, backward, step):
-        if step < n_chip // 2:
+        if step < far:
             return round_ring(forward, 1), round_ring(backward, -1)
-        return round_ring(forward[: rows // 2], 1), round_ring(backward[rows // 2 :], -1)
+        return round_ring(forward[:half_rows], 1), round_ring(backward[half_rows:], -1)
+
+    def total_of(terms, half):
+        at = slice(half * half_rows, (half + 1) * half_rows)
+        terms = [term if term.shape[0] == half_rows else term[at] for term in terms]
+        return functools.reduce(jnp.add, [term.astype(jnp.float32) for term in terms])
+
+    def after(blocks, results):
+        return lax.optimization_barrier((blocks, results))[0]
 
     forward, backward = send_on(tokens, tokens, 1)
-    weighted = experts_on([(0, [tokens], [swap_cores(tokens)])], None)
-    forward, backward, weighted = lax.optimization_barrier((forward, backward, weighted))
-    for step in range(1, n_chip // 2):
+    results = experts_on([(0, [tokens], [swap_cores(tokens)])])
+    forward, backward = after((forward, backward), results)
+    for step in range(1, far):
+        earlier = list(sums.values())
         chips = [
             (n_chip - step, [forward], [swap_cores(forward)]),
             (step, [backward], [swap_cores(backward)]),
         ]
         forward, backward = send_on(forward, backward, step + 1)
-        weighted = experts_on(chips, weighted)
-        forward, backward, weighted = lax.optimization_barrier((forward, backward, weighted))
+        results = experts_on(chips)
+        forward, backward = after((forward, backward), (results, earlier))
+
+    def total_at(direction, half, hop, carried):
+        offset = hop if direction > 0 else n_chip - hop
+        return total_of(sums[offset] + carried, half).astype(jnp.bfloat16)
+
     halves = [forward, backward]
     swapped = [swap_cores(half) for half in halves]
-    weighted = experts_on([(n_chip // 2, halves, swapped)], weighted)
-    partial = functools.reduce(jnp.add, weighted)
-    expert_sum = lax.psum_scatter(
-        partial,
-        "exp",
-        scatter_dimension=0,
-        axis_index_groups=[device_ring(n_exp)],
-        tiled=True,
-    )
-    result = (residual + expert_sum.astype(jnp.float32)).astype(jnp.bfloat16)
-    return result[None]
+    ahead = [total_at(1, 1, far - 1, []), total_at(-1, 0, far - 1, [])]
+    halves, swapped, ahead = lax.optimization_barrier((halves, swapped, ahead))
+    ahead = [round_ring(ahead[0], 1), round_ring(ahead[1], -1)]
+    experts_on([(far, halves, swapped)])
+
+    def running_sum(direction, half, hops, carried):
+        for hop in range(hops, 0, -1):
+            carried = [round_ring(total_at(direction, half, hop, carried), direction)]
+        return carried
+
+    arrived = [
+        running_sum(1, 0, far, []) + running_sum(-1, 0, far - 2, ahead[1:]),
+        running_sum(1, 1, far - 2, ahead[:1]) + running_sum(-1, 1, far, []),
+    ]
+    result = [
+        total_of([residual] + sums[0] + arrived[half], half).astype(jnp.bfloat16)
+        for half in range(2)
+    ]
+    return jnp.concatenate(result, axis=0)[None]
 
 
 def solution(mesh):

time: 204 us -> 204 us (level)
  starting transfers between devices: 17.5 us -> 34 us
  Pallas kernels: 33.1 us -> 23.6 us
  local copies, waits for them, and re-layouts: 11.3 us -> 5.65 us
  waiting for transfers between devices: 121 us -> 118 us
    reduce_scatter x1 -> x0, waiting for transfers between devices: 55.6 us -> none  [body(): lax.psum_scatter(partial, 'exp', scatter_dimension=0, axis_index_groups=[...]
    ppermute x8 -> x22, waiting for transfers between devices: 16.6 us -> 66.3 us  [round_ring(): return lax.ppermute(block, 'exp', route)]
    ppermute x8 -> x22, starting transfers between devices: 8.21 us -> 23.5 us  [round_ring(): return lax.ppermute(block, 'exp', route)]
    pallas_call x5, Pallas kernels: 29.9 us -> 20.4 us  [run_expert(): pl.pallas_call(functools.partial(expert_kernel, experts_all, groups, part...]
    unnamed x30 -> x24, local copies, waits for them, and re-layouts: 9.51 us -> 3.84 us
    ppermute x12 -> x20, waiting for transfers between devices: 4.3 us -> 7.31 us  [swap_cores(): return lax.ppermute(block, 'exp', [(i, i ^ 1) for i in range(n)])]
  transfers between devices with their start and end apart: 26 -> 47, of which waited for: 18 -> 29; matrix products, arithmetic and copies ran while one was open for 3% -> 4% of each run, Pallas kernels for 14% -> 10%
where the time goes in v1:
time: 204 us
  waiting for transfers between devices  118 us (58%)
  starting transfers between devices  34 us (17%)
  Pallas kernels  23.6 us (12%)
  between operations  13.7 us (7%)
  matrix products  6.65 us (3%)
  local copies, waits for them, and re-layouts  5.65 us (3%)
  other arithmetic  2.69 us (1%)
    ppermute x22, waiting for transfers between devices, round_ring(): return lax.ppermute(block, 'exp', route)  66.3 us
    ppermute x22, starting transfers between devices, round_ring(): return lax.ppermute(block, 'exp', route)  23.5 us
    ppermute x4, waiting for transfers between devices, rotate(): lax.ppermute(block, axis, [(i, (i + distance) % n) for i in range(n)])  22.3 us
    all_gather x1, waiting for transfers between devices, body(): lax.all_gather(lax.dynamic_slice_in_dim(out_proj, position * wide, wide,...  21.7 us
    pallas_call x5, Pallas kernels, run_expert(): pl.pallas_call(functools.partial(expert_kernel, experts_all, groups, part...  20.4 us
    ppermute x20, waiting for transfers between devices, swap_cores(): return lax.ppermute(block, 'exp', [(i, i ^ 1) for i in range(n)])  7.31 us
    ppermute x4, starting transfers between devices, rotate(): lax.ppermute(block, axis, [(i, (i + distance) % n) for i in range(n)])  6.66 us
    dot_general x4, matrix products, times_columns(): return jnp.dot(block, columns, preferred_element_type=jnp.float32)  6.65 us
  transfers between devices with their start and end apart: 47, of which 29 were waited for; matrix products, arithmetic and copies ran while one was open for 4% of the time, Pallas kernels for 10%

profile of v1, /device:TPU:0, one launch (start us, length us, event | category | flops | bytes accessed | tf_op | source)
XLA Modules:
  0.0 204.0 jit_solution(17569679379408354774)
XLA Ops:
  6.6 1.2 copy-done
  8.6 3.0 %collective-permute-start = (bf16[128,512]{1,0:T(8,128)(2,1)}, bf16[128,512]{1,0:T(8,128)(2,1)S(1)}, u32[]{:S(2)}, u32[]{:S(2)}) collective-permute-start(bf16[128,512]{1,0:T(8,128)(2,1)} %bitcast.44), channel_id=1, source_target_pairs={{0,16},{16,0},{1,17},{17,1},{2,18},{18,2},{3,19},{19,3},{4,20},{20... | collective-permute-start | bytes 393224 | tf_op jit(solution)/shard_map/ppermute | solution.py:49
  11.7 3.6 %collective-permute-done.refs_1_ = bf16[128,512]{1,0:T(8,128)(2,1)S(1)} collective-permute-done((bf16[128,512]{1,0:T(8,128)(2,1)}, bf16[128,512]{1,0:T(8,128)(2,1)S(1)}, u32[]{:S(2)}, u32[]{:S(2)}) %collective-permute-start) | collective-permute-done | bytes 131104 | tf_op jit(solution)/shard_map/ppermute | solution.py:49
  15.4 1.2 copy-done.4
  16.6 0.9 copy-done.6
  17.5 2.6 %attention.1 = bf16[2,128,2048]{2,1,0:T(8,128)(2,1)S(1)} custom-call(s32[2]{0:T(128)S(1)} %pad_add_fusion.pos_ref, bf16[128,4096]{1,0:T(8,128)(2,1)S(1)} %bitcast.40, bf16[128,512]{1,0:T(8,128)(2,1)S(1)} %bitcast.45, bf16[128,512]{1,0:T(8,128)(2,1)S(1)} %collective-permute-done.refs_1_), custom_call_target="tpu_custom_call" | custom-call | tf_op jit(solution)/shard_map/attention/pallas_call | solution.py:149
  20.1 0.9 slice_bitcast_fusion.1
  21.0 1.9 collective-permute-done.1
  22.9 1.7 collective-permute-start.4
  25.3 12.6 %collective-permute-done.4 = bf16[128,2048]{1,0:T(8,128)(2,1)} collective-permute-done((bf16[128,2048]{1,0:T(8,128)(2,1)S(1)}, bf16[128,2048]{1,0:T(8,128)(2,1)}, u32[]{:S(2)}, u32[]{:S(2)}) %collective-permute-start.4) | collective-permute-done | bytes 524320 | tf_op jit(solution)/shard_map/ppermute | solution.py:49
  37.8 21.7 %all-gather.2.cloned.1.call-done = bf16[2048,1024]{1,0:T(8,128)(2,1)} async-done(((bf16[256,1024]{1,0:T(8,128)(2,1)}), bf16[2048,1024]{1,0:T(8,128)(2,1)}) %all-gather.2.cloned.1.call-update) | async-done | bytes 4194320 | tf_op jit(solution)/shard_map/all_gather | solution.py:189
  59.5 3.2 %convolution_convert_fusion = bf16[128,1024]{1,0:T(8,128)(2,1)S(1)} fusion(bf16[128,2048]{1,0:T(8,128)(2,1)} %collective-permute-done.4, bf16[2048,1024]{1,0:T(8,128)(2,1)} %all-gather.2.cloned.1.call-done), kind=kOutput, calls=%fused_computation.3 | convolution fusion | flops 537001984 | bytes 4980736 | tf_op jit(solution)/shard_map/dot_general | solution.py:198
  64.4 1.9 fusion
  66.3 1.5 collective-permute-start.6
  68.6 6.1 %collective-permute-done.6.refs_1_ = bf16[128,1024]{1,0:T(8,128)(2,1)S(1)} collective-permute-done((bf16[128,1024]{1,0:T(8,128)(2,1)S(1)}, bf16[128,1024]{1,0:T(8,128)(2,1)S(1)}, u32[]{:S(2)}, u32[]{:S(2)}) %collective-permute-start.6) | collective-permute-done | bytes 262176 | tf_op jit(solution)/shard_map/ppermute | solution.py:49
  75.4 1.5 collective-permute-start.10
  77.5 2.6 %experts.5 = (bf16[128,2048]{1,0:T(8,128)(2,1)S(1)}, bf16[128,2048]{1,0:T(8,128)(2,1)S(1)}) custom-call(s32[1]{0:T(128)} %bitcast.9.expert_ref, bf16[2048,768]{1,0:T(8,128)(2,1)S(1)} %bitcast.25, bf16[2048,768]{1,0:T(8,128)(2,1)S(1)} %bitcast.30, bf16[768,2048]{1,0:T(8,128)(2,1)S(1)} %bitcast.35, bf16[128,2176]{1,0:T(8,128)(2,1)S(1)} %get-tuple-element.38.refs_3_, ...), custom_call_target="tpu_custom_call" | custom-call | flops 2415919104 | bytes 11534336 | tf_op jit(solution)/shard_map/experts/pallas_call | solution.py:164
  80.1 10.3 %collective-permute-done.10.refs_5_ = bf16[128,2176]{1,0:T(8,128)(2,1)S(1)} collective-permute-done((bf16[128,2176]{1,0:T(8,128)(2,1)S(1)}, bf16[128,2176]{1,0:T(8,128)(2,1)S(1)}, u32[]{:S(2)}, u32[]{:S(2)}) %collective-permute-start.10) | collective-permute-done | bytes 557088 | tf_op jit(solution)/shard_map/ppermute | solution.py:42
  90.4 1.2 collective-permute-done.9.refs_3_
  92.7 1.5 collective-permute-start.15
  94.4 5.1 %experts.6 = (bf16[128,2048]{1,0:T(8,128)(2,1)S(1)}, bf16[128,2048]{1,0:T(8,128)(2,1)S(1)}, bf16[128,2048]{1,0:T(8,128)(2,1)S(1)}, bf16[128,2048]{1,0:T(8,128)(2,1)S(1)}) custom-call(s32[1]{0:T(128)} %bitcast.9.expert_ref, bf16[2048,768]{1,0:T(8,128)(2,1)S(1)} %bitcast.26, bf16[2048,768]{1,0:T(8,128)(2,1)S(1)} %bitcast.31, bf16[768,2048]{1,0:T(8,128)(2,1)S(1)} %bitcast.36, ...), custom_call_target="tpu_custom_call" | custom-call | flops 4831838208 | bytes 13631488 | tf_op jit(solution)/shard_map/experts/pallas_call | solution.py:164
  99.5 7.2 %collective-permute-done.14.refs_3_ = bf16[128,2176]{1,0:T(8,128)(2,1)S(1)} collective-permute-done((bf16[128,2176]{1,0:T(8,128)(2,1)S(1)}, bf16[128,2176]{1,0:T(8,128)(2,1)S(1)}, u32[]{:S(2)}, u32[]{:S(2)}) %collective-permute-start.14) | collective-permute-done | bytes 557088 | tf_op jit(solution)/shard_map/ppermute | solution.py:42
  107.5 1.5 collective-permute-start.19
  110.0 5.1 %experts.7 = (bf16[128,2048]{1,0:T(8,128)(2,1)S(1)}, bf16[128,2048]{1,0:T(8,128)(2,1)S(1)}, bf16[128,2048]{1,0:T(8,128)(2,1)S(1)}, bf16[128,2048]{1,0:T(8,128)(2,1)S(1)}) custom-call(s32[1]{0:T(128)} %bitcast.9.expert_ref, bf16[2048,768]{1,0:T(8,128)(2,1)S(1)} %bitcast.27, bf16[2048,768]{1,0:T(8,128)(2,1)S(1)} %bitcast.32, bf16[768,2048]{1,0:T(8,128)(2,1)S(1)} %bitcast.37, ...), custom_call_target="tpu_custom_call" | custom-call | flops 4831838208 | bytes 13631488 | tf_op jit(solution)/shard_map/experts/pallas_call | solution.py:164
  115.1 6.9 %collective-permute-done.19.refs_3_ = bf16[128,2176]{1,0:T(8,128)(2,1)S(1)} collective-permute-done((bf16[128,2176]{1,0:T(8,128)(2,1)S(1)}, bf16[128,2176]{1,0:T(8,128)(2,1)S(1)}, u32[]{:S(2)}, u32[]{:S(2)}) %collective-permute-start.19) | collective-permute-done | bytes 557088 | tf_op jit(solution)/shard_map/ppermute | solution.py:42
  122.0 1.2 collective-permute-done.20.refs_5_
  124.2 0.9 collective-permute-done.22.refs_4_
  125.9 5.1 %experts.8 = (bf16[128,2048]{1,0:T(8,128)(2,1)S(1)}, bf16[128,2048]{1,0:T(8,128)(2,1)S(1)}, bf16[128,2048]{1,0:T(8,128)(2,1)S(1)}, bf16[128,2048]{1,0:T(8,128)(2,1)S(1)}) custom-call(s32[1]{0:T(128)} %bitcast.9.expert_ref, bf16[2048,768]{1,0:T(8,128)(2,1)S(1)} %bitcast.28, bf16[2048,768]{1,0:T(8,128)(2,1)S(1)} %bitcast.33, bf16[768,2048]{1,0:T(8,128)(2,1)S(1)} %bitcast.38, ...), custom_call_target="tpu_custom_call" | custom-call | flops 4831838208 | bytes 13631488 | tf_op jit(solution)/shard_map/experts/pallas_call | solution.py:164
  131.9 1.7 collective-permute-start.25
  133.6 6.6 %collective-permute-done.26.refs_4_ = bf16[64,2176]{1,0:T(8,128)(2,1)S(1)} collective-permute-done((bf16[64,2176]{1,0:T(8,128)(2,1)S(1)}, bf16[64,2176]{1,0:T(8,128)(2,1)S(1)}, u32[]{:S(2)}, u32[]{:S(2)}) %collective-permute-start.26) | collective-permute-done | bytes 278560 | tf_op jit(solution)/shard_map/ppermute | solution.py:42
  142.9 2.6 %experts.9 = (bf16[128,2048]{1,0:T(8,128)(2,1)S(1)}, bf16[128,2048]{1,0:T(8,128)(2,1)S(1)}) custom-call(s32[1]{0:T(128)} %bitcast.9.expert_ref, bf16[2048,768]{1,0:T(8,128)(2,1)S(1)} %bitcast.29, bf16[2048,768]{1,0:T(8,128)(2,1)S(1)} %bitcast.34, bf16[768,2048]{1,0:T(8,128)(2,1)S(1)} %bitcast.39, bf16[64,2176]{1,0:T(8,128)(2,1)S(1)} %collective-permute-done.25.refs_3_, ...), custom_call_target="tpu_custom_call" | custom-call | flops 2415919104 | bytes 11534336 | tf_op jit(solution)/shard_map/experts/pallas_call | solution.py:164
  145.7 1.8 collective-permute-done.31
  147.6 1.5 collective-permute-start.32
  149.7 1.5 collective-permute-start.39
  151.8 5.1 %collective-permute-done.32 = bf16[64,2048]{1,0:T(8,128)(2,1)S(1)} collective-permute-done((bf16[64,2048]{1,0:T(8,128)(2,1)S(1)}, bf16[64,2048]{1,0:T(8,128)(2,1)S(1)}, u32[]{:S(2)}, u32[]{:S(2)}) %collective-permute-start.32) | collective-permute-done | bytes 262176 | tf_op jit(solution)/shard_map/ppermute | solution.py:42
  156.9 1.5 collective-permute-start.33
  158.5 4.4 %collective-permute-done.42 = bf16[64,2048]{1,0:T(8,128)(2,1)S(1)} collective-permute-done((bf16[64,2048]{1,0:T(8,128)(2,1)S(1)}, bf16[64,2048]{1,0:T(8,128)(2,1)S(1)}, u32[]{:S(2)}, u32[]{:S(2)}) %collective-permute-start.42) | collective-permute-done | bytes 262176 | tf_op jit(solution)/shard_map/ppermute | solution.py:42
  163.6 3.7 %collective-permute-done.33 = bf16[64,2048]{1,0:T(8,128)(2,1)S(1)} collective-permute-done((bf16[64,2048]{1,0:T(8,128)(2,1)S(1)}, bf16[64,2048]{1,0:T(8,128)(2,1)S(1)}, u32[]{:S(2)}, u32[]{:S(2)}) %collective-permute-start.33) | collective-permute-done | bytes 262176 | tf_op jit(solution)/shard_map/ppermute | solution.py:42
  167.5 1.5 collective-permute-start.34
  169.1 1.5 collective-permute-start.40
  171.4 1.0 collective-permute-start.44
  172.4 4.4 %collective-permute-done.34 = bf16[64,2048]{1,0:T(8,128)(2,1)S(1)} collective-permute-done((bf16[64,2048]{1,0:T(8,128)(2,1)S(1)}, bf16[64,2048]{1,0:T(8,128)(2,1)S(1)}, u32[]{:S(2)}, u32[]{:S(2)}) %collective-permute-start.34) | collective-permute-done | bytes 262176 | tf_op jit(solution)/shard_map/ppermute | solution.py:42
  176.8 3.9 %collective-permute-done.40 = bf16[64,2048]{1,0:T(8,128)(2,1)S(1)} collective-permute-done((bf16[64,2048]{1,0:T(8,128)(2,1)S(1)}, bf16[64,2048]{1,0:T(8,128)(2,1)S(1)}, u32[]{:S(2)}, u32[]{:S(2)}) %collective-permute-start.40) | collective-permute-done | bytes 262176 | tf_op jit(solution)/shard_map/ppermute | solution.py:42
  181.0 1.5 collective-permute-start.35
  182.5 1.5 collective-permute-start.41
  185.4 4.9 %collective-permute-done.35 = bf16[64,2048]{1,0:T(8,128)(2,1)S(1)} collective-permute-done((bf16[64,2048]{1,0:T(8,128)(2,1)S(1)}, bf16[64,2048]{1,0:T(8,128)(2,1)S(1)}, u32[]{:S(2)}, u32[]{:S(2)}) %collective-permute-start.35) | collective-permute-done | bytes 262176 | tf_op jit(solution)/shard_map/ppermute | solution.py:42
  190.3 3.0 %collective-permute-done.41 = bf16[64,2048]{1,0:T(8,128)(2,1)S(1)} collective-permute-done((bf16[64,2048]{1,0:T(8,128)(2,1)S(1)}, bf16[64,2048]{1,0:T(8,128)(2,1)S(1)}, u32[]{:S(2)}, u32[]{:S(2)}) %collective-permute-start.41) | collective-permute-done | bytes 262176 | tf_op jit(solution)/shard_map/ppermute | solution.py:42
  193.2 2.7 %collective-permute-done.45 = bf16[64,2048]{1,0:T(8,128)(2,1)S(1)} collective-permute-done((bf16[64,2048]{1,0:T(8,128)(2,1)S(1)}, bf16[64,2048]{1,0:T(8,128)(2,1)S(1)}, u32[]{:S(2)}, u32[]{:S(2)}) %collective-permute-start.45) | collective-permute-done | bytes 262176 | tf_op jit(solution)/shard_map/ppermute | solution.py:42
  (99 shorter events, 19.7 us)
Async XLA Ops:
  6.5 18.3 %copy-start.10 = (f32[1,128,8]{1,2,0:T(8,128)S(1)}, f32[1,128,8]{1,2,0:T(8,128)}, u32[]{:S(2)}) copy-start(f32[1,128,8]{1,2,0:T(8,128)} %param.16) | copy-start | bytes 12292
  6.5 53.0 %all-gather.2.cloned.1.call-start = ((), (), s32[]{:S(2)}) async-start(), calls=%async_computation | async-start | bytes 4718592 | tf_op jit(solution)/shard_map/all_gather | solution.py:189
  8.6 6.7 %collective-permute-start = (bf16[128,512]{1,0:T(8,128)(2,1)}, bf16[128,512]{1,0:T(8,128)(2,1)S(1)}, u32[]{:S(2)}, u32[]{:S(2)}) collective-permute-start(bf16[128,512]{1,0:T(8,128)(2,1)} %bitcast.44), channel_id=1, source_target_pairs={{0,16},{16,0},{1,17},{17,1},{2,18},{18,2},{3,19},{19,3},{4,20},{20... | collective-permute-start | bytes 393224 | tf_op jit(solution)/shard_map/ppermute | solution.py:49
  21.0 1.9 collective-permute-start.1
  22.9 14.9 %collective-permute-start.4 = (bf16[128,2048]{1,0:T(8,128)(2,1)S(1)}, bf16[128,2048]{1,0:T(8,128)(2,1)}, u32[]{:S(2)}, u32[]{:S(2)}) collective-permute-start(bf16[128,2048]{1,0:T(8,128)(2,1)S(1)} %collective-permute-done.1), channel_id=1, source_target_pairs={{0,16},{16,0},{1,17},{17,1},{2,18},{18,2},{3,19},{19,3},{4,20},{20... | collective-permute-start | bytes 1572872 | tf_op jit(solution)/shard_map/ppermute | solution.py:49
  24.9 39.3 %collective-permute-start.3 = (bf16[128,2048]{1,0:T(8,128)(2,1)}, bf16[128,2048]{1,0:T(8,128)(2,1)}, u32[]{:S(2)}, u32[]{:S(2)}) collective-permute-start(bf16[128,2048]{1,0:T(8,128)(2,1)} %get-tuple-element.81), channel_id=1, source_target_pairs={{0,16},{16,0},{1,17},{17,1},{2,18},{18,2},{3,19},{19,3},{4,20},{20... | collective-permute-start | bytes 1572872 | tf_op jit(solution)/shard_map/ppermute | solution.py:49
  62.8 1.6 collective-permute-start.5
  63.9 4.0 %collective-permute-start.2 = (bf16[128,1024]{1,0:T(8,128)(2,1)S(1)}, bf16[128,1024]{1,0:T(8,128)(2,1)S(1)}, u32[]{:S(2)}, u32[]{:S(2)}) collective-permute-start(bf16[128,1024]{1,0:T(8,128)(2,1)S(1)} %convolution_convert_fusion.1), channel_id=1, source_target_pairs={{0,1},{1,0},{2,3},{3,2},{4,5},{5,4},{6,7},{7,6},{8,9},{9,8},{10,11... | collective-permute-start | bytes 786440 | tf_op jit(solution)/shard_map/ppermute | solution.py:34
  66.3 8.4 %collective-permute-start.6 = (bf16[128,1024]{1,0:T(8,128)(2,1)S(1)}, bf16[128,1024]{1,0:T(8,128)(2,1)S(1)}, u32[]{:S(2)}, u32[]{:S(2)}) collective-permute-start(bf16[128,1024]{1,0:T(8,128)(2,1)S(1)} %fusion), channel_id=1, source_target_pairs={{0,16},{16,0},{1,17},{17,1},{2,18},{18,2},{3,19},{19,3},{4,20},{20... | collective-permute-start | bytes 786440 | tf_op jit(solution)/shard_map/ppermute | solution.py:49
  75.3 2.2 %collective-permute-start.7 = (bf16[128,2176]{1,0:T(8,128)(2,1)S(1)}, bf16[128,2176]{1,0:T(8,128)(2,1)S(1)}, u32[]{:S(2)}, u32[]{:S(2)}) collective-permute-start(bf16[128,2176]{1,0:T(8,128)(2,1)S(1)} %get-tuple-element.38.refs_3_), channel_id=1, source_target_pairs={{0,1},{1,0},{2,3},{3,2},{4,5},{5,4},{6,7},{7,6},{8,9},{9,8},{10,11... | collective-permute-start | bytes 1671176 | tf_op jit(solution)/shard_map/ppermute | solution.py:34
  75.4 15.0 %collective-permute-start.10 = (bf16[128,2176]{1,0:T(8,128)(2,1)S(1)}, bf16[128,2176]{1,0:T(8,128)(2,1)S(1)}, u32[]{:S(2)}, u32[]{:S(2)}) collective-permute-start(bf16[128,2176]{1,0:T(8,128)(2,1)S(1)} %get-tuple-element.38.refs_3_), channel_id=1, source_target_pairs={{0,2},{4,0},{8,4},{12,8},{14,12},{10,14},{6,10},{2,6},{1,3},{5,1},... | collective-permute-start | bytes 1671176 | tf_op jit(solution)/shard_map/ppermute | solution.py:42
  76.9 14.7 %collective-permute-start.9 = (bf16[128,2176]{1,0:T(8,128)(2,1)S(1)}, bf16[128,2176]{1,0:T(8,128)(2,1)S(1)}, u32[]{:S(2)}, u32[]{:S(2)}) collective-permute-start(bf16[128,2176]{1,0:T(8,128)(2,1)S(1)} %get-tuple-element.38.refs_3_), channel_id=1, source_target_pairs={{0,4},{4,8},{8,12},{12,14},{14,10},{10,6},{6,2},{2,0},{1,5},{5,9},... | collective-permute-start | bytes 1671176 | tf_op jit(solution)/shard_map/ppermute | solution.py:42
  91.6 2.5 %collective-permute-start.11 = (bf16[128,2176]{1,0:T(8,128)(2,1)S(1)}, bf16[128,2176]{1,0:T(8,128)(2,1)S(1)}, u32[]{:S(2)}, u32[]{:S(2)}) collective-permute-start(bf16[128,2176]{1,0:T(8,128)(2,1)S(1)} %collective-permute-done.9.refs_3_), channel_id=1, source_target_pairs={{0,1},{1,0},{2,3},{3,2},{4,5},{5,4},{6,7},{7,6},{8,9},{9,8},{10,11... | collective-permute-start | bytes 1671176 | tf_op jit(solution)/shard_map/ppermute | solution.py:34
  91.6 2.8 %collective-permute-start.12 = (bf16[128,2176]{1,0:T(8,128)(2,1)S(1)}, bf16[128,2176]{1,0:T(8,128)(2,1)S(1)}, u32[]{:S(2)}, u32[]{:S(2)}) collective-permute-start(bf16[128,2176]{1,0:T(8,128)(2,1)S(1)} %collective-permute-done.10.refs_5_), channel_id=1, source_target_pairs={{0,1},{1,0},{2,3},{3,2},{4,5},{5,4},{6,7},{7,6},{8,9},{9,8},{10,11... | collective-permute-start | bytes 1671176 | tf_op jit(solution)/shard_map/ppermute | solution.py:34
  92.1 14.5 %collective-permute-start.14 = (bf16[128,2176]{1,0:T(8,128)(2,1)S(1)}, bf16[128,2176]{1,0:T(8,128)(2,1)S(1)}, u32[]{:S(2)}, u32[]{:S(2)}) collective-permute-start(bf16[128,2176]{1,0:T(8,128)(2,1)S(1)} %collective-permute-done.9.refs_3_), channel_id=1, source_target_pairs={{0,4},{4,8},{8,12},{12,14},{14,10},{10,6},{6,2},{2,0},{1,5},{5,9},... | collective-permute-start | bytes 1671176 | tf_op jit(solution)/shard_map/ppermute | solution.py:42
  92.7 14.3 %collective-permute-start.15 = (bf16[128,2176]{1,0:T(8,128)(2,1)S(1)}, bf16[128,2176]{1,0:T(8,128)(2,1)S(1)}, u32[]{:S(2)}, u32[]{:S(2)}) collective-permute-start(bf16[128,2176]{1,0:T(8,128)(2,1)S(1)} %collective-permute-done.10.refs_5_), channel_id=1, source_target_pairs={{0,2},{4,0},{8,4},{12,8},{14,12},{10,14},{6,10},{2,6},{1,3},{5,1},... | collective-permute-start | bytes 1671176 | tf_op jit(solution)/shard_map/ppermute | solution.py:42
  94.2 5.3 %collective-permute-start.8 = (bf16[128,2048]{1,0:T(8,128)(2,1)S(1)}, bf16[128,2048]{1,0:T(8,128)(2,1)S(1)}, u32[]{:S(2)}, u32[]{:S(2)}) collective-permute-start(bf16[128,2048]{1,0:T(8,128)(2,1)S(1)} %get-tuple-element.40), channel_id=1, source_target_pairs={{0,1},{1,0},{2,3},{3,2},{4,5},{5,4},{6,7},{7,6},{8,9},{9,8},{10,11... | collective-permute-start | bytes 1572872 | tf_op jit(solution)/shard_map/ppermute | solution.py:34
  106.9 2.5 %collective-permute-start.16 = (bf16[128,2176]{1,0:T(8,128)(2,1)S(1)}, bf16[128,2176]{1,0:T(8,128)(2,1)S(1)}, u32[]{:S(2)}, u32[]{:S(2)}) collective-permute-start(bf16[128,2176]{1,0:T(8,128)(2,1)S(1)} %collective-permute-done.14.refs_3_), channel_id=1, source_target_pairs={{0,1},{1,0},{2,3},{3,2},{4,5},{5,4},{6,7},{7,6},{8,9},{9,8},{10,11... | collective-permute-start | bytes 1671176 | tf_op jit(solution)/shard_map/ppermute | solution.py:34
  106.9 3.1 %collective-permute-start.17 = (bf16[128,2176]{1,0:T(8,128)(2,1)S(1)}, bf16[128,2176]{1,0:T(8,128)(2,1)S(1)}, u32[]{:S(2)}, u32[]{:S(2)}) collective-permute-start(bf16[128,2176]{1,0:T(8,128)(2,1)S(1)} %collective-permute-done.15.refs_5_), channel_id=1, source_target_pairs={{0,1},{1,0},{2,3},{3,2},{4,5},{5,4},{6,7},{7,6},{8,9},{9,8},{10,11... | collective-permute-start | bytes 1671176 | tf_op jit(solution)/shard_map/ppermute | solution.py:34
  107.5 14.5 %collective-permute-start.19 = (bf16[128,2176]{1,0:T(8,128)(2,1)S(1)}, bf16[128,2176]{1,0:T(8,128)(2,1)S(1)}, u32[]{:S(2)}, u32[]{:S(2)}) collective-permute-start(bf16[128,2176]{1,0:T(8,128)(2,1)S(1)} %collective-permute-done.14.refs_3_), channel_id=1, source_target_pairs={{0,4},{4,8},{8,12},{12,14},{14,10},{10,6},{6,2},{2,0},{1,5},{5,9},... | collective-permute-start | bytes 1671176 | tf_op jit(solution)/shard_map/ppermute | solution.py:42
  108.9 14.3 %collective-permute-start.20 = (bf16[128,2176]{1,0:T(8,128)(2,1)S(1)}, bf16[128,2176]{1,0:T(8,128)(2,1)S(1)}, u32[]{:S(2)}, u32[]{:S(2)}) collective-permute-start(bf16[128,2176]{1,0:T(8,128)(2,1)S(1)} %collective-permute-done.15.refs_5_), channel_id=1, source_target_pairs={{0,2},{4,0},{8,4},{12,8},{14,12},{10,14},{6,10},{2,6},{1,3},{5,1},... | collective-permute-start | bytes 1671176 | tf_op jit(solution)/shard_map/ppermute | solution.py:42
  109.5 5.6 %collective-permute-start.13 = (bf16[128,2048]{1,0:T(8,128)(2,1)S(1)}, bf16[128,2048]{1,0:T(8,128)(2,1)S(1)}, u32[]{:S(2)}, u32[]{:S(2)}) collective-permute-start(bf16[128,2048]{1,0:T(8,128)(2,1)S(1)} %get-tuple-element.44), channel_id=1, source_target_pairs={{0,1},{1,0},{2,3},{3,2},{4,5},{5,4},{6,7},{7,6},{8,9},{9,8},{10,11... | collective-permute-start | bytes 1572872 | tf_op jit(solution)/shard_map/ppermute | solution.py:34
  109.5 5.6 %collective-permute-start.21 = (bf16[128,2048]{1,0:T(8,128)(2,1)S(1)}, bf16[128,2048]{1,0:T(8,128)(2,1)S(1)}, u32[]{:S(2)}, u32[]{:S(2)}) collective-permute-start(bf16[128,2048]{1,0:T(8,128)(2,1)S(1)} %get-tuple-element.46), channel_id=1, source_target_pairs={{0,1},{1,0},{2,3},{3,2},{4,5},{5,4},{6,7},{7,6},{8,9},{9,8},{10,11... | collective-permute-start | bytes 1572872 | tf_op jit(solution)/shard_map/ppermute | solution.py:34
  123.2 2.0 collective-permute-start.22
  123.2 2.8 %collective-permute-start.23 = (bf16[128,2176]{1,0:T(8,128)(2,1)S(1)}, bf16[128,2176]{1,0:T(8,128)(2,1)S(1)}, u32[]{:S(2)}, u32[]{:S(2)}) collective-permute-start(bf16[128,2176]{1,0:T(8,128)(2,1)S(1)} %collective-permute-done.20.refs_5_), channel_id=1, source_target_pairs={{0,1},{1,0},{2,3},{3,2},{4,5},{5,4},{6,7},{7,6},{8,9},{9,8},{10,11... | collective-permute-start | bytes 1671176 | tf_op jit(solution)/shard_map/ppermute | solution.py:34
  123.7 17.1 %collective-permute-start.18 = (bf16[128,2048]{1,0:T(8,128)(2,1)S(1)}, bf16[128,2048]{1,0:T(8,128)(2,1)S(1)}, u32[]{:S(2)}, u32[]{:S(2)}) collective-permute-start(bf16[128,2048]{1,0:T(8,128)(2,1)S(1)} %get-tuple-element.50), channel_id=1, source_target_pairs={{0,1},{1,0},{2,3},{3,2},{4,5},{5,4},{6,7},{7,6},{8,9},{9,8},{10,11... | collective-permute-start | bytes 1572872 | tf_op jit(solution)/shard_map/ppermute | solution.py:34
  123.7 17.1 %collective-permute-start.27 = (bf16[128,2048]{1,0:T(8,128)(2,1)S(1)}, bf16[128,2048]{1,0:T(8,128)(2,1)S(1)}, u32[]{:S(2)}, u32[]{:S(2)}) collective-permute-start(bf16[128,2048]{1,0:T(8,128)(2,1)S(1)} %get-tuple-element.52), channel_id=1, source_target_pairs={{0,1},{1,0},{2,3},{3,2},{4,5},{5,4},{6,7},{7,6},{8,9},{9,8},{10,11... | collective-permute-start | bytes 1572872 | tf_op jit(solution)/shard_map/ppermute | solution.py:34
  131.0 10.3 %collective-permute-start.24 = (bf16[128,2048]{1,0:T(8,128)(2,1)S(1)}, bf16[128,2048]{1,0:T(8,128)(2,1)S(1)}, u32[]{:S(2)}, u32[]{:S(2)}) collective-permute-start(bf16[128,2048]{1,0:T(8,128)(2,1)S(1)} %get-tuple-element.56), channel_id=1, source_target_pairs={{0,1},{1,0},{2,3},{3,2},{4,5},{5,4},{6,7},{7,6},{8,9},{9,8},{10,11... | collective-permute-start | bytes 1572872 | tf_op jit(solution)/shard_map/ppermute | solution.py:34
  131.2 9.0 %collective-permute-start.26 = (bf16[64,2176]{1,0:T(8,128)(2,1)S(1)}, bf16[64,2176]{1,0:T(8,128)(2,1)S(1)}, u32[]{:S(2)}, u32[]{:S(2)}) collective-permute-start(bf16[64,2176]{1,0:T(8,128)(2,1)S(1)} %slice.126), channel_id=1, source_target_pairs={{0,2},{4,0},{8,4},{12,8},{14,12},{10,14},{6,10},{2,6},{1,3},{5,1},... | collective-permute-start | bytes 835592 | tf_op jit(solution)/shard_map/ppermute | solution.py:42
  131.9 8.9 %collective-permute-start.25 = (bf16[64,2176]{1,0:T(8,128)(2,1)S(1)}, bf16[64,2176]{1,0:T(8,128)(2,1)S(1)}, u32[]{:S(2)}, u32[]{:S(2)}) collective-permute-start(bf16[64,2176]{1,0:T(8,128)(2,1)S(1)} %slice.125), channel_id=1, source_target_pairs={{0,4},{4,8},{8,12},{12,14},{14,10},{10,6},{6,2},{2,0},{1,5},{5,9},... | collective-permute-start | bytes 835592 | tf_op jit(solution)/shard_map/ppermute | solution.py:42
  140.2 1.9 collective-permute-start.30
  140.8 1.7 collective-permute-start.28
  140.8 2.1 %collective-permute-start.29 = (bf16[64,2176]{1,0:T(8,128)(2,1)S(1)}, bf16[64,2176]{1,0:T(8,128)(2,1)S(1)}, u32[]{:S(2)}, u32[]{:S(2)}) collective-permute-start(bf16[64,2176]{1,0:T(8,128)(2,1)S(1)} %collective-permute-done.26.refs_4_), channel_id=1, source_target_pairs={{0,1},{1,0},{2,3},{3,2},{4,5},{5,4},{6,7},{7,6},{8,9},{9,8},{10,11... | collective-permute-start | bytes 835592 | tf_op jit(solution)/shard_map/ppermute | solution.py:34
  145.5 2.0 collective-permute-start.31
  147.6 9.2 %collective-permute-start.32 = (bf16[64,2048]{1,0:T(8,128)(2,1)S(1)}, bf16[64,2048]{1,0:T(8,128)(2,1)S(1)}, u32[]{:S(2)}, u32[]{:S(2)}) collective-permute-start(bf16[64,2048]{1,0:T(8,128)(2,1)S(1)} %get-tuple-element.75), channel_id=1, source_target_pairs={{0,4},{4,8},{8,12},{12,14},{14,10},{10,6},{6,2},{2,0},{1,5},{5,9},... | collective-permute-start | bytes 786440 | tf_op jit(solution)/shard_map/ppermute | solution.py:42
  149.2 21.4 %collective-permute-start.36 = (bf16[64,2048]{1,0:T(8,128)(2,1)S(1)}, bf16[64,2048]{1,0:T(8,128)(2,1)S(1)}, u32[]{:S(2)}, u32[]{:S(2)}) collective-permute-start(bf16[64,2048]{1,0:T(8,128)(2,1)S(1)} %add_convert_fusion.14), channel_id=1, source_target_pairs={{0,2},{4,0},{8,4},{12,8},{14,12},{10,14},{6,10},{2,6},{1,3},{5,1},... | collective-permute-start | bytes 786440 | tf_op jit(solution)/shard_map/ppermute | solution.py:42
  149.7 13.8 %collective-permute-start.39 = (bf16[64,2048]{1,0:T(8,128)(2,1)S(1)}, bf16[64,2048]{1,0:T(8,128)(2,1)S(1)}, u32[]{:S(2)}, u32[]{:S(2)}) collective-permute-start(bf16[64,2048]{1,0:T(8,128)(2,1)S(1)} %add_convert_fusion.15), channel_id=1, source_target_pairs={{0,4},{4,8},{8,12},{12,14},{14,10},{10,6},{6,2},{2,0},{1,5},{5,9},... | collective-permute-start | bytes 786440 | tf_op jit(solution)/shard_map/ppermute | solution.py:42
  151.2 11.7 %collective-permute-start.42 = (bf16[64,2048]{1,0:T(8,128)(2,1)S(1)}, bf16[64,2048]{1,0:T(8,128)(2,1)S(1)}, u32[]{:S(2)}, u32[]{:S(2)}) collective-permute-start(bf16[64,2048]{1,0:T(8,128)(2,1)S(1)} %get-tuple-element.76), channel_id=1, source_target_pairs={{0,2},{4,0},{8,4},{12,8},{14,12},{10,14},{6,10},{2,6},{1,3},{5,1},... | collective-permute-start | bytes 786440 | tf_op jit(solution)/shard_map/ppermute | solution.py:42
  156.9 10.3 %collective-permute-start.33 = (bf16[64,2048]{1,0:T(8,128)(2,1)S(1)}, bf16[64,2048]{1,0:T(8,128)(2,1)S(1)}, u32[]{:S(2)}, u32[]{:S(2)}) collective-permute-start(bf16[64,2048]{1,0:T(8,128)(2,1)S(1)} %add_convert_fusion.12), channel_id=1, source_target_pairs={{0,4},{4,8},{8,12},{12,14},{14,10},{10,6},{6,2},{2,0},{1,5},{5,9},... | collective-permute-start | bytes 786440 | tf_op jit(solution)/shard_map/ppermute | solution.py:42
  163.0 7.6 %collective-permute-start.43 = (bf16[64,2048]{1,0:T(8,128)(2,1)S(1)}, bf16[64,2048]{1,0:T(8,128)(2,1)S(1)}, u32[]{:S(2)}, u32[]{:S(2)}) collective-permute-start(bf16[64,2048]{1,0:T(8,128)(2,1)S(1)} %add_convert_fusion.3), channel_id=1, source_target_pairs={{0,2},{4,0},{8,4},{12,8},{14,12},{10,14},{6,10},{2,6},{1,3},{5,1},... | collective-permute-start | bytes 786440 | tf_op jit(solution)/shard_map/ppermute | solution.py:42
  167.5 9.3 %collective-permute-start.34 = (bf16[64,2048]{1,0:T(8,128)(2,1)S(1)}, bf16[64,2048]{1,0:T(8,128)(2,1)S(1)}, u32[]{:S(2)}, u32[]{:S(2)}) collective-permute-start(bf16[64,2048]{1,0:T(8,128)(2,1)S(1)} %get-tuple-element.73), channel_id=1, source_target_pairs={{0,4},{4,8},{8,12},{12,14},{14,10},{10,6},{6,2},{2,0},{1,5},{5,9},... | collective-permute-start | bytes 786440 | tf_op jit(solution)/shard_map/ppermute | solution.py:42
  169.1 11.7 %collective-permute-start.40 = (bf16[64,2048]{1,0:T(8,128)(2,1)S(1)}, bf16[64,2048]{1,0:T(8,128)(2,1)S(1)}, u32[]{:S(2)}, u32[]{:S(2)}) collective-permute-start(bf16[64,2048]{1,0:T(8,128)(2,1)S(1)} %get-tuple-element.74), channel_id=1, source_target_pairs={{0,4},{4,8},{8,12},{12,14},{14,10},{10,6},{6,2},{2,0},{1,5},{5,9},... | collective-permute-start | bytes 786440 | tf_op jit(solution)/shard_map/ppermute | solution.py:42
  170.8 13.2 %collective-permute-start.37 = (bf16[64,2048]{1,0:T(8,128)(2,1)S(1)}, bf16[64,2048]{1,0:T(8,128)(2,1)S(1)}, u32[]{:S(2)}, u32[]{:S(2)}) collective-permute-start(bf16[64,2048]{1,0:T(8,128)(2,1)S(1)} %get-tuple-element.79), channel_id=1, source_target_pairs={{0,2},{4,0},{8,4},{12,8},{14,12},{10,14},{6,10},{2,6},{1,3},{5,1},... | collective-permute-start | bytes 786440 | tf_op jit(solution)/shard_map/ppermute | solution.py:42
  171.4 12.6 %collective-permute-start.44 = (bf16[64,2048]{1,0:T(8,128)(2,1)S(1)}, bf16[64,2048]{1,0:T(8,128)(2,1)S(1)}, u32[]{:S(2)}, u32[]{:S(2)}) collective-permute-start(bf16[64,2048]{1,0:T(8,128)(2,1)S(1)} %get-tuple-element.80), channel_id=1, source_target_pairs={{0,2},{4,0},{8,4},{12,8},{14,12},{10,14},{6,10},{2,6},{1,3},{5,1},... | collective-permute-start | bytes 786440 | tf_op jit(solution)/shard_map/ppermute | solution.py:42
  181.0 9.3 %collective-permute-start.35 = (bf16[64,2048]{1,0:T(8,128)(2,1)S(1)}, bf16[64,2048]{1,0:T(8,128)(2,1)S(1)}, u32[]{:S(2)}, u32[]{:S(2)}) collective-permute-start(bf16[64,2048]{1,0:T(8,128)(2,1)S(1)} %get-tuple-element.71), channel_id=1, source_target_pairs={{0,4},{4,8},{8,12},{12,14},{14,10},{10,6},{6,2},{2,0},{1,5},{5,9},... | collective-permute-start | bytes 786440 | tf_op jit(solution)/shard_map/ppermute | solution.py:42
  182.5 10.7 %collective-permute-start.41 = (bf16[64,2048]{1,0:T(8,128)(2,1)S(1)}, bf16[64,2048]{1,0:T(8,128)(2,1)S(1)}, u32[]{:S(2)}, u32[]{:S(2)}) collective-permute-start(bf16[64,2048]{1,0:T(8,128)(2,1)S(1)} %get-tuple-element.72), channel_id=1, source_target_pairs={{0,4},{4,8},{8,12},{12,14},{14,10},{10,6},{6,2},{2,0},{1,5},{5,9},... | collective-permute-start | bytes 786440 | tf_op jit(solution)/shard_map/ppermute | solution.py:42
  184.2 9.0 %collective-permute-start.38 = (bf16[64,2048]{1,0:T(8,128)(2,1)S(1)}, bf16[64,2048]{1,0:T(8,128)(2,1)S(1)}, u32[]{:S(2)}, u32[]{:S(2)}) collective-permute-start(bf16[64,2048]{1,0:T(8,128)(2,1)S(1)} %get-tuple-element.77), channel_id=1, source_target_pairs={{0,2},{4,0},{8,4},{12,8},{14,12},{10,14},{6,10},{2,6},{1,3},{5,1},... | collective-permute-start | bytes 786440 | tf_op jit(solution)/shard_map/ppermute | solution.py:42
  184.8 11.1 %collective-permute-start.45 = (bf16[64,2048]{1,0:T(8,128)(2,1)S(1)}, bf16[64,2048]{1,0:T(8,128)(2,1)S(1)}, u32[]{:S(2)}, u32[]{:S(2)}) collective-permute-start(bf16[64,2048]{1,0:T(8,128)(2,1)S(1)} %get-tuple-element.78), channel_id=1, source_target_pairs={{0,2},{4,0},{8,4},{12,8},{14,12},{10,14},{6,10},{2,6},{1,3},{5,1},... | collective-permute-start | bytes 786440 | tf_op jit(solution)/shard_map/ppermute | solution.py:42
  (10 other events, 89.6 us)
Sparse Core Ops, SparseCore 0:
  8.9 50.5 all-gather.1

commit v2 on v1

--- a/solution.py
+++ b/solution.py
@@ -248,9 +248,10 @@
                 experts_all, expert, [(own, other) for _, own, other in chips], weights
             )
             total = pairs if total is None else jax.tree.map(jnp.add, total, pairs)
-        for offset, (own, other) in zip(offsets, total):
-            sums[offset] = [own, swap_cores(other)]
-        return total
+        return dict(zip(offsets, total))
+
+    def swap_results(results):
+        return {offset: [own, swap_cores(other)] for offset, (own, other) in results.items()}
 
     def send_on(forward, backward, step):
         if step < far:
@@ -262,41 +263,38 @@
         terms = [term if term.shape[0] == half_rows else term[at] for term in terms]
         return functools.reduce(jnp.add, [term.astype(jnp.float32) for term in terms])
 
-    def after(blocks, results):
-        return lax.optimization_barrier((blocks, results))[0]
-
+    barrier = lax.optimization_barrier
     forward, backward = send_on(tokens, tokens, 1)
     results = experts_on([(0, [tokens], [swap_cores(tokens)])])
-    forward, backward = after((forward, backward), results)
+    forward, backward, results = barrier((forward, backward, results))
     for step in range(1, far):
-        earlier = list(sums.values())
         chips = [
             (n_chip - step, [forward], [swap_cores(forward)]),
             (step, [backward], [swap_cores(backward)]),
         ]
         forward, backward = send_on(forward, backward, step + 1)
+        sums |= swap_results(results)
         results = experts_on(chips)
-        forward, backward = after((forward, backward), (results, earlier))
+        forward, backward, results, sums = barrier((forward, backward, results, sums))
+    halves = [forward, backward]
+    swapped = [swap_cores(half) for half in halves]
+    sums |= swap_results(results)
+    halves, swapped, sums = barrier((halves, swapped, sums))
+    sums |= swap_results(experts_on([(far, halves, swapped)]))
 
     def total_at(direction, half, hop, carried):
         offset = hop if direction > 0 else n_chip - hop
         return total_of(sums[offset] + carried, half).astype(jnp.bfloat16)
 
-    halves = [forward, backward]
-    swapped = [swap_cores(half) for half in halves]
-    ahead = [total_at(1, 1, far - 1, []), total_at(-1, 0, far - 1, [])]
-    halves, swapped, ahead = lax.optimization_barrier((halves, swapped, ahead))
-    ahead = [round_ring(ahead[0], 1), round_ring(ahead[1], -1)]
-    experts_on([(far, halves, swapped)])
-
-    def running_sum(direction, half, hops, carried):
+    def running_sum(direction, half, hops):
+        carried = []
         for hop in range(hops, 0, -1):
             carried = [round_ring(total_at(direction, half, hop, carried), direction)]
         return carried
 
     arrived = [
-        running_sum(1, 0, far, []) + running_sum(-1, 0, far - 2, ahead[1:]),
-        running_sum(1, 1, far - 2, ahead[:1]) + running_sum(-1, 1, far, []),
+        running_sum(1, 0, far) + running_sum(-1, 0, far - 1),
+        running_sum(1, 1, far - 1) + running_sum(-1, 1, far),
     ]
     result = [
         total_of([residual] + sums[0] + arrived[half], half).astype(jnp.bfloat16)

time: 204 us -> 199 us (0.975)
  waiting for transfers between devices: 118 us -> 113 us
    ppermute x22, waiting for transfers between devices: 66.3 us -> 62.2 us  [round_ring(): return lax.ppermute(block, 'exp', route)]
  transfers between devices with their start and end apart: 47 -> 47, of which waited for: 29 -> 27; matrix products, arithmetic and copies ran while one was open for 4% -> 5% of each run, Pallas kernels for 10% -> 10%
where the time goes in v2:
time: 199 us
  waiting for transfers between devices  113 us (57%)
  starting transfers between devices  33.4 us (17%)
  Pallas kernels  23.6 us (12%)
  between operations  13.7 us (7%)
  matrix products  6.65 us (3%)
  local copies, waits for them, and re-layouts  5.66 us (3%)
  other arithmetic  2.72 us (1%)
    ppermute x22, waiting for transfers between devices, round_ring(): return lax.ppermute(block, 'exp', route)  62.2 us
    ppermute x22, starting transfers between devices, round_ring(): return lax.ppermute(block, 'exp', route)  22.5 us
    ppermute x4, waiting for transfers between devices, rotate(): lax.ppermute(block, axis, [(i, (i + distance) % n) for i in range(n)])  22.3 us
    all_gather x1, waiting for transfers between devices, body(): lax.all_gather(lax.dynamic_slice_in_dim(out_proj, position * wide, wide,...  21.7 us
    pallas_call x5, Pallas kernels, run_expert(): pl.pallas_call(functools.partial(expert_kernel, experts_all, groups, part...  20.4 us
    ppermute x20, waiting for transfers between devices, swap_cores(): return lax.ppermute(block, 'exp', [(i, i ^ 1) for i in range(n)])  6.78 us
    ppermute x4, starting transfers between devices, rotate(): lax.ppermute(block, axis, [(i, (i + distance) % n) for i in range(n)])  6.67 us
    dot_general x4, matrix products, times_columns(): return jnp.dot(block, columns, preferred_element_type=jnp.float32)  6.65 us
  transfers between devices with their start and end apart: 47, of which 27 were waited for; matrix products, arithmetic and copies ran while one was open for 5% of the time, Pallas kernels for 10%

profile of v2, /device:TPU:0, one launch (start us, length us, event | category | flops | bytes accessed | tf_op | source)
XLA Modules:
  0.0 198.7 jit_solution(13935548157996694865)
XLA Ops:
  6.6 1.2 copy-done
  8.6 3.0 %collective-permute-start = (bf16[128,512]{1,0:T(8,128)(2,1)}, bf16[128,512]{1,0:T(8,128)(2,1)S(1)}, u32[]{:S(2)}, u32[]{:S(2)}) collective-permute-start(bf16[128,512]{1,0:T(8,128)(2,1)} %bitcast.44), channel_id=1, source_target_pairs={{0,16},{16,0},{1,17},{17,1},{2,18},{18,2},{3,19},{19,3},{4,20},{20... | collective-permute-start | bytes 393224 | tf_op jit(solution)/shard_map/ppermute | solution.py:49
  11.7 3.6 %collective-permute-done.refs_1_ = bf16[128,512]{1,0:T(8,128)(2,1)S(1)} collective-permute-done((bf16[128,512]{1,0:T(8,128)(2,1)}, bf16[128,512]{1,0:T(8,128)(2,1)S(1)}, u32[]{:S(2)}, u32[]{:S(2)}) %collective-permute-start) | collective-permute-done | bytes 131104 | tf_op jit(solution)/shard_map/ppermute | solution.py:49
  15.4 1.2 copy-done.4
  17.5 2.6 %attention.1 = bf16[2,128,2048]{2,1,0:T(8,128)(2,1)S(1)} custom-call(s32[2]{0:T(128)S(1)} %pad_add_fusion.pos_ref, bf16[128,4096]{1,0:T(8,128)(2,1)S(1)} %bitcast.40, bf16[128,512]{1,0:T(8,128)(2,1)S(1)} %bitcast.45, bf16[128,512]{1,0:T(8,128)(2,1)S(1)} %collective-permute-done.refs_1_), custom_call_target="tpu_custom_call" | custom-call | tf_op jit(solution)/shard_map/attention/pallas_call | solution.py:149
  20.1 0.9 slice_bitcast_fusion.1
  21.1 1.9 collective-permute-done.1
  23.0 1.7 collective-permute-start.4
  25.3 12.6 %collective-permute-done.4 = bf16[128,2048]{1,0:T(8,128)(2,1)} collective-permute-done((bf16[128,2048]{1,0:T(8,128)(2,1)S(1)}, bf16[128,2048]{1,0:T(8,128)(2,1)}, u32[]{:S(2)}, u32[]{:S(2)}) %collective-permute-start.4) | collective-permute-done | bytes 524320 | tf_op jit(solution)/shard_map/ppermute | solution.py:49
  37.8 21.7 %all-gather.2.cloned.1.call-done = bf16[2048,1024]{1,0:T(8,128)(2,1)} async-done(((bf16[256,1024]{1,0:T(8,128)(2,1)}), bf16[2048,1024]{1,0:T(8,128)(2,1)}) %all-gather.2.cloned.1.call-update) | async-done | bytes 4194320 | tf_op jit(solution)/shard_map/all_gather | solution.py:189
  59.5 3.2 %convolution_convert_fusion = bf16[128,1024]{1,0:T(8,128)(2,1)S(1)} fusion(bf16[128,2048]{1,0:T(8,128)(2,1)} %collective-permute-done.4, bf16[2048,1024]{1,0:T(8,128)(2,1)} %all-gather.2.cloned.1.call-done), kind=kOutput, calls=%fused_computation.3 | convolution fusion | flops 537001984 | bytes 4980736 | tf_op jit(solution)/shard_map/dot_general | solution.py:198
  64.4 1.9 fusion
  66.3 1.5 collective-permute-start.6
  68.6 6.1 %collective-permute-done.6.refs_1_ = bf16[128,1024]{1,0:T(8,128)(2,1)S(1)} collective-permute-done((bf16[128,1024]{1,0:T(8,128)(2,1)S(1)}, bf16[128,1024]{1,0:T(8,128)(2,1)S(1)}, u32[]{:S(2)}, u32[]{:S(2)}) %collective-permute-start.6) | collective-permute-done | bytes 262176 | tf_op jit(solution)/shard_map/ppermute | solution.py:49
  75.4 1.5 collective-permute-start.7
  77.5 2.6 %experts.5 = (bf16[128,2048]{1,0:T(8,128)(2,1)S(1)}, bf16[128,2048]{1,0:T(8,128)(2,1)S(1)}) custom-call(s32[1]{0:T(128)} %bitcast.9.expert_ref, bf16[2048,768]{1,0:T(8,128)(2,1)S(1)} %bitcast.25, bf16[2048,768]{1,0:T(8,128)(2,1)S(1)} %bitcast.30, bf16[768,2048]{1,0:T(8,128)(2,1)S(1)} %bitcast.35, bf16[128,2176]{1,0:T(8,128)(2,1)S(1)} %get-tuple-element.82.refs_3_, ...), custom_call_target="tpu_custom_call" | custom-call | flops 2415919104 | bytes 11534336 | tf_op jit(solution)/shard_map/experts/pallas_call | solution.py:164
  80.1 10.3 %collective-permute-done.7.refs_3_ = bf16[128,2176]{1,0:T(8,128)(2,1)S(1)} collective-permute-done((bf16[128,2176]{1,0:T(8,128)(2,1)S(1)}, bf16[128,2176]{1,0:T(8,128)(2,1)S(1)}, u32[]{:S(2)}, u32[]{:S(2)}) %collective-permute-start.7) | collective-permute-done | bytes 557088 | tf_op jit(solution)/shard_map/ppermute | solution.py:42
  90.4 1.2 collective-permute-done.8.refs_5_
  92.1 1.5 collective-permute-start.10
  94.4 5.1 %experts.6 = (bf16[128,2048]{1,0:T(8,128)(2,1)S(1)}, bf16[128,2048]{1,0:T(8,128)(2,1)S(1)}, bf16[128,2048]{1,0:T(8,128)(2,1)S(1)}, bf16[128,2048]{1,0:T(8,128)(2,1)S(1)}) custom-call(s32[1]{0:T(128)} %bitcast.9.expert_ref, bf16[2048,768]{1,0:T(8,128)(2,1)S(1)} %bitcast.26, bf16[2048,768]{1,0:T(8,128)(2,1)S(1)} %bitcast.31, bf16[768,2048]{1,0:T(8,128)(2,1)S(1)} %bitcast.36, ...), custom_call_target="tpu_custom_call" | custom-call | flops 4831838208 | bytes 13631488 | tf_op jit(solution)/shard_map/experts/pallas_call | solution.py:164
  99.4 7.2 %collective-permute-done.10.refs_3_ = bf16[128,2176]{1,0:T(8,128)(2,1)S(1)} collective-permute-done((bf16[128,2176]{1,0:T(8,128)(2,1)S(1)}, bf16[128,2176]{1,0:T(8,128)(2,1)S(1)}, u32[]{:S(2)}, u32[]{:S(2)}) %collective-permute-start.10) | collective-permute-done | bytes 557088 | tf_op jit(solution)/shard_map/ppermute | solution.py:42
  106.7 1.2 collective-permute-done.11.refs_5_
  108.4 1.5 collective-permute-start.15
  110.9 5.1 %experts.7 = (bf16[128,2048]{1,0:T(8,128)(2,1)S(1)}, bf16[128,2048]{1,0:T(8,128)(2,1)S(1)}, bf16[128,2048]{1,0:T(8,128)(2,1)S(1)}, bf16[128,2048]{1,0:T(8,128)(2,1)S(1)}) custom-call(s32[1]{0:T(128)} %bitcast.9.expert_ref, bf16[2048,768]{1,0:T(8,128)(2,1)S(1)} %bitcast.27, bf16[2048,768]{1,0:T(8,128)(2,1)S(1)} %bitcast.32, bf16[768,2048]{1,0:T(8,128)(2,1)S(1)} %bitcast.37, ...), custom_call_target="tpu_custom_call" | custom-call | flops 4831838208 | bytes 13631488 | tf_op jit(solution)/shard_map/experts/pallas_call | solution.py:164
  116.0 6.9 %collective-permute-done.15.refs_3_ = bf16[128,2176]{1,0:T(8,128)(2,1)S(1)} collective-permute-done((bf16[128,2176]{1,0:T(8,128)(2,1)S(1)}, bf16[128,2176]{1,0:T(8,128)(2,1)S(1)}, u32[]{:S(2)}, u32[]{:S(2)}) %collective-permute-start.15) | collective-permute-done | bytes 557088 | tf_op jit(solution)/shard_map/ppermute | solution.py:42
  122.9 1.2 collective-permute-done.16.refs_5_
  126.1 1.2 collective-permute-start.22
  127.3 5.1 %experts.8 = (bf16[128,2048]{1,0:T(8,128)(2,1)S(1)}, bf16[128,2048]{1,0:T(8,128)(2,1)S(1)}, bf16[128,2048]{1,0:T(8,128)(2,1)S(1)}, bf16[128,2048]{1,0:T(8,128)(2,1)S(1)}) custom-call(s32[1]{0:T(128)} %bitcast.9.expert_ref, bf16[2048,768]{1,0:T(8,128)(2,1)S(1)} %bitcast.28, bf16[2048,768]{1,0:T(8,128)(2,1)S(1)} %bitcast.33, bf16[768,2048]{1,0:T(8,128)(2,1)S(1)} %bitcast.38, ...), custom_call_target="tpu_custom_call" | custom-call | flops 4831838208 | bytes 13631488 | tf_op jit(solution)/shard_map/experts/pallas_call | solution.py:164
  132.3 1.5 collective-permute-done.21.refs_3_
  133.8 1.0 collective-permute-done.22.refs_4_
  135.8 2.0 %collective-permute-done.27.refs_5_ = bf16[64,2176]{1,0:T(8,128)(2,1)S(1)} collective-permute-done((bf16[64,2176]{1,0:T(8,128)(2,1)S(1)}, bf16[64,2176]{1,0:T(8,128)(2,1)S(1)}, u32[]{:S(2)}, u32[]{:S(2)}) %collective-permute-start.27) | collective-permute-done | bytes 278560 | tf_op jit(solution)/shard_map/ppermute | solution.py:34
  138.2 2.6 %experts.9 = (bf16[128,2048]{1,0:T(8,128)(2,1)S(1)}, bf16[128,2048]{1,0:T(8,128)(2,1)S(1)}) custom-call(s32[1]{0:T(128)} %bitcast.9.expert_ref, bf16[2048,768]{1,0:T(8,128)(2,1)S(1)} %bitcast.29, bf16[2048,768]{1,0:T(8,128)(2,1)S(1)} %bitcast.34, bf16[768,2048]{1,0:T(8,128)(2,1)S(1)} %bitcast.39, bf16[64,2176]{1,0:T(8,128)(2,1)S(1)} %collective-permute-done.21.refs_3_, ...), custom_call_target="tpu_custom_call" | custom-call | flops 2415919104 | bytes 11534336 | tf_op jit(solution)/shard_map/experts/pallas_call | solution.py:164
  141.1 1.8 collective-permute-done.31
  143.8 1.2 collective-permute-start.42
  145.0 6.3 %collective-permute-done.32 = bf16[64,2048]{1,0:T(8,128)(2,1)S(1)} collective-permute-done((bf16[64,2048]{1,0:T(8,128)(2,1)S(1)}, bf16[64,2048]{1,0:T(8,128)(2,1)S(1)}, u32[]{:S(2)}, u32[]{:S(2)}) %collective-permute-start.32) | collective-permute-done | bytes 262176 | tf_op jit(solution)/shard_map/ppermute | solution.py:42
  152.4 1.2 collective-permute-start.39
  154.7 1.2 collective-permute-start.43
  155.9 4.9 %collective-permute-done.33 = bf16[64,2048]{1,0:T(8,128)(2,1)S(1)} collective-permute-done((bf16[64,2048]{1,0:T(8,128)(2,1)S(1)}, bf16[64,2048]{1,0:T(8,128)(2,1)S(1)}, u32[]{:S(2)}, u32[]{:S(2)}) %collective-permute-start.33) | collective-permute-done | bytes 262176 | tf_op jit(solution)/shard_map/ppermute | solution.py:42
  160.8 3.9 %collective-permute-done.39 = bf16[64,2048]{1,0:T(8,128)(2,1)S(1)} collective-permute-done((bf16[64,2048]{1,0:T(8,128)(2,1)S(1)}, bf16[64,2048]{1,0:T(8,128)(2,1)S(1)}, u32[]{:S(2)}, u32[]{:S(2)}) %collective-permute-start.39) | collective-permute-done | bytes 262176 | tf_op jit(solution)/shard_map/ppermute | solution.py:42
  165.8 1.2 collective-permute-start.40
  168.2 1.2 collective-permute-start.44
  169.4 4.9 %collective-permute-done.34 = bf16[64,2048]{1,0:T(8,128)(2,1)S(1)} collective-permute-done((bf16[64,2048]{1,0:T(8,128)(2,1)S(1)}, bf16[64,2048]{1,0:T(8,128)(2,1)S(1)}, u32[]{:S(2)}, u32[]{:S(2)}) %collective-permute-start.34) | collective-permute-done | bytes 262176 | tf_op jit(solution)/shard_map/ppermute | solution.py:42
  174.3 3.0 %collective-permute-done.40 = bf16[64,2048]{1,0:T(8,128)(2,1)S(1)} collective-permute-done((bf16[64,2048]{1,0:T(8,128)(2,1)S(1)}, bf16[64,2048]{1,0:T(8,128)(2,1)S(1)}, u32[]{:S(2)}, u32[]{:S(2)}) %collective-permute-start.40) | collective-permute-done | bytes 262176 | tf_op jit(solution)/shard_map/ppermute | solution.py:42
  178.4 1.2 collective-permute-start.41
  180.7 1.2 collective-permute-start.45
  181.9 4.1 %collective-permute-done.35 = bf16[64,2048]{1,0:T(8,128)(2,1)S(1)} collective-permute-done((bf16[64,2048]{1,0:T(8,128)(2,1)S(1)}, bf16[64,2048]{1,0:T(8,128)(2,1)S(1)}, u32[]{:S(2)}, u32[]{:S(2)}) %collective-permute-start.35) | collective-permute-done | bytes 262176 | tf_op jit(solution)/shard_map/ppermute | solution.py:42
  186.0 2.8 %collective-permute-done.41 = bf16[64,2048]{1,0:T(8,128)(2,1)S(1)} collective-permute-done((bf16[64,2048]{1,0:T(8,128)(2,1)S(1)}, bf16[64,2048]{1,0:T(8,128)(2,1)S(1)}, u32[]{:S(2)}, u32[]{:S(2)}) %collective-permute-start.41) | collective-permute-done | bytes 262176 | tf_op jit(solution)/shard_map/ppermute | solution.py:42
  188.8 1.8 collective-permute-done.45
  (97 shorter events, 21.1 us)
Async XLA Ops:
  6.5 18.4 %copy-start.10 = (bf16[2048]{0:T(1024)(128)(2,1)S(1)}, bf16[2048]{0:T(1024)(128)(2,1)}, u32[]{:S(2)}) copy-start(bf16[2048]{0:T(1024)(128)(2,1)} %param.14) | copy-start | bytes 12292
  6.5 53.0 %all-gather.2.cloned.1.call-start = ((), (), s32[]{:S(2)}) async-start(), calls=%async_computation | async-start | bytes 4718592 | tf_op jit(solution)/shard_map/all_gather | solution.py:189
  8.6 6.7 %collective-permute-start = (bf16[128,512]{1,0:T(8,128)(2,1)}, bf16[128,512]{1,0:T(8,128)(2,1)S(1)}, u32[]{:S(2)}, u32[]{:S(2)}) collective-permute-start(bf16[128,512]{1,0:T(8,128)(2,1)} %bitcast.44), channel_id=1, source_target_pairs={{0,16},{16,0},{1,17},{17,1},{2,18},{18,2},{3,19},{19,3},{4,20},{20... | collective-permute-start | bytes 393224 | tf_op jit(solution)/shard_map/ppermute | solution.py:49
  21.0 1.9 collective-permute-start.1
  23.0 14.9 %collective-permute-start.4 = (bf16[128,2048]{1,0:T(8,128)(2,1)S(1)}, bf16[128,2048]{1,0:T(8,128)(2,1)}, u32[]{:S(2)}, u32[]{:S(2)}) collective-permute-start(bf16[128,2048]{1,0:T(8,128)(2,1)S(1)} %collective-permute-done.1), channel_id=1, source_target_pairs={{0,16},{16,0},{1,17},{17,1},{2,18},{18,2},{3,19},{19,3},{4,20},{20... | collective-permute-start | bytes 1572872 | tf_op jit(solution)/shard_map/ppermute | solution.py:49
  24.9 39.2 %collective-permute-start.3 = (bf16[128,2048]{1,0:T(8,128)(2,1)}, bf16[128,2048]{1,0:T(8,128)(2,1)}, u32[]{:S(2)}, u32[]{:S(2)}) collective-permute-start(bf16[128,2048]{1,0:T(8,128)(2,1)} %get-tuple-element.173), channel_id=1, source_target_pairs={{0,16},{16,0},{1,17},{17,1},{2,18},{18,2},{3,19},{19,3},{4,20},{20... | collective-permute-start | bytes 1572872 | tf_op jit(solution)/shard_map/ppermute | solution.py:49
  62.8 1.6 collective-permute-start.5
  63.9 4.0 %collective-permute-start.2 = (bf16[128,1024]{1,0:T(8,128)(2,1)S(1)}, bf16[128,1024]{1,0:T(8,128)(2,1)S(1)}, u32[]{:S(2)}, u32[]{:S(2)}) collective-permute-start(bf16[128,1024]{1,0:T(8,128)(2,1)S(1)} %convolution_convert_fusion.1), channel_id=1, source_target_pairs={{0,1},{1,0},{2,3},{3,2},{4,5},{5,4},{6,7},{7,6},{8,9},{9,8},{10,11... | collective-permute-start | bytes 786440 | tf_op jit(solution)/shard_map/ppermute | solution.py:34
  66.3 8.4 %collective-permute-start.6 = (bf16[128,1024]{1,0:T(8,128)(2,1)S(1)}, bf16[128,1024]{1,0:T(8,128)(2,1)S(1)}, u32[]{:S(2)}, u32[]{:S(2)}) collective-permute-start(bf16[128,1024]{1,0:T(8,128)(2,1)S(1)} %fusion), channel_id=1, source_target_pairs={{0,16},{16,0},{1,17},{17,1},{2,18},{18,2},{3,19},{19,3},{4,20},{20... | collective-permute-start | bytes 786440 | tf_op jit(solution)/shard_map/ppermute | solution.py:49
  75.3 2.2 %collective-permute-start.9 = (bf16[128,2176]{1,0:T(8,128)(2,1)S(1)}, bf16[128,2176]{1,0:T(8,128)(2,1)S(1)}, u32[]{:S(2)}, u32[]{:S(2)}) collective-permute-start(bf16[128,2176]{1,0:T(8,128)(2,1)S(1)} %get-tuple-element.82.refs_3_), channel_id=1, source_target_pairs={{0,1},{1,0},{2,3},{3,2},{4,5},{5,4},{6,7},{7,6},{8,9},{9,8},{10,11... | collective-permute-start | bytes 1671176 | tf_op jit(solution)/shard_map/ppermute | solution.py:34
  75.4 15.0 %collective-permute-start.7 = (bf16[128,2176]{1,0:T(8,128)(2,1)S(1)}, bf16[128,2176]{1,0:T(8,128)(2,1)S(1)}, u32[]{:S(2)}, u32[]{:S(2)}) collective-permute-start(bf16[128,2176]{1,0:T(8,128)(2,1)S(1)} %get-tuple-element.82.refs_3_), channel_id=1, source_target_pairs={{0,4},{4,8},{8,12},{12,14},{14,10},{10,6},{6,2},{2,0},{1,5},{5,9},... | collective-permute-start | bytes 1671176 | tf_op jit(solution)/shard_map/ppermute | solution.py:42
  76.9 14.7 %collective-permute-start.8 = (bf16[128,2176]{1,0:T(8,128)(2,1)S(1)}, bf16[128,2176]{1,0:T(8,128)(2,1)S(1)}, u32[]{:S(2)}, u32[]{:S(2)}) collective-permute-start(bf16[128,2176]{1,0:T(8,128)(2,1)S(1)} %get-tuple-element.82.refs_3_), channel_id=1, source_target_pairs={{0,2},{4,0},{8,4},{12,8},{14,12},{10,14},{6,10},{2,6},{1,3},{5,1},... | collective-permute-start | bytes 1671176 | tf_op jit(solution)/shard_map/ppermute | solution.py:42
  91.6 2.5 %collective-permute-start.12 = (bf16[128,2176]{1,0:T(8,128)(2,1)S(1)}, bf16[128,2176]{1,0:T(8,128)(2,1)S(1)}, u32[]{:S(2)}, u32[]{:S(2)}) collective-permute-start(bf16[128,2176]{1,0:T(8,128)(2,1)S(1)} %collective-permute-done.7.refs_3_), channel_id=1, source_target_pairs={{0,1},{1,0},{2,3},{3,2},{4,5},{5,4},{6,7},{7,6},{8,9},{9,8},{10,11... | collective-permute-start | bytes 1671176 | tf_op jit(solution)/shard_map/ppermute | solution.py:34
  91.6 2.8 %collective-permute-start.13 = (bf16[128,2176]{1,0:T(8,128)(2,1)S(1)}, bf16[128,2176]{1,0:T(8,128)(2,1)S(1)}, u32[]{:S(2)}, u32[]{:S(2)}) collective-permute-start(bf16[128,2176]{1,0:T(8,128)(2,1)S(1)} %collective-permute-done.8.refs_5_), channel_id=1, source_target_pairs={{0,1},{1,0},{2,3},{3,2},{4,5},{5,4},{6,7},{7,6},{8,9},{9,8},{10,11... | collective-permute-start | bytes 1671176 | tf_op jit(solution)/shard_map/ppermute | solution.py:34
  92.1 14.5 %collective-permute-start.10 = (bf16[128,2176]{1,0:T(8,128)(2,1)S(1)}, bf16[128,2176]{1,0:T(8,128)(2,1)S(1)}, u32[]{:S(2)}, u32[]{:S(2)}) collective-permute-start(bf16[128,2176]{1,0:T(8,128)(2,1)S(1)} %collective-permute-done.7.refs_3_), channel_id=1, source_target_pairs={{0,4},{4,8},{8,12},{12,14},{14,10},{10,6},{6,2},{2,0},{1,5},{5,9},... | collective-permute-start | bytes 1671176 | tf_op jit(solution)/shard_map/ppermute | solution.py:42
  93.6 14.3 %collective-permute-start.11 = (bf16[128,2176]{1,0:T(8,128)(2,1)S(1)}, bf16[128,2176]{1,0:T(8,128)(2,1)S(1)}, u32[]{:S(2)}, u32[]{:S(2)}) collective-permute-start(bf16[128,2176]{1,0:T(8,128)(2,1)S(1)} %collective-permute-done.8.refs_5_), channel_id=1, source_target_pairs={{0,2},{4,0},{8,4},{12,8},{14,12},{10,14},{6,10},{2,6},{1,3},{5,1},... | collective-permute-start | bytes 1671176 | tf_op jit(solution)/shard_map/ppermute | solution.py:42
  94.2 5.3 %collective-permute-start.14 = (bf16[128,2048]{1,0:T(8,128)(2,1)S(1)}, bf16[128,2048]{1,0:T(8,128)(2,1)S(1)}, u32[]{:S(2)}, u32[]{:S(2)}) collective-permute-start(bf16[128,2048]{1,0:T(8,128)(2,1)S(1)} %get-tuple-element.92), channel_id=1, source_target_pairs={{0,1},{1,0},{2,3},{3,2},{4,5},{5,4},{6,7},{7,6},{8,9},{9,8},{10,11... | collective-permute-start | bytes 1572872 | tf_op jit(solution)/shard_map/ppermute | solution.py:34
  107.9 2.5 %collective-permute-start.17 = (bf16[128,2176]{1,0:T(8,128)(2,1)S(1)}, bf16[128,2176]{1,0:T(8,128)(2,1)S(1)}, u32[]{:S(2)}, u32[]{:S(2)}) collective-permute-start(bf16[128,2176]{1,0:T(8,128)(2,1)S(1)} %collective-permute-done.10.refs_3_), channel_id=1, source_target_pairs={{0,1},{1,0},{2,3},{3,2},{4,5},{5,4},{6,7},{7,6},{8,9},{9,8},{10,11... | collective-permute-start | bytes 1671176 | tf_op jit(solution)/shard_map/ppermute | solution.py:34
  107.9 3.1 %collective-permute-start.18 = (bf16[128,2176]{1,0:T(8,128)(2,1)S(1)}, bf16[128,2176]{1,0:T(8,128)(2,1)S(1)}, u32[]{:S(2)}, u32[]{:S(2)}) collective-permute-start(bf16[128,2176]{1,0:T(8,128)(2,1)S(1)} %collective-permute-done.11.refs_5_), channel_id=1, source_target_pairs={{0,1},{1,0},{2,3},{3,2},{4,5},{5,4},{6,7},{7,6},{8,9},{9,8},{10,11... | collective-permute-start | bytes 1671176 | tf_op jit(solution)/shard_map/ppermute | solution.py:34
  108.4 14.5 %collective-permute-start.15 = (bf16[128,2176]{1,0:T(8,128)(2,1)S(1)}, bf16[128,2176]{1,0:T(8,128)(2,1)S(1)}, u32[]{:S(2)}, u32[]{:S(2)}) collective-permute-start(bf16[128,2176]{1,0:T(8,128)(2,1)S(1)} %collective-permute-done.10.refs_3_), channel_id=1, source_target_pairs={{0,4},{4,8},{8,12},{12,14},{14,10},{10,6},{6,2},{2,0},{1,5},{5,9},... | collective-permute-start | bytes 1671176 | tf_op jit(solution)/shard_map/ppermute | solution.py:42
  109.8 14.3 %collective-permute-start.16 = (bf16[128,2176]{1,0:T(8,128)(2,1)S(1)}, bf16[128,2176]{1,0:T(8,128)(2,1)S(1)}, u32[]{:S(2)}, u32[]{:S(2)}) collective-permute-start(bf16[128,2176]{1,0:T(8,128)(2,1)S(1)} %collective-permute-done.11.refs_5_), channel_id=1, source_target_pairs={{0,2},{4,0},{8,4},{12,8},{14,12},{10,14},{6,10},{2,6},{1,3},{5,1},... | collective-permute-start | bytes 1671176 | tf_op jit(solution)/shard_map/ppermute | solution.py:42
  110.4 5.6 %collective-permute-start.19 = (bf16[128,2048]{1,0:T(8,128)(2,1)S(1)}, bf16[128,2048]{1,0:T(8,128)(2,1)S(1)}, u32[]{:S(2)}, u32[]{:S(2)}) collective-permute-start(bf16[128,2048]{1,0:T(8,128)(2,1)S(1)} %get-tuple-element.102), channel_id=1, source_target_pairs={{0,1},{1,0},{2,3},{3,2},{4,5},{5,4},{6,7},{7,6},{8,9},{9,8},{10,11... | collective-permute-start | bytes 1572872 | tf_op jit(solution)/shard_map/ppermute | solution.py:34
  110.4 5.6 %collective-permute-start.20 = (bf16[128,2048]{1,0:T(8,128)(2,1)S(1)}, bf16[128,2048]{1,0:T(8,128)(2,1)S(1)}, u32[]{:S(2)}, u32[]{:S(2)}) collective-permute-start(bf16[128,2048]{1,0:T(8,128)(2,1)S(1)} %get-tuple-element.104), channel_id=1, source_target_pairs={{0,1},{1,0},{2,3},{3,2},{4,5},{5,4},{6,7},{7,6},{8,9},{9,8},{10,11... | collective-permute-start | bytes 1572872 | tf_op jit(solution)/shard_map/ppermute | solution.py:34
  124.1 2.0 collective-permute-start.23
  124.1 3.2 %collective-permute-start.24 = (bf16[128,2176]{1,0:T(8,128)(2,1)S(1)}, bf16[128,2176]{1,0:T(8,128)(2,1)S(1)}, u32[]{:S(2)}, u32[]{:S(2)}) collective-permute-start(bf16[128,2176]{1,0:T(8,128)(2,1)S(1)} %collective-permute-done.16.refs_5_), channel_id=1, source_target_pairs={{0,1},{1,0},{2,3},{3,2},{4,5},{5,4},{6,7},{7,6},{8,9},{9,8},{10,11... | collective-permute-start | bytes 1671176 | tf_op jit(solution)/shard_map/ppermute | solution.py:34
  124.6 10.1 %collective-permute-start.25 = (bf16[128,2048]{1,0:T(8,128)(2,1)S(1)}, bf16[128,2048]{1,0:T(8,128)(2,1)S(1)}, u32[]{:S(2)}, u32[]{:S(2)}) collective-permute-start(bf16[128,2048]{1,0:T(8,128)(2,1)S(1)} %get-tuple-element.116), channel_id=1, source_target_pairs={{0,1},{1,0},{2,3},{3,2},{4,5},{5,4},{6,7},{7,6},{8,9},{9,8},{10,11... | collective-permute-start | bytes 1572872 | tf_op jit(solution)/shard_map/ppermute | solution.py:34
  124.6 10.1 %collective-permute-start.26 = (bf16[128,2048]{1,0:T(8,128)(2,1)S(1)}, bf16[128,2048]{1,0:T(8,128)(2,1)S(1)}, u32[]{:S(2)}, u32[]{:S(2)}) collective-permute-start(bf16[128,2048]{1,0:T(8,128)(2,1)S(1)} %get-tuple-element.118), channel_id=1, source_target_pairs={{0,1},{1,0},{2,3},{3,2},{4,5},{5,4},{6,7},{7,6},{8,9},{9,8},{10,11... | collective-permute-start | bytes 1572872 | tf_op jit(solution)/shard_map/ppermute | solution.py:34
  125.2 8.6 %collective-permute-start.21 = (bf16[64,2176]{1,0:T(8,128)(2,1)S(1)}, bf16[64,2176]{1,0:T(8,128)(2,1)S(1)}, u32[]{:S(2)}, u32[]{:S(2)}) collective-permute-start(bf16[64,2176]{1,0:T(8,128)(2,1)S(1)} %slice.117), channel_id=1, source_target_pairs={{0,4},{4,8},{8,12},{12,14},{14,10},{10,6},{6,2},{2,0},{1,5},{5,9},... | collective-permute-start | bytes 835592 | tf_op jit(solution)/shard_map/ppermute | solution.py:42
  126.1 8.7 %collective-permute-start.22 = (bf16[64,2176]{1,0:T(8,128)(2,1)S(1)}, bf16[64,2176]{1,0:T(8,128)(2,1)S(1)}, u32[]{:S(2)}, u32[]{:S(2)}) collective-permute-start(bf16[64,2176]{1,0:T(8,128)(2,1)S(1)} %slice.118), channel_id=1, source_target_pairs={{0,2},{4,0},{8,4},{12,8},{14,12},{10,14},{6,10},{2,6},{1,3},{5,1},... | collective-permute-start | bytes 835592 | tf_op jit(solution)/shard_map/ppermute | solution.py:42
  134.8 3.5 %collective-permute-start.29 = (bf16[128,2048]{1,0:T(8,128)(2,1)S(1)}, bf16[128,2048]{1,0:T(8,128)(2,1)S(1)}, u32[]{:S(2)}, u32[]{:S(2)}) collective-permute-start(bf16[128,2048]{1,0:T(8,128)(2,1)S(1)} %get-tuple-element.130), channel_id=1, source_target_pairs={{0,1},{1,0},{2,3},{3,2},{4,5},{5,4},{6,7},{7,6},{8,9},{9,8},{10,11... | collective-permute-start | bytes 1572872 | tf_op jit(solution)/shard_map/ppermute | solution.py:34
  134.8 3.5 %collective-permute-start.30 = (bf16[128,2048]{1,0:T(8,128)(2,1)S(1)}, bf16[128,2048]{1,0:T(8,128)(2,1)S(1)}, u32[]{:S(2)}, u32[]{:S(2)}) collective-permute-start(bf16[128,2048]{1,0:T(8,128)(2,1)S(1)} %get-tuple-element.132), channel_id=1, source_target_pairs={{0,1},{1,0},{2,3},{3,2},{4,5},{5,4},{6,7},{7,6},{8,9},{9,8},{10,11... | collective-permute-start | bytes 1572872 | tf_op jit(solution)/shard_map/ppermute | solution.py:34
  135.3 2.5 %collective-permute-start.27 = (bf16[64,2176]{1,0:T(8,128)(2,1)S(1)}, bf16[64,2176]{1,0:T(8,128)(2,1)S(1)}, u32[]{:S(2)}, u32[]{:S(2)}) collective-permute-start(bf16[64,2176]{1,0:T(8,128)(2,1)S(1)} %collective-permute-done.21.refs_3_), channel_id=1, source_target_pairs={{0,1},{1,0},{2,3},{3,2},{4,5},{5,4},{6,7},{7,6},{8,9},{9,8},{10,11... | collective-permute-start | bytes 835592 | tf_op jit(solution)/shard_map/ppermute | solution.py:34
  135.3 2.9 %collective-permute-start.28 = (bf16[64,2176]{1,0:T(8,128)(2,1)S(1)}, bf16[64,2176]{1,0:T(8,128)(2,1)S(1)}, u32[]{:S(2)}, u32[]{:S(2)}) collective-permute-start(bf16[64,2176]{1,0:T(8,128)(2,1)S(1)} %collective-permute-done.22.refs_4_), channel_id=1, source_target_pairs={{0,1},{1,0},{2,3},{3,2},{4,5},{5,4},{6,7},{7,6},{8,9},{9,8},{10,11... | collective-permute-start | bytes 835592 | tf_op jit(solution)/shard_map/ppermute | solution.py:34
  140.8 2.0 collective-permute-start.31
  143.0 8.4 %collective-permute-start.32 = (bf16[64,2048]{1,0:T(8,128)(2,1)S(1)}, bf16[64,2048]{1,0:T(8,128)(2,1)S(1)}, u32[]{:S(2)}, u32[]{:S(2)}) collective-permute-start(bf16[64,2048]{1,0:T(8,128)(2,1)S(1)} %get-tuple-element.165), channel_id=1, source_target_pairs={{0,4},{4,8},{8,12},{12,14},{14,10},{10,6},{6,2},{2,0},{1,5},{5,9},... | collective-permute-start | bytes 786440 | tf_op jit(solution)/shard_map/ppermute | solution.py:42
  143.8 9.8 %collective-permute-start.42 = (bf16[64,2048]{1,0:T(8,128)(2,1)S(1)}, bf16[64,2048]{1,0:T(8,128)(2,1)S(1)}, u32[]{:S(2)}, u32[]{:S(2)}) collective-permute-start(bf16[64,2048]{1,0:T(8,128)(2,1)S(1)} %get-tuple-element.166), channel_id=1, source_target_pairs={{0,2},{4,0},{8,4},{12,8},{14,12},{10,14},{6,10},{2,6},{1,3},{5,1},... | collective-permute-start | bytes 786440 | tf_op jit(solution)/shard_map/ppermute | solution.py:42
  151.5 9.3 %collective-permute-start.33 = (bf16[64,2048]{1,0:T(8,128)(2,1)S(1)}, bf16[64,2048]{1,0:T(8,128)(2,1)S(1)}, u32[]{:S(2)}, u32[]{:S(2)}) collective-permute-start(bf16[64,2048]{1,0:T(8,128)(2,1)S(1)} %get-tuple-element.163), channel_id=1, source_target_pairs={{0,4},{4,8},{8,12},{12,14},{14,10},{10,6},{6,2},{2,0},{1,5},{5,9},... | collective-permute-start | bytes 786440 | tf_op jit(solution)/shard_map/ppermute | solution.py:42
  152.4 12.3 %collective-permute-start.39 = (bf16[64,2048]{1,0:T(8,128)(2,1)S(1)}, bf16[64,2048]{1,0:T(8,128)(2,1)S(1)}, u32[]{:S(2)}, u32[]{:S(2)}) collective-permute-start(bf16[64,2048]{1,0:T(8,128)(2,1)S(1)} %get-tuple-element.164), channel_id=1, source_target_pairs={{0,4},{4,8},{8,12},{12,14},{14,10},{10,6},{6,2},{2,0},{1,5},{5,9},... | collective-permute-start | bytes 786440 | tf_op jit(solution)/shard_map/ppermute | solution.py:42
  153.8 13.2 %collective-permute-start.36 = (bf16[64,2048]{1,0:T(8,128)(2,1)S(1)}, bf16[64,2048]{1,0:T(8,128)(2,1)S(1)}, u32[]{:S(2)}, u32[]{:S(2)}) collective-permute-start(bf16[64,2048]{1,0:T(8,128)(2,1)S(1)} %get-tuple-element.171), channel_id=1, source_target_pairs={{0,2},{4,0},{8,4},{12,8},{14,12},{10,14},{6,10},{2,6},{1,3},{5,1},... | collective-permute-start | bytes 786440 | tf_op jit(solution)/shard_map/ppermute | solution.py:42
  154.7 12.4 %collective-permute-start.43 = (bf16[64,2048]{1,0:T(8,128)(2,1)S(1)}, bf16[64,2048]{1,0:T(8,128)(2,1)S(1)}, u32[]{:S(2)}, u32[]{:S(2)}) collective-permute-start(bf16[64,2048]{1,0:T(8,128)(2,1)S(1)} %get-tuple-element.172), channel_id=1, source_target_pairs={{0,2},{4,0},{8,4},{12,8},{14,12},{10,14},{6,10},{2,6},{1,3},{5,1},... | collective-permute-start | bytes 786440 | tf_op jit(solution)/shard_map/ppermute | solution.py:42
  165.0 9.3 %collective-permute-start.34 = (bf16[64,2048]{1,0:T(8,128)(2,1)S(1)}, bf16[64,2048]{1,0:T(8,128)(2,1)S(1)}, u32[]{:S(2)}, u32[]{:S(2)}) collective-permute-start(bf16[64,2048]{1,0:T(8,128)(2,1)S(1)} %get-tuple-element.161), channel_id=1, source_target_pairs={{0,4},{4,8},{8,12},{12,14},{14,10},{10,6},{6,2},{2,0},{1,5},{5,9},... | collective-permute-start | bytes 786440 | tf_op jit(solution)/shard_map/ppermute | solution.py:42
  165.8 11.4 %collective-permute-start.40 = (bf16[64,2048]{1,0:T(8,128)(2,1)S(1)}, bf16[64,2048]{1,0:T(8,128)(2,1)S(1)}, u32[]{:S(2)}, u32[]{:S(2)}) collective-permute-start(bf16[64,2048]{1,0:T(8,128)(2,1)S(1)} %get-tuple-element.162), channel_id=1, source_target_pairs={{0,4},{4,8},{8,12},{12,14},{14,10},{10,6},{6,2},{2,0},{1,5},{5,9},... | collective-permute-start | bytes 786440 | tf_op jit(solution)/shard_map/ppermute | solution.py:42
  167.3 12.3 %collective-permute-start.37 = (bf16[64,2048]{1,0:T(8,128)(2,1)S(1)}, bf16[64,2048]{1,0:T(8,128)(2,1)S(1)}, u32[]{:S(2)}, u32[]{:S(2)}) collective-permute-start(bf16[64,2048]{1,0:T(8,128)(2,1)S(1)} %get-tuple-element.169), channel_id=1, source_target_pairs={{0,2},{4,0},{8,4},{12,8},{14,12},{10,14},{6,10},{2,6},{1,3},{5,1},... | collective-permute-start | bytes 786440 | tf_op jit(solution)/shard_map/ppermute | solution.py:42
  168.2 11.4 %collective-permute-start.44 = (bf16[64,2048]{1,0:T(8,128)(2,1)S(1)}, bf16[64,2048]{1,0:T(8,128)(2,1)S(1)}, u32[]{:S(2)}, u32[]{:S(2)}) collective-permute-start(bf16[64,2048]{1,0:T(8,128)(2,1)S(1)} %get-tuple-element.170), channel_id=1, source_target_pairs={{0,2},{4,0},{8,4},{12,8},{14,12},{10,14},{6,10},{2,6},{1,3},{5,1},... | collective-permute-start | bytes 786440 | tf_op jit(solution)/shard_map/ppermute | solution.py:42
  177.5 8.5 %collective-permute-start.35 = (bf16[64,2048]{1,0:T(8,128)(2,1)S(1)}, bf16[64,2048]{1,0:T(8,128)(2,1)S(1)}, u32[]{:S(2)}, u32[]{:S(2)}) collective-permute-start(bf16[64,2048]{1,0:T(8,128)(2,1)S(1)} %get-tuple-element.159), channel_id=1, source_target_pairs={{0,4},{4,8},{8,12},{12,14},{14,10},{10,6},{6,2},{2,0},{1,5},{5,9},... | collective-permute-start | bytes 786440 | tf_op jit(solution)/shard_map/ppermute | solution.py:42
  178.4 10.5 %collective-permute-start.41 = (bf16[64,2048]{1,0:T(8,128)(2,1)S(1)}, bf16[64,2048]{1,0:T(8,128)(2,1)S(1)}, u32[]{:S(2)}, u32[]{:S(2)}) collective-permute-start(bf16[64,2048]{1,0:T(8,128)(2,1)S(1)} %get-tuple-element.160), channel_id=1, source_target_pairs={{0,4},{4,8},{8,12},{12,14},{14,10},{10,6},{6,2},{2,0},{1,5},{5,9},... | collective-permute-start | bytes 786440 | tf_op jit(solution)/shard_map/ppermute | solution.py:42
  179.9 9.0 %collective-permute-start.38 = (bf16[64,2048]{1,0:T(8,128)(2,1)S(1)}, bf16[64,2048]{1,0:T(8,128)(2,1)S(1)}, u32[]{:S(2)}, u32[]{:S(2)}) collective-permute-start(bf16[64,2048]{1,0:T(8,128)(2,1)S(1)} %get-tuple-element.167), channel_id=1, source_target_pairs={{0,2},{4,0},{8,4},{12,8},{14,12},{10,14},{6,10},{2,6},{1,3},{5,1},... | collective-permute-start | bytes 786440 | tf_op jit(solution)/shard_map/ppermute | solution.py:42
  180.7 9.9 %collective-permute-start.45 = (bf16[64,2048]{1,0:T(8,128)(2,1)S(1)}, bf16[64,2048]{1,0:T(8,128)(2,1)S(1)}, u32[]{:S(2)}, u32[]{:S(2)}) collective-permute-start(bf16[64,2048]{1,0:T(8,128)(2,1)S(1)} %get-tuple-element.168), channel_id=1, source_target_pairs={{0,2},{4,0},{8,4},{12,8},{14,12},{10,14},{6,10},{2,6},{1,3},{5,1},... | collective-permute-start | bytes 786440 | tf_op jit(solution)/shard_map/ppermute | solution.py:42
  (10 other events, 89.7 us)
Sparse Core Ops, SparseCore 0:
  8.9 50.5 all-gather.1

commit v3 on v2

--- a/solution.py
+++ b/solution.py
@@ -12,8 +12,6 @@
 KVH = 2
 HD = 128
 TOP = 8
-LANES = 128
-TERMS = 3
 
 
 def chip_ring(n):
@@ -84,8 +82,12 @@
             out_ref[slot, :, at : at + HD] = (mixed / row_sum).astype(jnp.bfloat16)
 
 
-def norm_kernel(experts_all, pos_ref, hidden_ref, *refs):
-    *projected_refs, gain_ref, ids_ref, gates_ref, residual_ref, tokens_ref = refs
+def columns_kernel(pos_ref, source_ref, target_ref):
+    target_ref[...] = source_ref[...]
+
+
+def norm_kernel(pos_ref, hidden_ref, *refs):
+    *projected_refs, gain_ref, residual_ref, tokens_ref = refs
     n_ctx = len(projected_refs)
     wide = D // n_ctx
     square_sum = None
@@ -97,30 +99,28 @@
         square_sum = squares if square_sum is None else square_sum + squares
     scale_inv = lax.rsqrt(square_sum * (1.0 / D) + 1e-06)
     normed = residual_ref[...] * scale_inv * gain_ref[...].astype(jnp.float32)
-    tokens_ref[:, :D] = normed.astype(jnp.bfloat16)
-    shape = (tokens_ref.shape[0], tokens_ref.shape[1] - D)
-    column = lax.broadcasted_iota(jnp.int32, shape, 1)
-    expert = lax.rem(column, experts_all)
-    gates = jnp.zeros(shape, jnp.float32)
-    for k in range(TOP):
-        gates = gates + jnp.where(ids_ref[:, k : k + 1] == expert, gates_ref[:, k : k + 1], 0.0)
-    terms = jnp.zeros(shape, jnp.float32)
-    for term in range(TERMS):
-        rounded = gates.astype(jnp.bfloat16).astype(jnp.float32)
-        terms = jnp.where(column // experts_all == term, rounded, terms)
-        gates = gates - rounded
-    tokens_ref[:, D:] = terms.astype(jnp.bfloat16)
-
-
-def expert_kernel(experts_all, groups, parts, expert_ref, *refs):
+    tokens_ref[...] = normed.astype(jnp.bfloat16)
+
+
+def final_kernel(residual_ref, own_ref, sibling_ref, *refs):
+    *arrived_refs, out_ref = refs
+    rows = arrived_refs[0].shape[0]
+    for half in range(2):
+        at = pl.ds(half * rows, rows)
+        total = residual_ref[at, :]
+        for ref in (own_ref.at[at], sibling_ref.at[at], *arrived_refs[2 * half : 2 * half + 2]):
+            total = total + ref[...].astype(jnp.float32)
+        out_ref[0, at, :] = total.astype(jnp.bfloat16)
+
+
+def expert_kernel(groups, parts, expert_ref, *refs):
     gate_ref, up_ref, down_ref, *refs = refs
-    block_refs, out_refs = refs[: 2 * groups * parts], refs[2 * groups * parts :]
-    blocks = jnp.concatenate([ref[...] for ref in block_refs], axis=0)
-    terms = blocks[:, D:].astype(jnp.float32)
-    column = lax.broadcasted_iota(jnp.int32, terms.shape, 1)
-    mine = (lax.rem(column, experts_all) == expert_ref[0]) & (column < TERMS * experts_all)
-    gates = jnp.sum(jnp.where(mine, terms, 0.0), axis=1, keepdims=True)
-    tokens = blocks[:, :D]
+    blocks, refs = refs[: 2 * groups * parts], refs[2 * groups * parts :]
+    gate_refs, out_refs = refs[: 2 * groups], refs[2 * groups :]
+    tokens = jnp.concatenate([ref[...] for ref in blocks], axis=0)
+    gates = jnp.concatenate([ref[...] for ref in gate_refs], axis=0)
+    column = lax.broadcasted_iota(jnp.int32, gates.shape, 1)
+    gates = jnp.sum(jnp.where(column == expert_ref[0], gates, 0.0), axis=1, keepdims=True)
     gate_pre = jnp.dot(tokens, gate_ref[...], preferred_element_type=jnp.float32)
     up_pre = jnp.dot(tokens, up_ref[...], preferred_element_type=jnp.float32)
     activated = (gate_pre / (1.0 + jnp.exp(-gate_pre)) * up_pre).astype(jnp.bfloat16)
@@ -156,15 +156,33 @@
     )(jnp.stack([position, core]), queries, *blocks)
 
 
-def run_expert(experts_all, expert, chips, weights):
+def own_columns(position, matrix, n_parts):
+    rows, width = matrix.shape
+    wide = width // n_parts
+    return pl.pallas_call(
+        columns_kernel,
+        grid_spec=pltpu.PrefetchScalarGridSpec(
+            num_scalar_prefetch=1,
+            grid=(1,),
+            in_specs=[pl.BlockSpec((rows, wide), lambda i, pos: (0, pos[0]))],
+            out_specs=pl.BlockSpec((rows, wide), lambda i, pos: (0, 0)),
+        ),
+        out_shape=jax.ShapeDtypeStruct((rows, wide), matrix.dtype),
+        compiler_params=pltpu.CompilerParams(vmem_limit_bytes=60 * 1024 * 1024),
+        name="columns",
+    )(position.reshape(1), matrix)
+
+
+def run_expert(expert, chips, gates, weights):
     groups, parts = len(chips), len(chips[0][0])
     blocks = [block for own, other in chips for block in own + other]
-    rows = sum(block.shape[0] for block in blocks) // (2 * groups)
+    gates = [block for pair in gates for block in pair]
+    rows = gates[0].shape[0]
     ef = weights[0].shape[1]
     results = pl.pallas_call(
-        functools.partial(expert_kernel, experts_all, groups, parts),
+        functools.partial(expert_kernel, groups, parts),
         out_shape=[jax.ShapeDtypeStruct((rows, D), jnp.bfloat16)] * (2 * groups),
-        in_specs=[smem()] + [vmem()] * (3 + len(blocks)),
+        in_specs=[smem()] + [vmem()] * (3 + len(blocks) + len(gates)),
         out_specs=[vmem()] * (2 * groups),
         compiler_params=pltpu.CompilerParams(vmem_limit_bytes=38 * 1024 * 1024),
         cost_estimate=pl.CostEstimate(
@@ -173,7 +191,7 @@
             transcendentals=0,
         ),
         name="experts",
-    )(expert.reshape(1), *weights, *blocks)
+    )(expert.reshape(1), *weights, *blocks, *gates)
     return [(results[2 * g], results[2 * g + 1]) for g in range(groups)]
 
 
@@ -185,9 +203,8 @@
     position = lax.axis_index("ctx")
     rows = hidden_in.shape[1]
     proj_rows = out_proj.shape[0]
-    wide = D // n_ctx
     columns = lax.all_gather(
-        lax.dynamic_slice_in_dim(out_proj, position * wide, wide, axis=1),
+        own_columns(position, out_proj, n_ctx),
         "exp",
         axis=0,
         tiled=True,
@@ -201,6 +218,21 @@
     blocks = [keyval[0]] + [rotate(keyval[0], "ctx", back) for back in range(1, n_ctx)]
     attended = attend(position, core, query[0], blocks, n_exp, proj_rows)
     own_heads, other_heads = attended[0], attended[1]
+
+    local_experts = w_gate.shape[0]
+    experts = jnp.arange(n_exp * local_experts, dtype=jnp.int32)
+    named = expert_ids[0][:, :, None] == experts[None, None, :]
+    gates = jnp.sum(jnp.where(named, gate_weights[0][:, :, None], 0.0), axis=1)
+    n_chip = n_exp // 2
+    far = n_chip // 2
+    gates_at = {0: gates}
+    forward, backward = gates, gates
+    for step in range(1, far + 1):
+        forward, backward = round_ring(forward, 1), round_ring(backward, -1)
+        gates_at |= {n_chip - step: forward} if step == far else {n_chip - step: forward, step: backward}
+    gates_at = {offset: (block, swap_cores(block)) for offset, block in gates_at.items()}
+    own_heads, other_heads, gates_at = lax.optimization_barrier((own_heads, other_heads, gates_at))
+
     sibling_heads = swap_cores(other_heads)
     projected = []
     for back in range(n_ctx):
@@ -211,30 +243,18 @@
             part = rotate(part.astype(jnp.bfloat16), "ctx", -back)
         projected.append(part)
 
-    local_experts = w_gate.shape[0]
-    experts_all = n_exp * local_experts
-    extra = -(-TERMS * experts_all // LANES) * LANES
     residual, tokens = pl.pallas_call(
-        functools.partial(norm_kernel, experts_all),
+        norm_kernel,
         out_shape=(
             jax.ShapeDtypeStruct((rows, D), jnp.float32),
-            jax.ShapeDtypeStruct((rows, D + extra), jnp.bfloat16),
+            jax.ShapeDtypeStruct((rows, D), jnp.bfloat16),
         ),
-        in_specs=[smem()] + [vmem()] * (4 + n_ctx),
+        in_specs=[smem()] + [vmem()] * (2 + n_ctx),
         out_specs=(vmem(), vmem()),
         compiler_params=pltpu.CompilerParams(vmem_limit_bytes=16 * 1024 * 1024),
         name="norm",
-    )(
-        position.reshape(1),
-        hidden_in[0],
-        *projected,
-        norm_gain.reshape(1, D),
-        expert_ids[0],
-        gate_weights[0],
-    )
-
-    n_chip = n_exp // 2
-    far = n_chip // 2
+    )(position.reshape(1), hidden_in[0], *projected, norm_gain.reshape(1, D))
+
     half_rows = rows // 2
     sums = {}
 
@@ -245,7 +265,10 @@
             expert = lax.axis_index("exp") * local_experts + local
             weights = (w_gate[local], w_up[local], w_down[local])
             pairs = run_expert(
-                experts_all, expert, [(own, other) for _, own, other in chips], weights
+                expert,
+                [(own, other) for _, own, other in chips],
+                [gates_at[offset] for offset in offsets],
+                weights,
             )
             total = pairs if total is None else jax.tree.map(jnp.add, total, pairs)
         return dict(zip(offsets, total))
@@ -268,19 +291,22 @@
     results = experts_on([(0, [tokens], [swap_cores(tokens)])])
     forward, backward, results = barrier((forward, backward, results))
     for step in range(1, far):
-        chips = [
-            (n_chip - step, [forward], [swap_cores(forward)]),
-            (step, [backward], [swap_cores(backward)]),
-        ]
+        ours = forward, backward
+        swapped = swap_cores(forward), swap_cores(backward)
         forward, backward = send_on(forward, backward, step + 1)
+        if step + 1 < far:
+            swapped, results = barrier((swapped, results))
         sums |= swap_results(results)
-        results = experts_on(chips)
+        results = experts_on(
+            [(n_chip - step, [ours[0]], [swapped[0]]), (step, [ours[1]], [swapped[1]])]
+        )
         forward, backward, results, sums = barrier((forward, backward, results, sums))
-    halves = [forward, backward]
-    swapped = [swap_cores(half) for half in halves]
+    swapped = [swap_cores(forward), swap_cores(backward)]
+    swapped, results = barrier((swapped, results))
     sums |= swap_results(results)
-    halves, swapped, sums = barrier((halves, swapped, sums))
-    sums |= swap_results(experts_on([(far, halves, swapped)]))
+    results = experts_on([(far, [forward, backward], swapped)])
+    results, sums = barrier((results, sums))
+    sums |= swap_results(results)
 
     def total_at(direction, half, hop, carried):
         offset = hop if direction > 0 else n_chip - hop
@@ -296,11 +322,14 @@
         running_sum(1, 0, far) + running_sum(-1, 0, far - 1),
         running_sum(1, 1, far - 1) + running_sum(-1, 1, far),
     ]
-    result = [
-        total_of([residual] + sums[0] + arrived[half], half).astype(jnp.bfloat16)
-        for half in range(2)
-    ]
-    return jnp.concatenate(result, axis=0)[None]
+    return pl.pallas_call(
+        final_kernel,
+        out_shape=jax.ShapeDtypeStruct((1, rows, D), jnp.bfloat16),
+        in_specs=[vmem()] * 7,
+        out_specs=vmem(),
+        compiler_params=pltpu.CompilerParams(vmem_limit_bytes=16 * 1024 * 1024),
+        name="final",
+    )(residual, *sums[0], *arrived[0], *arrived[1])
 
 
 def solution(mesh):

time: 199 us -> 198 us (level)
  waiting for transfers between devices: 113 us -> 92.4 us
  starting transfers between devices: 33.4 us -> 42.9 us
  Pallas kernels: 23.6 us -> 29.5 us
  local copies, waits for them, and re-layouts: 5.66 us -> 10.8 us
    all_gather x1, waiting for transfers between devices: 21.7 us -> 6.94 us  [body(): lax.all_gather(own_columns(position, out_proj, n_ctx), 'exp', axis=0, til...]
    ppermute x22 -> x29, starting transfers between devices: 22.5 us -> 30.5 us  [round_ring(): return lax.ppermute(block, 'exp', route)]
    unnamed x24 -> x62, local copies, waits for them, and re-layouts: 3.84 us -> 10.4 us
    pallas_call x6 -> x8, Pallas kernels: 21 us -> 26.9 us  [the longest x5 22.8 us: run_expert(): pl.pallas_call(functools.partial(expert_kernel, groups, parts), out_shape...]
    ppermute x4, waiting for transfers between devices: 22.3 us -> 18.3 us  [rotate(): lax.ppermute(block, axis, [(i, (i + distance) % n) for i in range(n)])]
    ppermute x20 -> x28, starting transfers between devices: 4.17 us -> 6.46 us  [swap_cores(): return lax.ppermute(block, 'exp', [(i, i ^ 1) for i in range(n)])]
    ppermute x20 -> x28, waiting for transfers between devices: 6.78 us -> 5.51 us  [swap_cores(): return lax.ppermute(block, 'exp', [(i, i ^ 1) for i in range(n)])]
    ppermute x22 -> x29, waiting for transfers between devices: 62.2 us -> 61.6 us  [round_ring(): return lax.ppermute(block, 'exp', route)]
  transfers between devices with their start and end apart: 47 -> 62, of which waited for: 27 -> 30; matrix products, arithmetic and copies ran while one was open for 5% -> 4% of each run, Pallas kernels for 10% -> 13%
where the time goes in v3:
time: 198 us
  waiting for transfers between devices  92.4 us (47%)
  starting transfers between devices  42.9 us (22%)
  Pallas kernels  29.5 us (15%)
  between operations  13.8 us (7%)
  local copies, waits for them, and re-layouts  10.8 us (5%)
  matrix products  6.42 us (3%)
  other arithmetic  2.21 us (1%)
    ppermute x29, waiting for transfers between devices, round_ring(): return lax.ppermute(block, 'exp', route)  61.6 us
    ppermute x29, starting transfers between devices, round_ring(): return lax.ppermute(block, 'exp', route)  30.5 us
    pallas_call x5, Pallas kernels, run_expert(): pl.pallas_call(functools.partial(expert_kernel, groups, parts), out_shape...  22.8 us
    ppermute x4, waiting for transfers between devices, rotate(): lax.ppermute(block, axis, [(i, (i + distance) % n) for i in range(n)])  18.3 us
    unnamed x62, local copies, waits for them, and re-layouts  10.4 us
    all_gather x1, waiting for transfers between devices, body(): lax.all_gather(own_columns(position, out_proj, n_ctx), 'exp', axis=0, til...  6.94 us
    ppermute x28, starting transfers between devices, swap_cores(): return lax.ppermute(block, 'exp', [(i, i ^ 1) for i in range(n)])  6.46 us
    dot_general x4, matrix products, times_columns(): return jnp.dot(block, columns, preferred_element_type=jnp.float32)  6.42 us
  transfers between devices with their start and end apart: 62, of which 30 were waited for; matrix products, arithmetic and copies ran while one was open for 4% of the time, Pallas kernels for 13%

profile of v3, /device:TPU:0, one launch (start us, length us, event | category | flops | bytes accessed | tf_op | source)
XLA Modules:
  0.0 198.0 jit_solution(17716829745619219126)
XLA Ops:
  6.5 1.9 columns.1
  8.4 3.0 %collective-permute-start = (bf16[128,512]{1,0:T(8,128)(2,1)}, bf16[128,512]{1,0:T(8,128)(2,1)S(1)}, u32[]{:S(2)}, u32[]{:S(2)}) collective-permute-start(bf16[128,512]{1,0:T(8,128)(2,1)} %bitcast.40), channel_id=1, source_target_pairs={{0,16},{16,0},{1,17},{17,1},{2,18},{18,2},{3,19},{19,3},{4,20},{20... | collective-permute-start | bytes 393224 | tf_op jit(solution)/shard_map/ppermute | solution.py:47
  12.3 1.6 collective-permute-start.8
  14.4 2.2 %collective-permute-done.8.refs_7_ = f32[128,16]{1,0:T(8,128)S(1)} collective-permute-done((f32[128,16]{1,0:T(8,128)S(1)}, f32[128,16]{1,0:T(8,128)S(1)}, u32[]{:S(2)}, u32[]{:S(2)}) %collective-permute-start.8) | collective-permute-done | bytes 8224 | tf_op jit(solution)/shard_map/ppermute | solution.py:40
  16.6 1.6 collective-permute-start.9
  18.6 3.6 %collective-permute-done.9.refs_7_ = f32[128,16]{1,0:T(8,128)S(1)} collective-permute-done((f32[128,16]{1,0:T(8,128)S(1)}, f32[128,16]{1,0:T(8,128)S(1)}, u32[]{:S(2)}, u32[]{:S(2)}) %collective-permute-start.9) | collective-permute-done | bytes 8224 | tf_op jit(solution)/shard_map/ppermute | solution.py:40
  22.2 1.6 collective-permute-start.10
  24.4 3.5 %collective-permute-done.10.refs_7_ = f32[128,16]{1,0:T(8,128)S(1)} collective-permute-done((f32[128,16]{1,0:T(8,128)S(1)}, f32[128,16]{1,0:T(8,128)S(1)}, u32[]{:S(2)}, u32[]{:S(2)}) %collective-permute-start.10) | collective-permute-done | bytes 8224 | tf_op jit(solution)/shard_map/ppermute | solution.py:40
  27.9 1.5 collective-permute-start.6
  32.2 2.6 %attention.1 = bf16[2,128,2048]{2,1,0:T(8,128)(2,1)S(1)} custom-call(s32[2]{0:T(128)S(1)} %pad_add_fusion.pos_ref, bf16[128,4096]{1,0:T(8,128)(2,1)S(1)} %bitcast.38, bf16[128,512]{1,0:T(8,128)(2,1)S(1)} %bitcast.41, bf16[128,512]{1,0:T(8,128)(2,1)S(1)} %collective-permute-done.refs_1_), custom_call_target="tpu_custom_call" | custom-call | tf_op jit(solution)/shard_map/attention/pallas_call | solution.py:149
  39.8 1.5 collective-permute-done.16
  41.4 2.0 %collective-permute-start.18 = (bf16[128,2048]{1,0:T(8,128)(2,1)S(1)}, bf16[128,2048]{1,0:T(8,128)(2,1)S(1)}, u32[]{:S(2)}, u32[]{:S(2)}) collective-permute-start(bf16[128,2048]{1,0:T(8,128)(2,1)S(1)} %get-tuple-element.113), channel_id=1, source_target_pairs={{0,16},{16,0},{1,17},{17,1},{2,18},{18,2},{3,19},{19,3},{4,20},{20... | collective-permute-start | bytes 1572872 | tf_op jit(solution)/shard_map/ppermute | solution.py:47
  43.5 12.6 %collective-permute-done.19 = bf16[128,2048]{1,0:T(8,128)(2,1)S(1)} collective-permute-done((bf16[128,2048]{1,0:T(8,128)(2,1)S(1)}, bf16[128,2048]{1,0:T(8,128)(2,1)S(1)}, u32[]{:S(2)}, u32[]{:S(2)}) %collective-permute-start.19) | collective-permute-done | bytes 524320 | tf_op jit(solution)/shard_map/ppermute | solution.py:47
  56.1 6.9 %all-gather.2.cloned.1.call-done = bf16[2048,1024]{1,0:T(8,128)(2,1)} async-done(((bf16[256,1024]{1,0:T(8,128)(2,1)}), bf16[2048,1024]{1,0:T(8,128)(2,1)}) %all-gather.2.cloned.1.call-update) | async-done | bytes 4194320 | tf_op jit(solution)/shard_map/all_gather | solution.py:206
  63.0 3.0 %convolution_convert_fusion = bf16[128,1024]{1,0:T(8,128)(2,1)S(1)} fusion(bf16[128,2048]{1,0:T(8,128)(2,1)S(1)} %collective-permute-done.19, bf16[2048,1024]{1,0:T(8,128)(2,1)} %all-gather.2.cloned.1.call-done), kind=kOutput, calls=%fused_computation.3 | convolution fusion | flops 537001984 | bytes 4980736 | tf_op jit(solution)/shard_map/dot_general | solution.py:215
  69.3 1.9 convolution_add_fusion.1.refs_0_
  71.2 5.7 %collective-permute-done.21.refs_1_ = bf16[128,1024]{1,0:T(8,128)(2,1)S(1)} collective-permute-done((bf16[128,1024]{1,0:T(8,128)(2,1)S(1)}, bf16[128,1024]{1,0:T(8,128)(2,1)S(1)}, u32[]{:S(2)}, u32[]{:S(2)}) %collective-permute-start.21) | collective-permute-done | bytes 262176 | tf_op jit(solution)/shard_map/ppermute | solution.py:47
  79.6 1.4 collective-permute-start.23
  81.2 1.9 copy-done.1
  83.1 1.9 copy-done.2
  85.0 3.9 %experts.5 = (bf16[128,2048]{1,0:T(8,128)(2,1)S(1)}, bf16[128,2048]{1,0:T(8,128)(2,1)S(1)}) custom-call(s32[1]{0:T(128)} %bitcast.9.expert_ref, bf16[2048,768]{1,0:T(8,128)(2,1)S(1)} %bitcast.23, bf16[2048,768]{1,0:T(8,128)(2,1)S(1)} %bitcast.28, bf16[768,2048]{1,0:T(8,128)(2,1)S(1)} %bitcast.33, bf16[128,2048]{1,0:T(8,128)(2,1)} %get-tuple-element.116.refs_3_, ...), custom_call_target="tpu_custom_call" | custom-call | flops 2415919104 | bytes 11534336 | tf_op jit(solution)/shard_map/experts/pallas_call | solution.py:182
  88.9 4.7 %collective-permute-done.22.refs_3_ = bf16[128,2048]{1,0:T(8,128)(2,1)} collective-permute-done((bf16[128,2048]{1,0:T(8,128)(2,1)}, bf16[128,2048]{1,0:T(8,128)(2,1)}, u32[]{:S(2)}, u32[]{:S(2)}) %collective-permute-start.22) | collective-permute-done | bytes 524320 | tf_op jit(solution)/shard_map/ppermute | solution.py:40
  94.5 1.6 collective-permute-start.25
  97.0 6.3 %experts.6 = (bf16[128,2048]{1,0:T(8,128)(2,1)S(1)}, bf16[128,2048]{1,0:T(8,128)(2,1)S(1)}, bf16[128,2048]{1,0:T(8,128)(2,1)S(1)}, bf16[128,2048]{1,0:T(8,128)(2,1)S(1)}) custom-call(s32[1]{0:T(128)} %bitcast.9.expert_ref, bf16[2048,768]{1,0:T(8,128)(2,1)S(1)} %bitcast.24, bf16[2048,768]{1,0:T(8,128)(2,1)S(1)} %bitcast.29, bf16[768,2048]{1,0:T(8,128)(2,1)S(1)} %bitcast.34, ...), custom_call_target="tpu_custom_call" | custom-call | flops 4831838208 | bytes 13631488 | tf_op jit(solution)/shard_map/experts/pallas_call | solution.py:182
  103.2 5.3 %collective-permute-done.25.refs_3_ = bf16[128,2048]{1,0:T(8,128)(2,1)S(1)} collective-permute-done((bf16[128,2048]{1,0:T(8,128)(2,1)}, bf16[128,2048]{1,0:T(8,128)(2,1)S(1)}, u32[]{:S(2)}, u32[]{:S(2)}) %collective-permute-start.25) | collective-permute-done | bytes 524320 | tf_op jit(solution)/shard_map/ppermute | solution.py:40
  108.6 1.3 collective-permute-done.26.refs_5_
  110.5 1.6 collective-permute-start.30
  113.1 5.1 %experts.7 = (bf16[128,2048]{1,0:T(8,128)(2,1)S(1)}, bf16[128,2048]{1,0:T(8,128)(2,1)S(1)}, bf16[128,2048]{1,0:T(8,128)(2,1)S(1)}, bf16[128,2048]{1,0:T(8,128)(2,1)S(1)}) custom-call(s32[1]{0:T(128)} %bitcast.9.expert_ref, bf16[2048,768]{1,0:T(8,128)(2,1)S(1)} %bitcast.25, bf16[2048,768]{1,0:T(8,128)(2,1)S(1)} %bitcast.30, bf16[768,2048]{1,0:T(8,128)(2,1)S(1)} %bitcast.35, ...), custom_call_target="tpu_custom_call" | custom-call | flops 4831838208 | bytes 13631488 | tf_op jit(solution)/shard_map/experts/pallas_call | solution.py:182
  118.2 6.2 %collective-permute-done.30.refs_3_ = bf16[128,2048]{1,0:T(8,128)(2,1)S(1)} collective-permute-done((bf16[128,2048]{1,0:T(8,128)(2,1)S(1)}, bf16[128,2048]{1,0:T(8,128)(2,1)S(1)}, u32[]{:S(2)}, u32[]{:S(2)}) %collective-permute-start.30) | collective-permute-done | bytes 524320 | tf_op jit(solution)/shard_map/ppermute | solution.py:40
  124.4 1.3 collective-permute-done.31.refs_5_
  126.7 1.5 collective-permute-start.36
  128.8 5.1 %experts.8 = (bf16[128,2048]{1,0:T(8,128)(2,1)S(1)}, bf16[128,2048]{1,0:T(8,128)(2,1)S(1)}, bf16[128,2048]{1,0:T(8,128)(2,1)S(1)}, bf16[128,2048]{1,0:T(8,128)(2,1)S(1)}) custom-call(s32[1]{0:T(128)} %bitcast.9.expert_ref, bf16[2048,768]{1,0:T(8,128)(2,1)S(1)} %bitcast.26, bf16[2048,768]{1,0:T(8,128)(2,1)S(1)} %bitcast.31, bf16[768,2048]{1,0:T(8,128)(2,1)S(1)} %bitcast.36, ...), custom_call_target="tpu_custom_call" | custom-call | flops 4831838208 | bytes 13631488 | tf_op jit(solution)/shard_map/experts/pallas_call | solution.py:182
  138.7 2.6 %experts.9 = (bf16[128,2048]{1,0:T(8,128)(2,1)S(1)}, bf16[128,2048]{1,0:T(8,128)(2,1)S(1)}) custom-call(s32[1]{0:T(128)} %bitcast.9.expert_ref, bf16[2048,768]{1,0:T(8,128)(2,1)S(1)} %bitcast.27, bf16[2048,768]{1,0:T(8,128)(2,1)S(1)} %bitcast.32, bf16[768,2048]{1,0:T(8,128)(2,1)S(1)} %bitcast.37, bf16[64,2048]{1,0:T(8,128)(2,1)S(1)} %collective-permute-done.36.refs_3_, ...), custom_call_target="tpu_custom_call" | custom-call | flops 2415919104 | bytes 11534336 | tf_op jit(solution)/shard_map/experts/pallas_call | solution.py:182
  141.6 1.8 collective-permute-done.46
  144.1 1.5 collective-permute-start.47
  145.6 6.3 %collective-permute-done.57 = bf16[64,2048]{1,0:T(8,128)(2,1)S(1)} collective-permute-done((bf16[64,2048]{1,0:T(8,128)(2,1)S(1)}, bf16[64,2048]{1,0:T(8,128)(2,1)S(1)}, u32[]{:S(2)}, u32[]{:S(2)}) %collective-permute-start.57) | collective-permute-done | bytes 262176 | tf_op jit(solution)/shard_map/ppermute | solution.py:40
  153.3 1.6 collective-permute-start.48
  154.9 1.5 collective-permute-start.54
  156.4 4.9 %collective-permute-done.51 = bf16[64,2048]{1,0:T(8,128)(2,1)S(1)} collective-permute-done((bf16[64,2048]{1,0:T(8,128)(2,1)S(1)}, bf16[64,2048]{1,0:T(8,128)(2,1)S(1)}, u32[]{:S(2)}, u32[]{:S(2)}) %collective-permute-start.51) | collective-permute-done | bytes 262176 | tf_op jit(solution)/shard_map/ppermute | solution.py:40
  161.3 3.9 %collective-permute-done.58 = bf16[64,2048]{1,0:T(8,128)(2,1)S(1)} collective-permute-done((bf16[64,2048]{1,0:T(8,128)(2,1)S(1)}, bf16[64,2048]{1,0:T(8,128)(2,1)S(1)}, u32[]{:S(2)}, u32[]{:S(2)}) %collective-permute-start.58) | collective-permute-done | bytes 262176 | tf_op jit(solution)/shard_map/ppermute | solution.py:40
  166.8 1.6 collective-permute-start.49
  168.4 1.5 collective-permute-start.55
  169.9 4.9 %collective-permute-done.52 = bf16[64,2048]{1,0:T(8,128)(2,1)S(1)} collective-permute-done((bf16[64,2048]{1,0:T(8,128)(2,1)S(1)}, bf16[64,2048]{1,0:T(8,128)(2,1)S(1)}, u32[]{:S(2)}, u32[]{:S(2)}) %collective-permute-start.52) | collective-permute-done | bytes 262176 | tf_op jit(solution)/shard_map/ppermute | solution.py:40
  174.8 3.0 %collective-permute-done.59 = bf16[64,2048]{1,0:T(8,128)(2,1)S(1)} collective-permute-done((bf16[64,2048]{1,0:T(8,128)(2,1)S(1)}, bf16[64,2048]{1,0:T(8,128)(2,1)S(1)}, u32[]{:S(2)}, u32[]{:S(2)}) %collective-permute-start.59) | collective-permute-done | bytes 262176 | tf_op jit(solution)/shard_map/ppermute | solution.py:40
  179.3 1.6 collective-permute-start.50
  180.9 1.5 collective-permute-start.56
  182.4 4.1 %collective-permute-done.53.refs_1_ = bf16[64,2048]{1,0:T(8,128)(2,1)S(1)} collective-permute-done((bf16[64,2048]{1,0:T(8,128)(2,1)S(1)}, bf16[64,2048]{1,0:T(8,128)(2,1)S(1)}, u32[]{:S(2)}, u32[]{:S(2)}) %collective-permute-start.53) | collective-permute-done | bytes 262176 | tf_op jit(solution)/shard_map/ppermute | solution.py:40
  186.5 2.8 %collective-permute-done.60.refs_3_ = bf16[64,2048]{1,0:T(8,128)(2,1)S(1)} collective-permute-done((bf16[64,2048]{1,0:T(8,128)(2,1)S(1)}, bf16[64,2048]{1,0:T(8,128)(2,1)S(1)}, u32[]{:S(2)}, u32[]{:S(2)}) %collective-permute-start.60) | collective-permute-done | bytes 262176 | tf_op jit(solution)/shard_map/ppermute | solution.py:40
  (167 shorter events, 33.1 us)
Async XLA Ops:
  6.5 56.5 %all-gather.2.cloned.1.call-start = ((), (), s32[]{:S(2)}) async-start(), calls=%async_computation | async-start | bytes 4718592 | tf_op jit(solution)/shard_map/all_gather | solution.py:206
  8.4 21.0 %collective-permute-start = (bf16[128,512]{1,0:T(8,128)(2,1)}, bf16[128,512]{1,0:T(8,128)(2,1)S(1)}, u32[]{:S(2)}, u32[]{:S(2)}) collective-permute-start(bf16[128,512]{1,0:T(8,128)(2,1)} %bitcast.40), channel_id=1, source_target_pairs={{0,16},{16,0},{1,17},{17,1},{2,18},{18,2},{3,19},{19,3},{4,20},{20... | collective-permute-start | bytes 393224 | tf_op jit(solution)/shard_map/ppermute | solution.py:47
  12.3 4.3 %collective-permute-start.8 = (f32[128,16]{1,0:T(8,128)S(1)}, f32[128,16]{1,0:T(8,128)S(1)}, u32[]{:S(2)}, u32[]{:S(2)}) collective-permute-start(f32[128,16]{1,0:T(8,128)S(1)} %copy.13), channel_id=1, source_target_pairs={{0,4},{4,8},{8,12},{12,14},{14,10},{10,6},{6,2},{2,0},{1,5},{5,9},... | collective-permute-start | bytes 24584 | tf_op jit(solution)/shard_map/ppermute | solution.py:40
  13.9 4.3 %collective-permute-start.2 = (f32[128,16]{1,0:T(8,128)S(1)}, f32[128,16]{1,0:T(8,128)S(1)}, u32[]{:S(2)}, u32[]{:S(2)}) collective-permute-start(f32[128,16]{1,0:T(8,128)S(1)} %copy.13), channel_id=1, source_target_pairs={{0,2},{4,0},{8,4},{12,8},{14,12},{10,14},{6,10},{2,6},{1,3},{5,1},... | collective-permute-start | bytes 24584 | tf_op jit(solution)/shard_map/ppermute | solution.py:40
  16.6 5.6 %collective-permute-start.9 = (f32[128,16]{1,0:T(8,128)S(1)}, f32[128,16]{1,0:T(8,128)S(1)}, u32[]{:S(2)}, u32[]{:S(2)}) collective-permute-start(f32[128,16]{1,0:T(8,128)S(1)} %collective-permute-done.8.refs_7_), channel_id=1, source_target_pairs={{0,4},{4,8},{8,12},{12,14},{14,10},{10,6},{6,2},{2,0},{1,5},{5,9},... | collective-permute-start | bytes 24584 | tf_op jit(solution)/shard_map/ppermute | solution.py:40
  18.2 6.2 %collective-permute-start.4 = (f32[128,16]{1,0:T(8,128)S(1)}, f32[128,16]{1,0:T(8,128)S(1)}, u32[]{:S(2)}, u32[]{:S(2)}) collective-permute-start(f32[128,16]{1,0:T(8,128)S(1)} %collective-permute-done.2.refs_9_), channel_id=1, source_target_pairs={{0,2},{4,0},{8,4},{12,8},{14,12},{10,14},{6,10},{2,6},{1,3},{5,1},... | collective-permute-start | bytes 24584 | tf_op jit(solution)/shard_map/ppermute | solution.py:40
  22.2 5.7 %collective-permute-start.10 = (f32[128,16]{1,0:T(8,128)S(1)}, f32[128,16]{1,0:T(8,128)S(1)}, u32[]{:S(2)}, u32[]{:S(2)}) collective-permute-start(f32[128,16]{1,0:T(8,128)S(1)} %collective-permute-done.9.refs_7_), channel_id=1, source_target_pairs={{0,4},{4,8},{8,12},{12,14},{14,10},{10,6},{6,2},{2,0},{1,5},{5,9},... | collective-permute-start | bytes 24584 | tf_op jit(solution)/shard_map/ppermute | solution.py:40
  23.8 11.0 %collective-permute-start.1 = (f32[128,16]{1,0:T(8,128)S(1)}, f32[128,16]{1,0:T(8,128)S(1)}, u32[]{:S(2)}, u32[]{:S(2)}) collective-permute-start(f32[128,16]{1,0:T(8,128)S(1)} %copy.13), channel_id=1, source_target_pairs={{0,1},{1,0},{2,3},{3,2},{4,5},{5,4},{6,7},{7,6},{8,9},{9,8},{10,11... | collective-permute-start | bytes 24584 | tf_op jit(solution)/shard_map/ppermute | solution.py:32
  23.8 11.1 %collective-permute-start.15 = (f32[128,16]{1,0:T(8,128)S(1)}, f32[128,16]{1,0:T(8,128)S(1)}, u32[]{:S(2)}, u32[]{:S(2)}) collective-permute-start(f32[128,16]{1,0:T(8,128)S(1)} %collective-permute-done.8.refs_7_), channel_id=1, source_target_pairs={{0,1},{1,0},{2,3},{3,2},{4,5},{5,4},{6,7},{7,6},{8,9},{9,8},{10,11... | collective-permute-start | bytes 24584 | tf_op jit(solution)/shard_map/ppermute | solution.py:32
  24.4 11.7 %collective-permute-start.3 = (f32[128,16]{1,0:T(8,128)S(1)}, f32[128,16]{1,0:T(8,128)S(1)}, u32[]{:S(2)}, u32[]{:S(2)}) collective-permute-start(f32[128,16]{1,0:T(8,128)S(1)} %collective-permute-done.2.refs_9_), channel_id=1, source_target_pairs={{0,1},{1,0},{2,3},{3,2},{4,5},{5,4},{6,7},{7,6},{8,9},{9,8},{10,11... | collective-permute-start | bytes 24584 | tf_op jit(solution)/shard_map/ppermute | solution.py:32
  27.9 8.2 %collective-permute-start.6 = (f32[128,16]{1,0:T(8,128)S(1)}, f32[128,16]{1,0:T(8,128)S(1)}, u32[]{:S(2)}, u32[]{:S(2)}) collective-permute-start(f32[128,16]{1,0:T(8,128)S(1)} %collective-permute-done.4.refs_9_), channel_id=1, source_target_pairs={{0,2},{4,0},{8,4},{12,8},{14,12},{10,14},{6,10},{2,6},{1,3},{5,1},... | collective-permute-start | bytes 24584 | tf_op jit(solution)/shard_map/ppermute | solution.py:40
  29.4 7.2 %collective-permute-start.11 = (f32[128,16]{1,0:T(8,128)S(1)}, f32[128,16]{1,0:T(8,128)S(1)}, u32[]{:S(2)}, u32[]{:S(2)}) collective-permute-start(f32[128,16]{1,0:T(8,128)S(1)} %collective-permute-done.10.refs_7_), channel_id=1, source_target_pairs={{0,4},{4,8},{8,12},{12,14},{14,10},{10,6},{6,2},{2,0},{1,5},{5,9},... | collective-permute-start | bytes 24584 | tf_op jit(solution)/shard_map/ppermute | solution.py:40
  36.6 2.8 %collective-permute-start.12 = (f32[128,16]{1,0:T(8,128)S(1)}, f32[128,16]{1,0:T(8,128)S(1)}, u32[]{:S(2)}, u32[]{:S(2)}) collective-permute-start(f32[128,16]{1,0:T(8,128)S(1)} %collective-permute-done.11.refs_7_), channel_id=1, source_target_pairs={{0,1},{1,0},{2,3},{3,2},{4,5},{5,4},{6,7},{7,6},{8,9},{9,8},{10,11... | collective-permute-start | bytes 24584 | tf_op jit(solution)/shard_map/ppermute | solution.py:32
  41.3 14.8 %collective-permute-start.19 = (bf16[128,2048]{1,0:T(8,128)(2,1)S(1)}, bf16[128,2048]{1,0:T(8,128)(2,1)S(1)}, u32[]{:S(2)}, u32[]{:S(2)}) collective-permute-start(bf16[128,2048]{1,0:T(8,128)(2,1)S(1)} %collective-permute-done.16), channel_id=1, source_target_pairs={{0,16},{16,0},{1,17},{17,1},{2,18},{18,2},{3,19},{19,3},{4,20},{20... | collective-permute-start | bytes 1572872 | tf_op jit(solution)/shard_map/ppermute | solution.py:47
  41.4 26.1 %collective-permute-start.18 = (bf16[128,2048]{1,0:T(8,128)(2,1)S(1)}, bf16[128,2048]{1,0:T(8,128)(2,1)S(1)}, u32[]{:S(2)}, u32[]{:S(2)}) collective-permute-start(bf16[128,2048]{1,0:T(8,128)(2,1)S(1)} %get-tuple-element.113), channel_id=1, source_target_pairs={{0,16},{16,0},{1,17},{17,1},{2,18},{18,2},{3,19},{19,3},{4,20},{20... | collective-permute-start | bytes 1572872 | tf_op jit(solution)/shard_map/ppermute | solution.py:47
  68.5 8.4 %collective-permute-start.21 = (bf16[128,1024]{1,0:T(8,128)(2,1)S(1)}, bf16[128,1024]{1,0:T(8,128)(2,1)S(1)}, u32[]{:S(2)}, u32[]{:S(2)}) collective-permute-start(bf16[128,1024]{1,0:T(8,128)(2,1)S(1)} %fusion), channel_id=1, source_target_pairs={{0,16},{16,0},{1,17},{17,1},{2,18},{18,2},{3,19},{19,3},{4,20},{20... | collective-permute-start | bytes 786440 | tf_op jit(solution)/shard_map/ppermute | solution.py:47
  79.0 14.7 %collective-permute-start.22 = (bf16[128,2048]{1,0:T(8,128)(2,1)}, bf16[128,2048]{1,0:T(8,128)(2,1)}, u32[]{:S(2)}, u32[]{:S(2)}) collective-permute-start(bf16[128,2048]{1,0:T(8,128)(2,1)} %get-tuple-element.116.refs_3_), channel_id=1, source_target_pairs={{0,4},{4,8},{8,12},{12,14},{14,10},{10,6},{6,2},{2,0},{1,5},{5,9},... | collective-permute-start | bytes 1572872 | tf_op jit(solution)/shard_map/ppermute | solution.py:40
  79.6 14.4 %collective-permute-start.23 = (bf16[128,2048]{1,0:T(8,128)(2,1)}, bf16[128,2048]{1,0:T(8,128)(2,1)}, u32[]{:S(2)}, u32[]{:S(2)}) collective-permute-start(bf16[128,2048]{1,0:T(8,128)(2,1)} %get-tuple-element.116.refs_3_), channel_id=1, source_target_pairs={{0,2},{4,0},{8,4},{12,8},{14,12},{10,14},{6,10},{2,6},{1,3},{5,1},... | collective-permute-start | bytes 1572872 | tf_op jit(solution)/shard_map/ppermute | solution.py:40
  94.0 2.9 %collective-permute-start.28 = (bf16[128,2048]{1,0:T(8,128)(2,1)}, bf16[128,2048]{1,0:T(8,128)(2,1)S(1)}, u32[]{:S(2)}, u32[]{:S(2)}) collective-permute-start(bf16[128,2048]{1,0:T(8,128)(2,1)} %collective-permute-done.23.refs_5_), channel_id=1, source_target_pairs={{0,1},{1,0},{2,3},{3,2},{4,5},{5,4},{6,7},{7,6},{8,9},{9,8},{10,11... | collective-permute-start | bytes 1572872 | tf_op jit(solution)/shard_map/ppermute | solution.py:32
  94.5 14.1 %collective-permute-start.25 = (bf16[128,2048]{1,0:T(8,128)(2,1)}, bf16[128,2048]{1,0:T(8,128)(2,1)S(1)}, u32[]{:S(2)}, u32[]{:S(2)}) collective-permute-start(bf16[128,2048]{1,0:T(8,128)(2,1)} %collective-permute-done.22.refs_3_), channel_id=1, source_target_pairs={{0,4},{4,8},{8,12},{12,14},{14,10},{10,6},{6,2},{2,0},{1,5},{5,9},... | collective-permute-start | bytes 1572872 | tf_op jit(solution)/shard_map/ppermute | solution.py:40
  96.0 13.8 %collective-permute-start.26 = (bf16[128,2048]{1,0:T(8,128)(2,1)}, bf16[128,2048]{1,0:T(8,128)(2,1)S(1)}, u32[]{:S(2)}, u32[]{:S(2)}) collective-permute-start(bf16[128,2048]{1,0:T(8,128)(2,1)} %collective-permute-done.23.refs_5_), channel_id=1, source_target_pairs={{0,2},{4,0},{8,4},{12,8},{14,12},{10,14},{6,10},{2,6},{1,3},{5,1},... | collective-permute-start | bytes 1572872 | tf_op jit(solution)/shard_map/ppermute | solution.py:40
  96.8 13.1 %collective-permute-start.29 = (bf16[128,2048]{1,0:T(8,128)(2,1)S(1)}, bf16[128,2048]{1,0:T(8,128)(2,1)S(1)}, u32[]{:S(2)}, u32[]{:S(2)}) collective-permute-start(bf16[128,2048]{1,0:T(8,128)(2,1)S(1)} %get-tuple-element.136), channel_id=1, source_target_pairs={{0,1},{1,0},{2,3},{3,2},{4,5},{5,4},{6,7},{7,6},{8,9},{9,8},{10,11... | collective-permute-start | bytes 1572872 | tf_op jit(solution)/shard_map/ppermute | solution.py:32
  110.0 2.6 %collective-permute-start.33 = (bf16[128,2048]{1,0:T(8,128)(2,1)S(1)}, bf16[128,2048]{1,0:T(8,128)(2,1)S(1)}, u32[]{:S(2)}, u32[]{:S(2)}) collective-permute-start(bf16[128,2048]{1,0:T(8,128)(2,1)S(1)} %collective-permute-done.26.refs_5_), channel_id=1, source_target_pairs={{0,1},{1,0},{2,3},{3,2},{4,5},{5,4},{6,7},{7,6},{8,9},{9,8},{10,11... | collective-permute-start | bytes 1572872 | tf_op jit(solution)/shard_map/ppermute | solution.py:32
  110.5 13.9 %collective-permute-start.30 = (bf16[128,2048]{1,0:T(8,128)(2,1)S(1)}, bf16[128,2048]{1,0:T(8,128)(2,1)S(1)}, u32[]{:S(2)}, u32[]{:S(2)}) collective-permute-start(bf16[128,2048]{1,0:T(8,128)(2,1)S(1)} %collective-permute-done.25.refs_3_), channel_id=1, source_target_pairs={{0,4},{4,8},{8,12},{12,14},{14,10},{10,6},{6,2},{2,0},{1,5},{5,9},... | collective-permute-start | bytes 1572872 | tf_op jit(solution)/shard_map/ppermute | solution.py:40
  112.0 13.6 %collective-permute-start.31 = (bf16[128,2048]{1,0:T(8,128)(2,1)S(1)}, bf16[128,2048]{1,0:T(8,128)(2,1)S(1)}, u32[]{:S(2)}, u32[]{:S(2)}) collective-permute-start(bf16[128,2048]{1,0:T(8,128)(2,1)S(1)} %collective-permute-done.26.refs_5_), channel_id=1, source_target_pairs={{0,2},{4,0},{8,4},{12,8},{14,12},{10,14},{6,10},{2,6},{1,3},{5,1},... | collective-permute-start | bytes 1572872 | tf_op jit(solution)/shard_map/ppermute | solution.py:40
  112.6 13.1 %collective-permute-start.34 = (bf16[128,2048]{1,0:T(8,128)(2,1)S(1)}, bf16[128,2048]{1,0:T(8,128)(2,1)S(1)}, u32[]{:S(2)}, u32[]{:S(2)}) collective-permute-start(bf16[128,2048]{1,0:T(8,128)(2,1)S(1)} %get-tuple-element.156), channel_id=1, source_target_pairs={{0,1},{1,0},{2,3},{3,2},{4,5},{5,4},{6,7},{7,6},{8,9},{9,8},{10,11... | collective-permute-start | bytes 1572872 | tf_op jit(solution)/shard_map/ppermute | solution.py:32
  112.7 12.9 %collective-permute-start.35 = (bf16[128,2048]{1,0:T(8,128)(2,1)S(1)}, bf16[128,2048]{1,0:T(8,128)(2,1)S(1)}, u32[]{:S(2)}, u32[]{:S(2)}) collective-permute-start(bf16[128,2048]{1,0:T(8,128)(2,1)S(1)} %get-tuple-element.158), channel_id=1, source_target_pairs={{0,1},{1,0},{2,3},{3,2},{4,5},{5,4},{6,7},{7,6},{8,9},{9,8},{10,11... | collective-permute-start | bytes 1572872 | tf_op jit(solution)/shard_map/ppermute | solution.py:32
  125.7 3.1 %collective-permute-start.39 = (bf16[128,2048]{1,0:T(8,128)(2,1)S(1)}, bf16[128,2048]{1,0:T(8,128)(2,1)S(1)}, u32[]{:S(2)}, u32[]{:S(2)}) collective-permute-start(bf16[128,2048]{1,0:T(8,128)(2,1)S(1)} %collective-permute-done.31.refs_5_), channel_id=1, source_target_pairs={{0,1},{1,0},{2,3},{3,2},{4,5},{5,4},{6,7},{7,6},{8,9},{9,8},{10,11... | collective-permute-start | bytes 1572872 | tf_op jit(solution)/shard_map/ppermute | solution.py:32
  126.2 10.1 %collective-permute-start.40 = (bf16[128,2048]{1,0:T(8,128)(2,1)S(1)}, bf16[128,2048]{1,0:T(8,128)(2,1)S(1)}, u32[]{:S(2)}, u32[]{:S(2)}) collective-permute-start(bf16[128,2048]{1,0:T(8,128)(2,1)S(1)} %get-tuple-element.174), channel_id=1, source_target_pairs={{0,1},{1,0},{2,3},{3,2},{4,5},{5,4},{6,7},{7,6},{8,9},{9,8},{10,11... | collective-permute-start | bytes 1572872 | tf_op jit(solution)/shard_map/ppermute | solution.py:32
  126.3 10.0 %collective-permute-start.41 = (bf16[128,2048]{1,0:T(8,128)(2,1)S(1)}, bf16[128,2048]{1,0:T(8,128)(2,1)S(1)}, u32[]{:S(2)}, u32[]{:S(2)}) collective-permute-start(bf16[128,2048]{1,0:T(8,128)(2,1)S(1)} %get-tuple-element.176), channel_id=1, source_target_pairs={{0,1},{1,0},{2,3},{3,2},{4,5},{5,4},{6,7},{7,6},{8,9},{9,8},{10,11... | collective-permute-start | bytes 1572872 | tf_op jit(solution)/shard_map/ppermute | solution.py:32
  126.7 8.3 %collective-permute-start.36 = (bf16[64,2048]{1,0:T(8,128)(2,1)S(1)}, bf16[64,2048]{1,0:T(8,128)(2,1)S(1)}, u32[]{:S(2)}, u32[]{:S(2)}) collective-permute-start(bf16[64,2048]{1,0:T(8,128)(2,1)S(1)} %slice.98), channel_id=1, source_target_pairs={{0,4},{4,8},{8,12},{12,14},{14,10},{10,6},{6,2},{2,0},{1,5},{5,9},... | collective-permute-start | bytes 786440 | tf_op jit(solution)/shard_map/ppermute | solution.py:40
  128.3 8.0 %collective-permute-start.37 = (bf16[64,2048]{1,0:T(8,128)(2,1)S(1)}, bf16[64,2048]{1,0:T(8,128)(2,1)S(1)}, u32[]{:S(2)}, u32[]{:S(2)}) collective-permute-start(bf16[64,2048]{1,0:T(8,128)(2,1)S(1)} %slice.99), channel_id=1, source_target_pairs={{0,2},{4,0},{8,4},{12,8},{14,12},{10,14},{6,10},{2,6},{1,3},{5,1},... | collective-permute-start | bytes 786440 | tf_op jit(solution)/shard_map/ppermute | solution.py:40
  138.2 3.1 %collective-permute-start.44 = (bf16[128,2048]{1,0:T(8,128)(2,1)S(1)}, bf16[128,2048]{1,0:T(8,128)(2,1)S(1)}, u32[]{:S(2)}, u32[]{:S(2)}) collective-permute-start(bf16[128,2048]{1,0:T(8,128)(2,1)S(1)} %get-tuple-element.198), channel_id=1, source_target_pairs={{0,1},{1,0},{2,3},{3,2},{4,5},{5,4},{6,7},{7,6},{8,9},{9,8},{10,11... | collective-permute-start | bytes 1572872 | tf_op jit(solution)/shard_map/ppermute | solution.py:32
  138.4 3.0 %collective-permute-start.45 = (bf16[128,2048]{1,0:T(8,128)(2,1)S(1)}, bf16[128,2048]{1,0:T(8,128)(2,1)S(1)}, u32[]{:S(2)}, u32[]{:S(2)}) collective-permute-start(bf16[128,2048]{1,0:T(8,128)(2,1)S(1)} %get-tuple-element.200), channel_id=1, source_target_pairs={{0,1},{1,0},{2,3},{3,2},{4,5},{5,4},{6,7},{7,6},{8,9},{9,8},{10,11... | collective-permute-start | bytes 1572872 | tf_op jit(solution)/shard_map/ppermute | solution.py:32
  143.5 8.4 %collective-permute-start.57 = (bf16[64,2048]{1,0:T(8,128)(2,1)S(1)}, bf16[64,2048]{1,0:T(8,128)(2,1)S(1)}, u32[]{:S(2)}, u32[]{:S(2)}) collective-permute-start(bf16[64,2048]{1,0:T(8,128)(2,1)S(1)} %get-tuple-element.227), channel_id=1, source_target_pairs={{0,2},{4,0},{8,4},{12,8},{14,12},{10,14},{6,10},{2,6},{1,3},{5,1},... | collective-permute-start | bytes 786440 | tf_op jit(solution)/shard_map/ppermute | solution.py:40
  144.1 9.0 %collective-permute-start.47 = (bf16[64,2048]{1,0:T(8,128)(2,1)S(1)}, bf16[64,2048]{1,0:T(8,128)(2,1)S(1)}, u32[]{:S(2)}, u32[]{:S(2)}) collective-permute-start(bf16[64,2048]{1,0:T(8,128)(2,1)S(1)} %get-tuple-element.228), channel_id=1, source_target_pairs={{0,4},{4,8},{8,12},{12,14},{14,10},{10,6},{6,2},{2,0},{1,5},{5,9},... | collective-permute-start | bytes 786440 | tf_op jit(solution)/shard_map/ppermute | solution.py:40
  152.1 9.3 %collective-permute-start.51 = (bf16[64,2048]{1,0:T(8,128)(2,1)S(1)}, bf16[64,2048]{1,0:T(8,128)(2,1)S(1)}, u32[]{:S(2)}, u32[]{:S(2)}) collective-permute-start(bf16[64,2048]{1,0:T(8,128)(2,1)S(1)} %get-tuple-element.226), channel_id=1, source_target_pairs={{0,2},{4,0},{8,4},{12,8},{14,12},{10,14},{6,10},{2,6},{1,3},{5,1},... | collective-permute-start | bytes 786440 | tf_op jit(solution)/shard_map/ppermute | solution.py:40
  152.6 12.6 %collective-permute-start.58 = (bf16[64,2048]{1,0:T(8,128)(2,1)S(1)}, bf16[64,2048]{1,0:T(8,128)(2,1)S(1)}, u32[]{:S(2)}, u32[]{:S(2)}) collective-permute-start(bf16[64,2048]{1,0:T(8,128)(2,1)S(1)} %get-tuple-element.225), channel_id=1, source_target_pairs={{0,2},{4,0},{8,4},{12,8},{14,12},{10,14},{6,10},{2,6},{1,3},{5,1},... | collective-permute-start | bytes 786440 | tf_op jit(solution)/shard_map/ppermute | solution.py:40
  153.3 13.2 %collective-permute-start.48 = (bf16[64,2048]{1,0:T(8,128)(2,1)S(1)}, bf16[64,2048]{1,0:T(8,128)(2,1)S(1)}, u32[]{:S(2)}, u32[]{:S(2)}) collective-permute-start(bf16[64,2048]{1,0:T(8,128)(2,1)S(1)} %get-tuple-element.234), channel_id=1, source_target_pairs={{0,4},{4,8},{8,12},{12,14},{14,10},{10,6},{6,2},{2,0},{1,5},{5,9},... | collective-permute-start | bytes 786440 | tf_op jit(solution)/shard_map/ppermute | solution.py:40
  154.9 11.6 %collective-permute-start.54 = (bf16[64,2048]{1,0:T(8,128)(2,1)S(1)}, bf16[64,2048]{1,0:T(8,128)(2,1)S(1)}, u32[]{:S(2)}, u32[]{:S(2)}) collective-permute-start(bf16[64,2048]{1,0:T(8,128)(2,1)S(1)} %get-tuple-element.233), channel_id=1, source_target_pairs={{0,4},{4,8},{8,12},{12,14},{14,10},{10,6},{6,2},{2,0},{1,5},{5,9},... | collective-permute-start | bytes 786440 | tf_op jit(solution)/shard_map/ppermute | solution.py:40
  165.5 9.3 %collective-permute-start.52 = (bf16[64,2048]{1,0:T(8,128)(2,1)S(1)}, bf16[64,2048]{1,0:T(8,128)(2,1)S(1)}, u32[]{:S(2)}, u32[]{:S(2)}) collective-permute-start(bf16[64,2048]{1,0:T(8,128)(2,1)S(1)} %get-tuple-element.224), channel_id=1, source_target_pairs={{0,2},{4,0},{8,4},{12,8},{14,12},{10,14},{6,10},{2,6},{1,3},{5,1},... | collective-permute-start | bytes 786440 | tf_op jit(solution)/shard_map/ppermute | solution.py:40
  166.1 11.7 %collective-permute-start.59 = (bf16[64,2048]{1,0:T(8,128)(2,1)S(1)}, bf16[64,2048]{1,0:T(8,128)(2,1)S(1)}, u32[]{:S(2)}, u32[]{:S(2)}) collective-permute-start(bf16[64,2048]{1,0:T(8,128)(2,1)S(1)} %get-tuple-element.223), channel_id=1, source_target_pairs={{0,2},{4,0},{8,4},{12,8},{14,12},{10,14},{6,10},{2,6},{1,3},{5,1},... | collective-permute-start | bytes 786440 | tf_op jit(solution)/shard_map/ppermute | solution.py:40
  166.8 12.3 %collective-permute-start.49 = (bf16[64,2048]{1,0:T(8,128)(2,1)S(1)}, bf16[64,2048]{1,0:T(8,128)(2,1)S(1)}, u32[]{:S(2)}, u32[]{:S(2)}) collective-permute-start(bf16[64,2048]{1,0:T(8,128)(2,1)S(1)} %get-tuple-element.232), channel_id=1, source_target_pairs={{0,4},{4,8},{8,12},{12,14},{14,10},{10,6},{6,2},{2,0},{1,5},{5,9},... | collective-permute-start | bytes 786440 | tf_op jit(solution)/shard_map/ppermute | solution.py:40
  168.4 10.6 %collective-permute-start.55 = (bf16[64,2048]{1,0:T(8,128)(2,1)S(1)}, bf16[64,2048]{1,0:T(8,128)(2,1)S(1)}, u32[]{:S(2)}, u32[]{:S(2)}) collective-permute-start(bf16[64,2048]{1,0:T(8,128)(2,1)S(1)} %get-tuple-element.231), channel_id=1, source_target_pairs={{0,4},{4,8},{8,12},{12,14},{14,10},{10,6},{6,2},{2,0},{1,5},{5,9},... | collective-permute-start | bytes 786440 | tf_op jit(solution)/shard_map/ppermute | solution.py:40
  178.0 8.5 %collective-permute-start.53 = (bf16[64,2048]{1,0:T(8,128)(2,1)S(1)}, bf16[64,2048]{1,0:T(8,128)(2,1)S(1)}, u32[]{:S(2)}, u32[]{:S(2)}) collective-permute-start(bf16[64,2048]{1,0:T(8,128)(2,1)S(1)} %get-tuple-element.222), channel_id=1, source_target_pairs={{0,2},{4,0},{8,4},{12,8},{14,12},{10,14},{6,10},{2,6},{1,3},{5,1},... | collective-permute-start | bytes 786440 | tf_op jit(solution)/shard_map/ppermute | solution.py:40
  178.6 10.8 %collective-permute-start.60 = (bf16[64,2048]{1,0:T(8,128)(2,1)S(1)}, bf16[64,2048]{1,0:T(8,128)(2,1)S(1)}, u32[]{:S(2)}, u32[]{:S(2)}) collective-permute-start(bf16[64,2048]{1,0:T(8,128)(2,1)S(1)} %get-tuple-element.221), channel_id=1, source_target_pairs={{0,2},{4,0},{8,4},{12,8},{14,12},{10,14},{6,10},{2,6},{1,3},{5,1},... | collective-permute-start | bytes 786440 | tf_op jit(solution)/shard_map/ppermute | solution.py:40
  179.3 10.1 %collective-permute-start.50 = (bf16[64,2048]{1,0:T(8,128)(2,1)S(1)}, bf16[64,2048]{1,0:T(8,128)(2,1)S(1)}, u32[]{:S(2)}, u32[]{:S(2)}) collective-permute-start(bf16[64,2048]{1,0:T(8,128)(2,1)S(1)} %get-tuple-element.230), channel_id=1, source_target_pairs={{0,4},{4,8},{8,12},{12,14},{14,10},{10,6},{6,2},{2,0},{1,5},{5,9},... | collective-permute-start | bytes 786440 | tf_op jit(solution)/shard_map/ppermute | solution.py:40
  180.9 9.2 %collective-permute-start.56 = (bf16[64,2048]{1,0:T(8,128)(2,1)S(1)}, bf16[64,2048]{1,0:T(8,128)(2,1)S(1)}, u32[]{:S(2)}, u32[]{:S(2)}) collective-permute-start(bf16[64,2048]{1,0:T(8,128)(2,1)S(1)} %get-tuple-element.229), channel_id=1, source_target_pairs={{0,4},{4,8},{8,12},{12,14},{14,10},{10,6},{6,2},{2,0},{1,5},{5,9},... | collective-permute-start | bytes 786440 | tf_op jit(solution)/shard_map/ppermute | solution.py:40
  (45 other events, 474.9 us)
Sparse Core Ops, SparseCore 0:
  8.9 54.0 all-gather.1

commit v4 on v2

--- a/solution.py
+++ b/solution.py
@@ -112,6 +112,17 @@
     tokens_ref[:, D:] = terms.astype(jnp.bfloat16)
 
 
+def final_kernel(residual_ref, own_ref, sibling_ref, *refs):
+    *arrived_refs, out_ref = refs
+    rows = arrived_refs[0].shape[0]
+    for half in range(2):
+        at = pl.ds(half * rows, rows)
+        total = residual_ref[at, :]
+        for ref in (own_ref.at[at], sibling_ref.at[at], *arrived_refs[2 * half : 2 * half + 2]):
+            total = total + ref[...].astype(jnp.float32)
+        out_ref[0, at, :] = total.astype(jnp.bfloat16)
+
+
 def expert_kernel(experts_all, groups, parts, expert_ref, *refs):
     gate_ref, up_ref, down_ref, *refs = refs
     block_refs, out_refs = refs[: 2 * groups * parts], refs[2 * groups * parts :]
@@ -203,13 +214,15 @@
     own_heads, other_heads = attended[0], attended[1]
     sibling_heads = swap_cores(other_heads)
     projected = []
-    for back in range(n_ctx):
+    for back in list(range(1, n_ctx)) + [0]:
         heads = [rotate(own_heads, "ctx", back), rotate(sibling_heads, "ctx", back)]
         from_sibling = swap_cores(times_columns(heads[1]).astype(jnp.bfloat16))
-        part = times_columns(heads[0]) + from_sibling.astype(jnp.float32)
+        part = lax.optimization_barrier(times_columns(heads[0]))
+        part = part + from_sibling.astype(jnp.float32)
         if back:
             part = rotate(part.astype(jnp.bfloat16), "ctx", -back)
         projected.append(part)
+    projected = projected[-1:] + projected[:-1]
 
     local_experts = w_gate.shape[0]
     experts_all = n_exp * local_experts
@@ -268,19 +281,22 @@
     results = experts_on([(0, [tokens], [swap_cores(tokens)])])
     forward, backward, results = barrier((forward, backward, results))
     for step in range(1, far):
-        chips = [
-            (n_chip - step, [forward], [swap_cores(forward)]),
-            (step, [backward], [swap_cores(backward)]),
-        ]
+        ours = forward, backward
+        swapped = swap_cores(forward), swap_cores(backward)
         forward, backward = send_on(forward, backward, step + 1)
+        if step + 1 < far:
+            swapped, results = barrier((swapped, results))
         sums |= swap_results(results)
-        results = experts_on(chips)
+        results = experts_on(
+            [(n_chip - step, [ours[0]], [swapped[0]]), (step, [ours[1]], [swapped[1]])]
+        )
         forward, backward, results, sums = barrier((forward, backward, results, sums))
-    halves = [forward, backward]
-    swapped = [swap_cores(half) for half in halves]
+    swapped = [swap_cores(forward), swap_cores(backward)]
+    swapped, results = barrier((swapped, results))
     sums |= swap_results(results)
-    halves, swapped, sums = barrier((halves, swapped, sums))
-    sums |= swap_results(experts_on([(far, halves, swapped)]))
+    results = experts_on([(far, [forward, backward], swapped)])
+    results, sums = barrier((results, sums))
+    sums |= swap_results(results)
 
     def total_at(direction, half, hop, carried):
         offset = hop if direction > 0 else n_chip - hop
@@ -296,11 +312,14 @@
         running_sum(1, 0, far) + running_sum(-1, 0, far - 1),
         running_sum(1, 1, far - 1) + running_sum(-1, 1, far),
     ]
-    result = [
-        total_of([residual] + sums[0] + arrived[half], half).astype(jnp.bfloat16)
-        for half in range(2)
-    ]
-    return jnp.concatenate(result, axis=0)[None]
+    return pl.pallas_call(
+        final_kernel,
+        out_shape=jax.ShapeDtypeStruct((1, rows, D), jnp.bfloat16),
+        in_specs=[vmem()] * 7,
+        out_specs=vmem(),
+        compiler_params=pltpu.CompilerParams(vmem_limit_bytes=16 * 1024 * 1024),
+        name="final",
+    )(residual, *sums[0], *arrived[0], *arrived[1])
 
 
 def solution(mesh):

time: 199 us -> 197 us (0.990)
  waiting for transfers between devices: 113 us -> 111 us
  transfers between devices with their start and end apart: 47 -> 47, of which waited for: 27 -> 27; matrix products, arithmetic and copies ran while one was open for 5% -> 5% of each run, Pallas kernels for 10% -> 12%
where the time goes in v4:
time: 197 us
  waiting for transfers between devices  111 us (56%)
  starting transfers between devices  33.5 us (17%)
  Pallas kernels  24.7 us (13%)
  between operations  13.7 us (7%)
  matrix products  6.48 us (3%)
  local copies, waits for them, and re-layouts  5.64 us (3%)
    ppermute x22, waiting for transfers between devices, round_ring(): return lax.ppermute(block, 'exp', route)  61.2 us
    ppermute x22, starting transfers between devices, round_ring(): return lax.ppermute(block, 'exp', route)  22.5 us
    ppermute x4, waiting for transfers between devices, rotate(): lax.ppermute(block, axis, [(i, (i + distance) % n) for i in range(n)])  22.5 us
    all_gather x1, waiting for transfers between devices, body(): lax.all_gather(lax.dynamic_slice_in_dim(out_proj, position * wide, wide,...  21.7 us
    pallas_call x5, Pallas kernels, run_expert(): pl.pallas_call(functools.partial(expert_kernel, experts_all, groups, part...  20.4 us
    ppermute x4, starting transfers between devices, rotate(): lax.ppermute(block, axis, [(i, (i + distance) % n) for i in range(n)])  6.59 us
    dot_general x4, matrix products, times_columns(): return jnp.dot(block, columns, preferred_element_type=jnp.float32)  6.48 us
    ppermute x20, waiting for transfers between devices, swap_cores(): return lax.ppermute(block, 'exp', [(i, i ^ 1) for i in range(n)])  5.82 us
  transfers between devices with their start and end apart: 47, of which 27 were waited for; matrix products, arithmetic and copies ran while one was open for 5% of the time, Pallas kernels for 12%

profile of v4, /device:TPU:0, one launch (start us, length us, event | category | flops | bytes accessed | tf_op | source)
XLA Modules:
  0.0 196.9 jit_solution(4875734376135383540)
XLA Ops:
  6.6 1.2 copy-done
  8.6 3.0 %collective-permute-start = (bf16[128,512]{1,0:T(8,128)(2,1)}, bf16[128,512]{1,0:T(8,128)(2,1)S(1)}, u32[]{:S(2)}, u32[]{:S(2)}) collective-permute-start(bf16[128,512]{1,0:T(8,128)(2,1)} %bitcast.42), channel_id=1, source_target_pairs={{0,16},{16,0},{1,17},{17,1},{2,18},{18,2},{3,19},{19,3},{4,20},{20... | collective-permute-start | bytes 393224 | tf_op jit(solution)/shard_map/ppermute | solution.py:49
  11.7 3.6 %collective-permute-done.refs_1_ = bf16[128,512]{1,0:T(8,128)(2,1)S(1)} collective-permute-done((bf16[128,512]{1,0:T(8,128)(2,1)}, bf16[128,512]{1,0:T(8,128)(2,1)S(1)}, u32[]{:S(2)}, u32[]{:S(2)}) %collective-permute-start) | collective-permute-done | bytes 131104 | tf_op jit(solution)/shard_map/ppermute | solution.py:49
  15.4 1.2 copy-done.4
  17.5 2.6 %attention.1 = bf16[2,128,2048]{2,1,0:T(8,128)(2,1)S(1)} custom-call(s32[2]{0:T(128)S(1)} %pad_add_fusion.pos_ref, bf16[128,4096]{1,0:T(8,128)(2,1)S(1)} %bitcast.38, bf16[128,512]{1,0:T(8,128)(2,1)S(1)} %bitcast.43, bf16[128,512]{1,0:T(8,128)(2,1)S(1)} %collective-permute-done.refs_1_), custom_call_target="tpu_custom_call" | custom-call | tf_op jit(solution)/shard_map/attention/pallas_call | solution.py:160
  20.1 0.9 slice_bitcast_fusion.1
  21.0 1.9 collective-permute-done.1
  22.9 1.7 collective-permute-start.4
  25.2 12.6 %collective-permute-done.4 = bf16[128,2048]{1,0:T(8,128)(2,1)} collective-permute-done((bf16[128,2048]{1,0:T(8,128)(2,1)S(1)}, bf16[128,2048]{1,0:T(8,128)(2,1)}, u32[]{:S(2)}, u32[]{:S(2)}) %collective-permute-start.4) | collective-permute-done | bytes 524320 | tf_op jit(solution)/shard_map/ppermute | solution.py:49
  37.8 21.7 %all-gather.2.cloned.1.call-done = bf16[2048,1024]{1,0:T(8,128)(2,1)} async-done(((bf16[256,1024]{1,0:T(8,128)(2,1)}), bf16[2048,1024]{1,0:T(8,128)(2,1)}) %all-gather.2.cloned.1.call-update) | async-done | bytes 4194320 | tf_op jit(solution)/shard_map/all_gather | solution.py:200
  59.5 3.2 %convolution_convert_fusion = bf16[128,1024]{1,0:T(8,128)(2,1)S(1)} fusion(bf16[128,2048]{1,0:T(8,128)(2,1)} %collective-permute-done.4, bf16[2048,1024]{1,0:T(8,128)(2,1)} %all-gather.2.cloned.1.call-done), kind=kOutput, calls=%fused_computation | convolution fusion | flops 537001984 | bytes 4980736 | tf_op jit(solution)/shard_map/dot_general | solution.py:209
  63.1 1.8 fusion.1
  66.1 1.5 collective-permute-start.6
  68.4 6.2 %collective-permute-done.6.refs_1_ = bf16[128,1024]{1,0:T(8,128)(2,1)S(1)} collective-permute-done((bf16[128,1024]{1,0:T(8,128)(2,1)S(1)}, bf16[128,1024]{1,0:T(8,128)(2,1)S(1)}, u32[]{:S(2)}, u32[]{:S(2)}) %collective-permute-start.6) | collective-permute-done | bytes 262176 | tf_op jit(solution)/shard_map/ppermute | solution.py:49
  75.3 1.5 collective-permute-start.7
  77.4 2.6 %experts.5 = (bf16[128,2048]{1,0:T(8,128)(2,1)S(1)}, bf16[128,2048]{1,0:T(8,128)(2,1)S(1)}) custom-call(s32[1]{0:T(128)} %bitcast.9.expert_ref, bf16[2048,768]{1,0:T(8,128)(2,1)S(1)} %bitcast.23, bf16[2048,768]{1,0:T(8,128)(2,1)S(1)} %bitcast.28, bf16[768,2048]{1,0:T(8,128)(2,1)S(1)} %bitcast.33, bf16[128,2176]{1,0:T(8,128)(2,1)S(1)} %get-tuple-element.96.refs_3_, ...), custom_call_target="tpu_custom_call" | custom-call | flops 2415919104 | bytes 11534336 | tf_op jit(solution)/shard_map/experts/pallas_call | solution.py:175
  80.0 10.3 %collective-permute-done.7.refs_3_ = bf16[128,2176]{1,0:T(8,128)(2,1)S(1)} collective-permute-done((bf16[128,2176]{1,0:T(8,128)(2,1)S(1)}, bf16[128,2176]{1,0:T(8,128)(2,1)S(1)}, u32[]{:S(2)}, u32[]{:S(2)}) %collective-permute-start.7) | collective-permute-done | bytes 557088 | tf_op jit(solution)/shard_map/ppermute | solution.py:42
  90.3 1.2 collective-permute-done.8.refs_5_
  92.0 1.5 collective-permute-start.10
  94.4 5.1 %experts.6 = (bf16[128,2048]{1,0:T(8,128)(2,1)S(1)}, bf16[128,2048]{1,0:T(8,128)(2,1)S(1)}, bf16[128,2048]{1,0:T(8,128)(2,1)S(1)}, bf16[128,2048]{1,0:T(8,128)(2,1)S(1)}) custom-call(s32[1]{0:T(128)} %bitcast.9.expert_ref, bf16[2048,768]{1,0:T(8,128)(2,1)S(1)} %bitcast.24, bf16[2048,768]{1,0:T(8,128)(2,1)S(1)} %bitcast.29, bf16[768,2048]{1,0:T(8,128)(2,1)S(1)} %bitcast.34, ...), custom_call_target="tpu_custom_call" | custom-call | flops 4831838208 | bytes 13631488 | tf_op jit(solution)/shard_map/experts/pallas_call | solution.py:175
  99.5 7.1 %collective-permute-done.10.refs_3_ = bf16[128,2176]{1,0:T(8,128)(2,1)S(1)} collective-permute-done((bf16[128,2176]{1,0:T(8,128)(2,1)S(1)}, bf16[128,2176]{1,0:T(8,128)(2,1)S(1)}, u32[]{:S(2)}, u32[]{:S(2)}) %collective-permute-start.10) | collective-permute-done | bytes 557088 | tf_op jit(solution)/shard_map/ppermute | solution.py:42
  106.6 1.2 collective-permute-done.11.refs_5_
  108.3 1.5 collective-permute-start.15
  111.0 5.1 %experts.7 = (bf16[128,2048]{1,0:T(8,128)(2,1)S(1)}, bf16[128,2048]{1,0:T(8,128)(2,1)S(1)}, bf16[128,2048]{1,0:T(8,128)(2,1)S(1)}, bf16[128,2048]{1,0:T(8,128)(2,1)S(1)}) custom-call(s32[1]{0:T(128)} %bitcast.9.expert_ref, bf16[2048,768]{1,0:T(8,128)(2,1)S(1)} %bitcast.25, bf16[2048,768]{1,0:T(8,128)(2,1)S(1)} %bitcast.30, bf16[768,2048]{1,0:T(8,128)(2,1)S(1)} %bitcast.35, ...), custom_call_target="tpu_custom_call" | custom-call | flops 4831838208 | bytes 13631488 | tf_op jit(solution)/shard_map/experts/pallas_call | solution.py:175
  116.1 6.7 %collective-permute-done.15.refs_3_ = bf16[128,2176]{1,0:T(8,128)(2,1)S(1)} collective-permute-done((bf16[128,2176]{1,0:T(8,128)(2,1)S(1)}, bf16[128,2176]{1,0:T(8,128)(2,1)S(1)}, u32[]{:S(2)}, u32[]{:S(2)}) %collective-permute-start.15) | collective-permute-done | bytes 557088 | tf_op jit(solution)/shard_map/ppermute | solution.py:42
  122.8 1.2 collective-permute-done.16.refs_5_
  126.0 1.2 collective-permute-start.22
  127.2 5.1 %experts.8 = (bf16[128,2048]{1,0:T(8,128)(2,1)S(1)}, bf16[128,2048]{1,0:T(8,128)(2,1)S(1)}, bf16[128,2048]{1,0:T(8,128)(2,1)S(1)}, bf16[128,2048]{1,0:T(8,128)(2,1)S(1)}) custom-call(s32[1]{0:T(128)} %bitcast.9.expert_ref, bf16[2048,768]{1,0:T(8,128)(2,1)S(1)} %bitcast.26, bf16[2048,768]{1,0:T(8,128)(2,1)S(1)} %bitcast.31, bf16[768,2048]{1,0:T(8,128)(2,1)S(1)} %bitcast.36, ...), custom_call_target="tpu_custom_call" | custom-call | flops 4831838208 | bytes 13631488 | tf_op jit(solution)/shard_map/experts/pallas_call | solution.py:175
  132.2 1.5 collective-permute-done.21.refs_3_
  135.2 1.0 collective-permute-done.27.refs_5_
  137.2 2.6 %experts.9 = (bf16[128,2048]{1,0:T(8,128)(2,1)S(1)}, bf16[128,2048]{1,0:T(8,128)(2,1)S(1)}) custom-call(s32[1]{0:T(128)} %bitcast.9.expert_ref, bf16[2048,768]{1,0:T(8,128)(2,1)S(1)} %bitcast.27, bf16[2048,768]{1,0:T(8,128)(2,1)S(1)} %bitcast.32, bf16[768,2048]{1,0:T(8,128)(2,1)S(1)} %bitcast.37, bf16[64,2176]{1,0:T(8,128)(2,1)S(1)} %collective-permute-done.21.refs_3_, ...), custom_call_target="tpu_custom_call" | custom-call | flops 2415919104 | bytes 11534336 | tf_op jit(solution)/shard_map/experts/pallas_call | solution.py:175
  140.0 1.8 collective-permute-done.31
  142.8 1.2 collective-permute-start.32
  144.0 6.3 %collective-permute-done.42 = bf16[64,2048]{1,0:T(8,128)(2,1)S(1)} collective-permute-done((bf16[64,2048]{1,0:T(8,128)(2,1)S(1)}, bf16[64,2048]{1,0:T(8,128)(2,1)S(1)}, u32[]{:S(2)}, u32[]{:S(2)}) %collective-permute-start.42) | collective-permute-done | bytes 262176 | tf_op jit(solution)/shard_map/ppermute | solution.py:42
  152.2 1.5 collective-permute-start.33
  153.7 1.2 collective-permute-start.39
  154.9 4.9 %collective-permute-done.36 = bf16[64,2048]{1,0:T(8,128)(2,1)S(1)} collective-permute-done((bf16[64,2048]{1,0:T(8,128)(2,1)S(1)}, bf16[64,2048]{1,0:T(8,128)(2,1)S(1)}, u32[]{:S(2)}, u32[]{:S(2)}) %collective-permute-start.36) | collective-permute-done | bytes 262176 | tf_op jit(solution)/shard_map/ppermute | solution.py:42
  159.8 3.9 %collective-permute-done.43 = bf16[64,2048]{1,0:T(8,128)(2,1)S(1)} collective-permute-done((bf16[64,2048]{1,0:T(8,128)(2,1)S(1)}, bf16[64,2048]{1,0:T(8,128)(2,1)S(1)}, u32[]{:S(2)}, u32[]{:S(2)}) %collective-permute-start.43) | collective-permute-done | bytes 262176 | tf_op jit(solution)/shard_map/ppermute | solution.py:42
  165.7 1.5 collective-permute-start.34
  167.2 1.2 collective-permute-start.40
  168.3 4.9 %collective-permute-done.37 = bf16[64,2048]{1,0:T(8,128)(2,1)S(1)} collective-permute-done((bf16[64,2048]{1,0:T(8,128)(2,1)S(1)}, bf16[64,2048]{1,0:T(8,128)(2,1)S(1)}, u32[]{:S(2)}, u32[]{:S(2)}) %collective-permute-start.37) | collective-permute-done | bytes 262176 | tf_op jit(solution)/shard_map/ppermute | solution.py:42
  173.2 3.0 %collective-permute-done.44 = bf16[64,2048]{1,0:T(8,128)(2,1)S(1)} collective-permute-done((bf16[64,2048]{1,0:T(8,128)(2,1)S(1)}, bf16[64,2048]{1,0:T(8,128)(2,1)S(1)}, u32[]{:S(2)}, u32[]{:S(2)}) %collective-permute-start.44) | collective-permute-done | bytes 262176 | tf_op jit(solution)/shard_map/ppermute | solution.py:42
  178.2 1.5 collective-permute-start.35
  179.7 1.2 collective-permute-start.41
  180.9 4.1 %collective-permute-done.38.refs_1_ = bf16[64,2048]{1,0:T(8,128)(2,1)S(1)} collective-permute-done((bf16[64,2048]{1,0:T(8,128)(2,1)S(1)}, bf16[64,2048]{1,0:T(8,128)(2,1)S(1)}, u32[]{:S(2)}, u32[]{:S(2)}) %collective-permute-start.38) | collective-permute-done | bytes 262176 | tf_op jit(solution)/shard_map/ppermute | solution.py:42
  185.0 2.8 %collective-permute-done.45.refs_3_ = bf16[64,2048]{1,0:T(8,128)(2,1)S(1)} collective-permute-done((bf16[64,2048]{1,0:T(8,128)(2,1)S(1)}, bf16[64,2048]{1,0:T(8,128)(2,1)S(1)}, u32[]{:S(2)}, u32[]{:S(2)}) %collective-permute-start.45) | collective-permute-done | bytes 262176 | tf_op jit(solution)/shard_map/ppermute | solution.py:42
  187.8 1.2 collective-permute-done.41.refs_2_
  189.0 1.1 final.1
  (98 shorter events, 20.3 us)
Async XLA Ops:
  6.5 18.6 %copy-start.10 = (bf16[2048]{0:T(1024)(128)(2,1)S(1)}, bf16[2048]{0:T(1024)(128)(2,1)}, u32[]{:S(2)}) copy-start(bf16[2048]{0:T(1024)(128)(2,1)} %param.14) | copy-start | bytes 12292
  6.5 53.0 %all-gather.2.cloned.1.call-start = ((), (), s32[]{:S(2)}) async-start(), calls=%async_computation | async-start | bytes 4718592 | tf_op jit(solution)/shard_map/all_gather | solution.py:200
  8.6 6.7 %collective-permute-start = (bf16[128,512]{1,0:T(8,128)(2,1)}, bf16[128,512]{1,0:T(8,128)(2,1)S(1)}, u32[]{:S(2)}, u32[]{:S(2)}) collective-permute-start(bf16[128,512]{1,0:T(8,128)(2,1)} %bitcast.42), channel_id=1, source_target_pairs={{0,16},{16,0},{1,17},{17,1},{2,18},{18,2},{3,19},{19,3},{4,20},{20... | collective-permute-start | bytes 393224 | tf_op jit(solution)/shard_map/ppermute | solution.py:49
  21.0 1.9 collective-permute-start.1
  22.9 14.9 %collective-permute-start.4 = (bf16[128,2048]{1,0:T(8,128)(2,1)S(1)}, bf16[128,2048]{1,0:T(8,128)(2,1)}, u32[]{:S(2)}, u32[]{:S(2)}) collective-permute-start(bf16[128,2048]{1,0:T(8,128)(2,1)S(1)} %collective-permute-done.1), channel_id=1, source_target_pairs={{0,16},{16,0},{1,17},{17,1},{2,18},{18,2},{3,19},{19,3},{4,20},{20... | collective-permute-start | bytes 1572872 | tf_op jit(solution)/shard_map/ppermute | solution.py:49
  24.7 38.2 %collective-permute-start.3 = (bf16[128,2048]{1,0:T(8,128)(2,1)}, bf16[128,2048]{1,0:T(8,128)(2,1)}, u32[]{:S(2)}, u32[]{:S(2)}) collective-permute-start(bf16[128,2048]{1,0:T(8,128)(2,1)} %get-tuple-element.199), channel_id=1, source_target_pairs={{0,16},{16,0},{1,17},{17,1},{2,18},{18,2},{3,19},{19,3},{4,20},{20... | collective-permute-start | bytes 1572872 | tf_op jit(solution)/shard_map/ppermute | solution.py:49
  62.8 3.2 %collective-permute-start.5 = (bf16[128,1024]{1,0:T(8,128)(2,1)S(1)}, bf16[128,1024]{1,0:T(8,128)(2,1)S(1)}, u32[]{:S(2)}, u32[]{:S(2)}) collective-permute-start(bf16[128,1024]{1,0:T(8,128)(2,1)S(1)} %convolution_convert_fusion), channel_id=1, source_target_pairs={{0,1},{1,0},{2,3},{3,2},{4,5},{5,4},{6,7},{7,6},{8,9},{9,8},{10,11... | collective-permute-start | bytes 786440 | tf_op jit(solution)/shard_map/ppermute | solution.py:34
  65.7 2.6 %collective-permute-start.2 = (bf16[128,1024]{1,0:T(8,128)(2,1)S(1)}, bf16[128,1024]{1,0:T(8,128)(2,1)S(1)}, u32[]{:S(2)}, u32[]{:S(2)}) collective-permute-start(bf16[128,1024]{1,0:T(8,128)(2,1)S(1)} %convolution_convert_fusion.1), channel_id=1, source_target_pairs={{0,1},{1,0},{2,3},{3,2},{4,5},{5,4},{6,7},{7,6},{8,9},{9,8},{10,11... | collective-permute-start | bytes 786440 | tf_op jit(solution)/shard_map/ppermute | solution.py:34
  66.1 8.6 %collective-permute-start.6 = (bf16[128,1024]{1,0:T(8,128)(2,1)S(1)}, bf16[128,1024]{1,0:T(8,128)(2,1)S(1)}, u32[]{:S(2)}, u32[]{:S(2)}) collective-permute-start(bf16[128,1024]{1,0:T(8,128)(2,1)S(1)} %add_convert_fusion.14), channel_id=1, source_target_pairs={{0,16},{16,0},{1,17},{17,1},{2,18},{18,2},{3,19},{19,3},{4,20},{20... | collective-permute-start | bytes 786440 | tf_op jit(solution)/shard_map/ppermute | solution.py:49
  75.2 2.2 %collective-permute-start.9 = (bf16[128,2176]{1,0:T(8,128)(2,1)S(1)}, bf16[128,2176]{1,0:T(8,128)(2,1)S(1)}, u32[]{:S(2)}, u32[]{:S(2)}) collective-permute-start(bf16[128,2176]{1,0:T(8,128)(2,1)S(1)} %get-tuple-element.96.refs_3_), channel_id=1, source_target_pairs={{0,1},{1,0},{2,3},{3,2},{4,5},{5,4},{6,7},{7,6},{8,9},{9,8},{10,11... | collective-permute-start | bytes 1671176 | tf_op jit(solution)/shard_map/ppermute | solution.py:34
  75.3 15.0 %collective-permute-start.7 = (bf16[128,2176]{1,0:T(8,128)(2,1)S(1)}, bf16[128,2176]{1,0:T(8,128)(2,1)S(1)}, u32[]{:S(2)}, u32[]{:S(2)}) collective-permute-start(bf16[128,2176]{1,0:T(8,128)(2,1)S(1)} %get-tuple-element.96.refs_3_), channel_id=1, source_target_pairs={{0,4},{4,8},{8,12},{12,14},{14,10},{10,6},{6,2},{2,0},{1,5},{5,9},... | collective-permute-start | bytes 1671176 | tf_op jit(solution)/shard_map/ppermute | solution.py:42
  76.8 14.7 %collective-permute-start.8 = (bf16[128,2176]{1,0:T(8,128)(2,1)S(1)}, bf16[128,2176]{1,0:T(8,128)(2,1)S(1)}, u32[]{:S(2)}, u32[]{:S(2)}) collective-permute-start(bf16[128,2176]{1,0:T(8,128)(2,1)S(1)} %get-tuple-element.96.refs_3_), channel_id=1, source_target_pairs={{0,2},{4,0},{8,4},{12,8},{14,12},{10,14},{6,10},{2,6},{1,3},{5,1},... | collective-permute-start | bytes 1671176 | tf_op jit(solution)/shard_map/ppermute | solution.py:42
  91.5 2.5 %collective-permute-start.12 = (bf16[128,2176]{1,0:T(8,128)(2,1)S(1)}, bf16[128,2176]{1,0:T(8,128)(2,1)S(1)}, u32[]{:S(2)}, u32[]{:S(2)}) collective-permute-start(bf16[128,2176]{1,0:T(8,128)(2,1)S(1)} %collective-permute-done.7.refs_3_), channel_id=1, source_target_pairs={{0,1},{1,0},{2,3},{3,2},{4,5},{5,4},{6,7},{7,6},{8,9},{9,8},{10,11... | collective-permute-start | bytes 1671176 | tf_op jit(solution)/shard_map/ppermute | solution.py:34
  91.5 2.8 %collective-permute-start.13 = (bf16[128,2176]{1,0:T(8,128)(2,1)S(1)}, bf16[128,2176]{1,0:T(8,128)(2,1)S(1)}, u32[]{:S(2)}, u32[]{:S(2)}) collective-permute-start(bf16[128,2176]{1,0:T(8,128)(2,1)S(1)} %collective-permute-done.8.refs_5_), channel_id=1, source_target_pairs={{0,1},{1,0},{2,3},{3,2},{4,5},{5,4},{6,7},{7,6},{8,9},{9,8},{10,11... | collective-permute-start | bytes 1671176 | tf_op jit(solution)/shard_map/ppermute | solution.py:34
  92.0 14.5 %collective-permute-start.10 = (bf16[128,2176]{1,0:T(8,128)(2,1)S(1)}, bf16[128,2176]{1,0:T(8,128)(2,1)S(1)}, u32[]{:S(2)}, u32[]{:S(2)}) collective-permute-start(bf16[128,2176]{1,0:T(8,128)(2,1)S(1)} %collective-permute-done.7.refs_3_), channel_id=1, source_target_pairs={{0,4},{4,8},{8,12},{12,14},{14,10},{10,6},{6,2},{2,0},{1,5},{5,9},... | collective-permute-start | bytes 1671176 | tf_op jit(solution)/shard_map/ppermute | solution.py:42
  93.5 14.3 %collective-permute-start.11 = (bf16[128,2176]{1,0:T(8,128)(2,1)S(1)}, bf16[128,2176]{1,0:T(8,128)(2,1)S(1)}, u32[]{:S(2)}, u32[]{:S(2)}) collective-permute-start(bf16[128,2176]{1,0:T(8,128)(2,1)S(1)} %collective-permute-done.8.refs_5_), channel_id=1, source_target_pairs={{0,2},{4,0},{8,4},{12,8},{14,12},{10,14},{6,10},{2,6},{1,3},{5,1},... | collective-permute-start | bytes 1671176 | tf_op jit(solution)/shard_map/ppermute | solution.py:42
  94.3 13.5 %collective-permute-start.14 = (bf16[128,2048]{1,0:T(8,128)(2,1)S(1)}, bf16[128,2048]{1,0:T(8,128)(2,1)S(1)}, u32[]{:S(2)}, u32[]{:S(2)}) collective-permute-start(bf16[128,2048]{1,0:T(8,128)(2,1)S(1)} %get-tuple-element.110), channel_id=1, source_target_pairs={{0,1},{1,0},{2,3},{3,2},{4,5},{5,4},{6,7},{7,6},{8,9},{9,8},{10,11... | collective-permute-start | bytes 1572872 | tf_op jit(solution)/shard_map/ppermute | solution.py:34
  107.8 2.5 %collective-permute-start.17 = (bf16[128,2176]{1,0:T(8,128)(2,1)S(1)}, bf16[128,2176]{1,0:T(8,128)(2,1)S(1)}, u32[]{:S(2)}, u32[]{:S(2)}) collective-permute-start(bf16[128,2176]{1,0:T(8,128)(2,1)S(1)} %collective-permute-done.10.refs_3_), channel_id=1, source_target_pairs={{0,1},{1,0},{2,3},{3,2},{4,5},{5,4},{6,7},{7,6},{8,9},{9,8},{10,11... | collective-permute-start | bytes 1671176 | tf_op jit(solution)/shard_map/ppermute | solution.py:34
  107.8 2.8 %collective-permute-start.18 = (bf16[128,2176]{1,0:T(8,128)(2,1)S(1)}, bf16[128,2176]{1,0:T(8,128)(2,1)S(1)}, u32[]{:S(2)}, u32[]{:S(2)}) collective-permute-start(bf16[128,2176]{1,0:T(8,128)(2,1)S(1)} %collective-permute-done.11.refs_5_), channel_id=1, source_target_pairs={{0,1},{1,0},{2,3},{3,2},{4,5},{5,4},{6,7},{7,6},{8,9},{9,8},{10,11... | collective-permute-start | bytes 1671176 | tf_op jit(solution)/shard_map/ppermute | solution.py:34
  108.3 14.5 %collective-permute-start.15 = (bf16[128,2176]{1,0:T(8,128)(2,1)S(1)}, bf16[128,2176]{1,0:T(8,128)(2,1)S(1)}, u32[]{:S(2)}, u32[]{:S(2)}) collective-permute-start(bf16[128,2176]{1,0:T(8,128)(2,1)S(1)} %collective-permute-done.10.refs_3_), channel_id=1, source_target_pairs={{0,4},{4,8},{8,12},{12,14},{14,10},{10,6},{6,2},{2,0},{1,5},{5,9},... | collective-permute-start | bytes 1671176 | tf_op jit(solution)/shard_map/ppermute | solution.py:42
  109.8 14.3 %collective-permute-start.16 = (bf16[128,2176]{1,0:T(8,128)(2,1)S(1)}, bf16[128,2176]{1,0:T(8,128)(2,1)S(1)}, u32[]{:S(2)}, u32[]{:S(2)}) collective-permute-start(bf16[128,2176]{1,0:T(8,128)(2,1)S(1)} %collective-permute-done.11.refs_5_), channel_id=1, source_target_pairs={{0,2},{4,0},{8,4},{12,8},{14,12},{10,14},{6,10},{2,6},{1,3},{5,1},... | collective-permute-start | bytes 1671176 | tf_op jit(solution)/shard_map/ppermute | solution.py:42
  110.5 13.5 %collective-permute-start.19 = (bf16[128,2048]{1,0:T(8,128)(2,1)S(1)}, bf16[128,2048]{1,0:T(8,128)(2,1)S(1)}, u32[]{:S(2)}, u32[]{:S(2)}) collective-permute-start(bf16[128,2048]{1,0:T(8,128)(2,1)S(1)} %get-tuple-element.126), channel_id=1, source_target_pairs={{0,1},{1,0},{2,3},{3,2},{4,5},{5,4},{6,7},{7,6},{8,9},{9,8},{10,11... | collective-permute-start | bytes 1572872 | tf_op jit(solution)/shard_map/ppermute | solution.py:34
  110.7 13.3 %collective-permute-start.20 = (bf16[128,2048]{1,0:T(8,128)(2,1)S(1)}, bf16[128,2048]{1,0:T(8,128)(2,1)S(1)}, u32[]{:S(2)}, u32[]{:S(2)}) collective-permute-start(bf16[128,2048]{1,0:T(8,128)(2,1)S(1)} %get-tuple-element.128), channel_id=1, source_target_pairs={{0,1},{1,0},{2,3},{3,2},{4,5},{5,4},{6,7},{7,6},{8,9},{9,8},{10,11... | collective-permute-start | bytes 1572872 | tf_op jit(solution)/shard_map/ppermute | solution.py:34
  124.0 2.0 collective-permute-start.23
  124.0 3.2 %collective-permute-start.24 = (bf16[128,2176]{1,0:T(8,128)(2,1)S(1)}, bf16[128,2176]{1,0:T(8,128)(2,1)S(1)}, u32[]{:S(2)}, u32[]{:S(2)}) collective-permute-start(bf16[128,2176]{1,0:T(8,128)(2,1)S(1)} %collective-permute-done.16.refs_5_), channel_id=1, source_target_pairs={{0,1},{1,0},{2,3},{3,2},{4,5},{5,4},{6,7},{7,6},{8,9},{9,8},{10,11... | collective-permute-start | bytes 1671176 | tf_op jit(solution)/shard_map/ppermute | solution.py:34
  124.5 10.1 %collective-permute-start.25 = (bf16[128,2048]{1,0:T(8,128)(2,1)S(1)}, bf16[128,2048]{1,0:T(8,128)(2,1)S(1)}, u32[]{:S(2)}, u32[]{:S(2)}) collective-permute-start(bf16[128,2048]{1,0:T(8,128)(2,1)S(1)} %get-tuple-element.140), channel_id=1, source_target_pairs={{0,1},{1,0},{2,3},{3,2},{4,5},{5,4},{6,7},{7,6},{8,9},{9,8},{10,11... | collective-permute-start | bytes 1572872 | tf_op jit(solution)/shard_map/ppermute | solution.py:34
  124.6 10.1 %collective-permute-start.26 = (bf16[128,2048]{1,0:T(8,128)(2,1)S(1)}, bf16[128,2048]{1,0:T(8,128)(2,1)S(1)}, u32[]{:S(2)}, u32[]{:S(2)}) collective-permute-start(bf16[128,2048]{1,0:T(8,128)(2,1)S(1)} %get-tuple-element.142), channel_id=1, source_target_pairs={{0,1},{1,0},{2,3},{3,2},{4,5},{5,4},{6,7},{7,6},{8,9},{9,8},{10,11... | collective-permute-start | bytes 1572872 | tf_op jit(solution)/shard_map/ppermute | solution.py:34
  125.1 8.7 %collective-permute-start.21 = (bf16[64,2176]{1,0:T(8,128)(2,1)S(1)}, bf16[64,2176]{1,0:T(8,128)(2,1)S(1)}, u32[]{:S(2)}, u32[]{:S(2)}) collective-permute-start(bf16[64,2176]{1,0:T(8,128)(2,1)S(1)} %slice.98), channel_id=1, source_target_pairs={{0,4},{4,8},{8,12},{12,14},{14,10},{10,6},{6,2},{2,0},{1,5},{5,9},... | collective-permute-start | bytes 835592 | tf_op jit(solution)/shard_map/ppermute | solution.py:42
  126.0 8.7 %collective-permute-start.22 = (bf16[64,2176]{1,0:T(8,128)(2,1)S(1)}, bf16[64,2176]{1,0:T(8,128)(2,1)S(1)}, u32[]{:S(2)}, u32[]{:S(2)}) collective-permute-start(bf16[64,2176]{1,0:T(8,128)(2,1)S(1)} %slice.99), channel_id=1, source_target_pairs={{0,2},{4,0},{8,4},{12,8},{14,12},{10,14},{6,10},{2,6},{1,3},{5,1},... | collective-permute-start | bytes 835592 | tf_op jit(solution)/shard_map/ppermute | solution.py:42
  134.7 1.6 collective-permute-start.27
  134.7 1.9 collective-permute-start.28
  136.6 3.1 %collective-permute-start.29 = (bf16[128,2048]{1,0:T(8,128)(2,1)S(1)}, bf16[128,2048]{1,0:T(8,128)(2,1)S(1)}, u32[]{:S(2)}, u32[]{:S(2)}) collective-permute-start(bf16[128,2048]{1,0:T(8,128)(2,1)S(1)} %get-tuple-element.162), channel_id=1, source_target_pairs={{0,1},{1,0},{2,3},{3,2},{4,5},{5,4},{6,7},{7,6},{8,9},{9,8},{10,11... | collective-permute-start | bytes 1572872 | tf_op jit(solution)/shard_map/ppermute | solution.py:34
  136.8 3.0 %collective-permute-start.30 = (bf16[128,2048]{1,0:T(8,128)(2,1)S(1)}, bf16[128,2048]{1,0:T(8,128)(2,1)S(1)}, u32[]{:S(2)}, u32[]{:S(2)}) collective-permute-start(bf16[128,2048]{1,0:T(8,128)(2,1)S(1)} %get-tuple-element.164), channel_id=1, source_target_pairs={{0,1},{1,0},{2,3},{3,2},{4,5},{5,4},{6,7},{7,6},{8,9},{9,8},{10,11... | collective-permute-start | bytes 1572872 | tf_op jit(solution)/shard_map/ppermute | solution.py:34
  139.8 2.0 %collective-permute-start.31 = (bf16[128,2048]{1,0:T(8,128)(2,1)S(1)}, bf16[128,2048]{1,0:T(8,128)(2,1)S(1)}, u32[]{:S(2)}, u32[]{:S(2)}) collective-permute-start(bf16[128,2048]{1,0:T(8,128)(2,1)S(1)} %get-tuple-element.178), channel_id=1, source_target_pairs={{0,1},{1,0},{2,3},{3,2},{4,5},{5,4},{6,7},{7,6},{8,9},{9,8},{10,11... | collective-permute-start | bytes 1572872 | tf_op jit(solution)/shard_map/ppermute | solution.py:34
  141.9 8.4 %collective-permute-start.42 = (bf16[64,2048]{1,0:T(8,128)(2,1)S(1)}, bf16[64,2048]{1,0:T(8,128)(2,1)S(1)}, u32[]{:S(2)}, u32[]{:S(2)}) collective-permute-start(bf16[64,2048]{1,0:T(8,128)(2,1)S(1)} %get-tuple-element.191), channel_id=1, source_target_pairs={{0,2},{4,0},{8,4},{12,8},{14,12},{10,14},{6,10},{2,6},{1,3},{5,1},... | collective-permute-start | bytes 786440 | tf_op jit(solution)/shard_map/ppermute | solution.py:42
  142.8 9.1 %collective-permute-start.32 = (bf16[64,2048]{1,0:T(8,128)(2,1)S(1)}, bf16[64,2048]{1,0:T(8,128)(2,1)S(1)}, u32[]{:S(2)}, u32[]{:S(2)}) collective-permute-start(bf16[64,2048]{1,0:T(8,128)(2,1)S(1)} %get-tuple-element.192), channel_id=1, source_target_pairs={{0,4},{4,8},{8,12},{12,14},{14,10},{10,6},{6,2},{2,0},{1,5},{5,9},... | collective-permute-start | bytes 786440 | tf_op jit(solution)/shard_map/ppermute | solution.py:42
  150.5 9.3 %collective-permute-start.36 = (bf16[64,2048]{1,0:T(8,128)(2,1)S(1)}, bf16[64,2048]{1,0:T(8,128)(2,1)S(1)}, u32[]{:S(2)}, u32[]{:S(2)}) collective-permute-start(bf16[64,2048]{1,0:T(8,128)(2,1)S(1)} %get-tuple-element.190), channel_id=1, source_target_pairs={{0,2},{4,0},{8,4},{12,8},{14,12},{10,14},{6,10},{2,6},{1,3},{5,1},... | collective-permute-start | bytes 786440 | tf_op jit(solution)/shard_map/ppermute | solution.py:42
  151.4 12.3 %collective-permute-start.43 = (bf16[64,2048]{1,0:T(8,128)(2,1)S(1)}, bf16[64,2048]{1,0:T(8,128)(2,1)S(1)}, u32[]{:S(2)}, u32[]{:S(2)}) collective-permute-start(bf16[64,2048]{1,0:T(8,128)(2,1)S(1)} %get-tuple-element.189), channel_id=1, source_target_pairs={{0,2},{4,0},{8,4},{12,8},{14,12},{10,14},{6,10},{2,6},{1,3},{5,1},... | collective-permute-start | bytes 786440 | tf_op jit(solution)/shard_map/ppermute | solution.py:42
  152.2 13.2 %collective-permute-start.33 = (bf16[64,2048]{1,0:T(8,128)(2,1)S(1)}, bf16[64,2048]{1,0:T(8,128)(2,1)S(1)}, u32[]{:S(2)}, u32[]{:S(2)}) collective-permute-start(bf16[64,2048]{1,0:T(8,128)(2,1)S(1)} %get-tuple-element.198), channel_id=1, source_target_pairs={{0,4},{4,8},{8,12},{12,14},{14,10},{10,6},{6,2},{2,0},{1,5},{5,9},... | collective-permute-start | bytes 786440 | tf_op jit(solution)/shard_map/ppermute | solution.py:42
  153.7 11.7 %collective-permute-start.39 = (bf16[64,2048]{1,0:T(8,128)(2,1)S(1)}, bf16[64,2048]{1,0:T(8,128)(2,1)S(1)}, u32[]{:S(2)}, u32[]{:S(2)}) collective-permute-start(bf16[64,2048]{1,0:T(8,128)(2,1)S(1)} %get-tuple-element.197), channel_id=1, source_target_pairs={{0,4},{4,8},{8,12},{12,14},{14,10},{10,6},{6,2},{2,0},{1,5},{5,9},... | collective-permute-start | bytes 786440 | tf_op jit(solution)/shard_map/ppermute | solution.py:42
  163.9 9.3 %collective-permute-start.37 = (bf16[64,2048]{1,0:T(8,128)(2,1)S(1)}, bf16[64,2048]{1,0:T(8,128)(2,1)S(1)}, u32[]{:S(2)}, u32[]{:S(2)}) collective-permute-start(bf16[64,2048]{1,0:T(8,128)(2,1)S(1)} %get-tuple-element.188), channel_id=1, source_target_pairs={{0,2},{4,0},{8,4},{12,8},{14,12},{10,14},{6,10},{2,6},{1,3},{5,1},... | collective-permute-start | bytes 786440 | tf_op jit(solution)/shard_map/ppermute | solution.py:42
  164.8 11.4 %collective-permute-start.44 = (bf16[64,2048]{1,0:T(8,128)(2,1)S(1)}, bf16[64,2048]{1,0:T(8,128)(2,1)S(1)}, u32[]{:S(2)}, u32[]{:S(2)}) collective-permute-start(bf16[64,2048]{1,0:T(8,128)(2,1)S(1)} %get-tuple-element.187), channel_id=1, source_target_pairs={{0,2},{4,0},{8,4},{12,8},{14,12},{10,14},{6,10},{2,6},{1,3},{5,1},... | collective-permute-start | bytes 786440 | tf_op jit(solution)/shard_map/ppermute | solution.py:42
  165.7 12.3 %collective-permute-start.34 = (bf16[64,2048]{1,0:T(8,128)(2,1)S(1)}, bf16[64,2048]{1,0:T(8,128)(2,1)S(1)}, u32[]{:S(2)}, u32[]{:S(2)}) collective-permute-start(bf16[64,2048]{1,0:T(8,128)(2,1)S(1)} %get-tuple-element.196), channel_id=1, source_target_pairs={{0,4},{4,8},{8,12},{12,14},{14,10},{10,6},{6,2},{2,0},{1,5},{5,9},... | collective-permute-start | bytes 786440 | tf_op jit(solution)/shard_map/ppermute | solution.py:42
  167.2 10.7 %collective-permute-start.40 = (bf16[64,2048]{1,0:T(8,128)(2,1)S(1)}, bf16[64,2048]{1,0:T(8,128)(2,1)S(1)}, u32[]{:S(2)}, u32[]{:S(2)}) collective-permute-start(bf16[64,2048]{1,0:T(8,128)(2,1)S(1)} %get-tuple-element.195), channel_id=1, source_target_pairs={{0,4},{4,8},{8,12},{12,14},{14,10},{10,6},{6,2},{2,0},{1,5},{5,9},... | collective-permute-start | bytes 786440 | tf_op jit(solution)/shard_map/ppermute | solution.py:42
  176.4 8.5 %collective-permute-start.38 = (bf16[64,2048]{1,0:T(8,128)(2,1)S(1)}, bf16[64,2048]{1,0:T(8,128)(2,1)S(1)}, u32[]{:S(2)}, u32[]{:S(2)}) collective-permute-start(bf16[64,2048]{1,0:T(8,128)(2,1)S(1)} %get-tuple-element.186), channel_id=1, source_target_pairs={{0,2},{4,0},{8,4},{12,8},{14,12},{10,14},{6,10},{2,6},{1,3},{5,1},... | collective-permute-start | bytes 786440 | tf_op jit(solution)/shard_map/ppermute | solution.py:42
  177.4 10.4 %collective-permute-start.45 = (bf16[64,2048]{1,0:T(8,128)(2,1)S(1)}, bf16[64,2048]{1,0:T(8,128)(2,1)S(1)}, u32[]{:S(2)}, u32[]{:S(2)}) collective-permute-start(bf16[64,2048]{1,0:T(8,128)(2,1)S(1)} %get-tuple-element.185), channel_id=1, source_target_pairs={{0,2},{4,0},{8,4},{12,8},{14,12},{10,14},{6,10},{2,6},{1,3},{5,1},... | collective-permute-start | bytes 786440 | tf_op jit(solution)/shard_map/ppermute | solution.py:42
  178.2 9.6 %collective-permute-start.35 = (bf16[64,2048]{1,0:T(8,128)(2,1)S(1)}, bf16[64,2048]{1,0:T(8,128)(2,1)S(1)}, u32[]{:S(2)}, u32[]{:S(2)}) collective-permute-start(bf16[64,2048]{1,0:T(8,128)(2,1)S(1)} %get-tuple-element.194), channel_id=1, source_target_pairs={{0,4},{4,8},{8,12},{12,14},{14,10},{10,6},{6,2},{2,0},{1,5},{5,9},... | collective-permute-start | bytes 786440 | tf_op jit(solution)/shard_map/ppermute | solution.py:42
  179.7 9.3 %collective-permute-start.41 = (bf16[64,2048]{1,0:T(8,128)(2,1)S(1)}, bf16[64,2048]{1,0:T(8,128)(2,1)S(1)}, u32[]{:S(2)}, u32[]{:S(2)}) collective-permute-start(bf16[64,2048]{1,0:T(8,128)(2,1)S(1)} %get-tuple-element.193), channel_id=1, source_target_pairs={{0,4},{4,8},{8,12},{12,14},{14,10},{10,6},{6,2},{2,0},{1,5},{5,9},... | collective-permute-start | bytes 786440 | tf_op jit(solution)/shard_map/ppermute | solution.py:42
  (10 other events, 88.0 us)
Sparse Core Ops, SparseCore 0:
  8.9 50.5 all-gather.1

commit v5 on v4

--- a/solution.py
+++ b/solution.py
@@ -84,6 +84,10 @@
             out_ref[slot, :, at : at + HD] = (mixed / row_sum).astype(jnp.bfloat16)
 
 
+def columns_kernel(pos_ref, source_ref, target_ref):
+    target_ref[...] = source_ref[...]
+
+
 def norm_kernel(experts_all, pos_ref, hidden_ref, *refs):
     *projected_refs, gain_ref, ids_ref, gates_ref, residual_ref, tokens_ref = refs
     n_ctx = len(projected_refs)
@@ -167,6 +171,23 @@
     )(jnp.stack([position, core]), queries, *blocks)
 
 
+def own_columns(position, matrix, n_parts):
+    rows, width = matrix.shape
+    wide, step = width // n_parts, rows // 4
+    return pl.pallas_call(
+        columns_kernel,
+        grid_spec=pltpu.PrefetchScalarGridSpec(
+            num_scalar_prefetch=1,
+            grid=(4,),
+            in_specs=[pl.BlockSpec((step, wide), lambda i, pos: (i, pos[0]))],
+            out_specs=pl.BlockSpec((step, wide), lambda i, pos: (i, 0)),
+        ),
+        out_shape=jax.ShapeDtypeStruct((rows, wide), matrix.dtype),
+        compiler_params=pltpu.CompilerParams(vmem_limit_bytes=60 * 1024 * 1024),
+        name="columns",
+    )(position.reshape(1), matrix)
+
+
 def run_expert(experts_all, expert, chips, weights):
     groups, parts = len(chips), len(chips[0][0])
     blocks = [block for own, other in chips for block in own + other]
@@ -196,9 +217,8 @@
     position = lax.axis_index("ctx")
     rows = hidden_in.shape[1]
     proj_rows = out_proj.shape[0]
-    wide = D // n_ctx
     columns = lax.all_gather(
-        lax.dynamic_slice_in_dim(out_proj, position * wide, wide, axis=1),
+        own_columns(position, out_proj, n_ctx),
         "exp",
         axis=0,
         tiled=True,
@@ -214,15 +234,13 @@
     own_heads, other_heads = attended[0], attended[1]
     sibling_heads = swap_cores(other_heads)
     projected = []
-    for back in list(range(1, n_ctx)) + [0]:
+    for back in range(n_ctx):
         heads = [rotate(own_heads, "ctx", back), rotate(sibling_heads, "ctx", back)]
         from_sibling = swap_cores(times_columns(heads[1]).astype(jnp.bfloat16))
-        part = lax.optimization_barrier(times_columns(heads[0]))
-        part = part + from_sibling.astype(jnp.float32)
+        part = times_columns(heads[0]) + from_sibling.astype(jnp.float32)
         if back:
             part = rotate(part.astype(jnp.bfloat16), "ctx", -back)
         projected.append(part)
-    projected = projected[-1:] + projected[:-1]
 
     local_experts = w_gate.shape[0]
     experts_all = n_exp * local_experts

time: 197 us -> 197 us (level)
  Pallas kernels: 24.7 us -> 27.9 us
  local copies, waits for them, and re-layouts: 5.64 us -> 2.78 us
    pallas_call x0 -> x1, Pallas kernels: none -> 3.19 us  [own_columns(): pl.pallas_call(columns_kernel, grid_spec=pltpu.PrefetchScalarGridSpec(num...]
  transfers between devices with their start and end apart: 47 -> 47, of which waited for: 27 -> 28; matrix products, arithmetic and copies ran while one was open for 5% -> 4% of each run, Pallas kernels for 12% -> 12%
where the time goes in v5:
time: 197 us
  waiting for transfers between devices  112 us (57%)
  starting transfers between devices  33.6 us (17%)
  Pallas kernels  27.9 us (14%)
  between operations  13.7 us (7%)
  matrix products  5.28 us (3%)
  local copies, waits for them, and re-layouts  2.78 us (1%)
    ppermute x22, waiting for transfers between devices, round_ring(): return lax.ppermute(block, 'exp', route)  61.2 us
    ppermute x22, starting transfers between devices, round_ring(): return lax.ppermute(block, 'exp', route)  22.5 us
    all_gather x1, waiting for transfers between devices, body(): lax.all_gather(own_columns(position, out_proj, n_ctx), 'exp', axis=0, til...  22.4 us
    ppermute x4, waiting for transfers between devices, rotate(): lax.ppermute(block, axis, [(i, (i + distance) % n) for i in range(n)])  22.2 us
    pallas_call x5, Pallas kernels, run_expert(): pl.pallas_call(functools.partial(expert_kernel, experts_all, groups, part...  20.4 us
    ppermute x4, starting transfers between devices, rotate(): lax.ppermute(block, axis, [(i, (i + distance) % n) for i in range(n)])  6.66 us
    ppermute x20, waiting for transfers between devices, swap_cores(): return lax.ppermute(block, 'exp', [(i, i ^ 1) for i in range(n)])  6.01 us
    dot_general x4, matrix products, times_columns(): return jnp.dot(block, columns, preferred_element_type=jnp.float32)  5.28 us
  transfers between devices with their start and end apart: 47, of which 28 were waited for; matrix products, arithmetic and copies ran while one was open for 4% of the time, Pallas kernels for 12%

profile of v5, /device:TPU:0, one launch (start us, length us, event | category | flops | bytes accessed | tf_op | source)
XLA Modules:
  0.0 196.6 jit_solution(1449478409074640880)
XLA Ops:
  6.5 3.2 %columns.1 = bf16[256,1024]{1,0:T(8,128)(2,1)} custom-call(s32[1]{0:T(128)} %bitcast.pos_ref, bf16[256,2048]{1,0:T(8,128)(2,1)} %source_ref.1), custom_call_target="tpu_custom_call" | custom-call | tf_op jit(solution)/shard_map/columns/pallas_call | solution.py:177
  9.8 3.0 %collective-permute-start = (bf16[128,512]{1,0:T(8,128)(2,1)}, bf16[128,512]{1,0:T(8,128)(2,1)S(1)}, u32[]{:S(2)}, u32[]{:S(2)}) collective-permute-start(bf16[128,512]{1,0:T(8,128)(2,1)} %bitcast.42), channel_id=1, source_target_pairs={{0,16},{16,0},{1,17},{17,1},{2,18},{18,2},{3,19},{19,3},{4,20},{20... | collective-permute-start | bytes 393224 | tf_op jit(solution)/shard_map/ppermute | solution.py:49
  12.9 3.6 %collective-permute-done.refs_1_ = bf16[128,512]{1,0:T(8,128)(2,1)S(1)} collective-permute-done((bf16[128,512]{1,0:T(8,128)(2,1)}, bf16[128,512]{1,0:T(8,128)(2,1)S(1)}, u32[]{:S(2)}, u32[]{:S(2)}) %collective-permute-start) | collective-permute-done | bytes 131104 | tf_op jit(solution)/shard_map/ppermute | solution.py:49
  16.5 1.2 copy-done.3
  17.7 0.9 copy-done.5
  18.6 2.6 %attention.1 = bf16[2,128,2048]{2,1,0:T(8,128)(2,1)S(1)} custom-call(s32[2]{0:T(128)S(1)} %pad_add_fusion.pos_ref, bf16[128,4096]{1,0:T(8,128)(2,1)S(1)} %bitcast.38, bf16[128,512]{1,0:T(8,128)(2,1)S(1)} %bitcast.43, bf16[128,512]{1,0:T(8,128)(2,1)S(1)} %collective-permute-done.refs_1_), custom_call_target="tpu_custom_call" | custom-call | tf_op jit(solution)/shard_map/attention/pallas_call | solution.py:164
  21.4 1.9 collective-permute-done.1
  23.3 1.7 collective-permute-start.4
  25.7 12.4 %collective-permute-done.4 = bf16[128,2048]{1,0:T(8,128)(2,1)S(1)} collective-permute-done((bf16[128,2048]{1,0:T(8,128)(2,1)S(1)}, bf16[128,2048]{1,0:T(8,128)(2,1)S(1)}, u32[]{:S(2)}, u32[]{:S(2)}) %collective-permute-start.4) | collective-permute-done | bytes 524320 | tf_op jit(solution)/shard_map/ppermute | solution.py:49
  38.1 22.4 %all-gather.2.cloned.1.call-done = bf16[2048,1024]{1,0:T(8,128)(2,1)} async-done(((bf16[256,1024]{1,0:T(8,128)(2,1)}), bf16[2048,1024]{1,0:T(8,128)(2,1)}) %all-gather.2.cloned.1.call-update) | async-done | bytes 4194320 | tf_op jit(solution)/shard_map/all_gather | solution.py:220
  60.5 3.1 %convolution_convert_fusion = bf16[128,1024]{1,0:T(8,128)(2,1)S(1)} fusion(bf16[128,2048]{1,0:T(8,128)(2,1)S(1)} %collective-permute-done.4, bf16[2048,1024]{1,0:T(8,128)(2,1)} %all-gather.2.cloned.1.call-done), kind=kOutput, calls=%fused_computation.3 | convolution fusion | flops 537001984 | bytes 4980736 | tf_op jit(solution)/shard_map/dot_general | solution.py:229
  66.0 1.5 collective-permute-start.6
  68.3 6.1 %collective-permute-done.6.refs_1_ = bf16[128,1024]{1,0:T(8,128)(2,1)S(1)} collective-permute-done((bf16[128,1024]{1,0:T(8,128)(2,1)S(1)}, bf16[128,1024]{1,0:T(8,128)(2,1)S(1)}, u32[]{:S(2)}, u32[]{:S(2)}) %collective-permute-start.6) | collective-permute-done | bytes 262176 | tf_op jit(solution)/shard_map/ppermute | solution.py:49
  75.0 1.5 collective-permute-start.7
  77.1 2.6 %experts.5 = (bf16[128,2048]{1,0:T(8,128)(2,1)S(1)}, bf16[128,2048]{1,0:T(8,128)(2,1)S(1)}) custom-call(s32[1]{0:T(128)} %bitcast.9.expert_ref, bf16[2048,768]{1,0:T(8,128)(2,1)S(1)} %bitcast.23, bf16[2048,768]{1,0:T(8,128)(2,1)S(1)} %bitcast.28, bf16[768,2048]{1,0:T(8,128)(2,1)S(1)} %bitcast.33, bf16[128,2176]{1,0:T(8,128)(2,1)S(1)} %get-tuple-element.96.refs_3_, ...), custom_call_target="tpu_custom_call" | custom-call | flops 2415919104 | bytes 11534336 | tf_op jit(solution)/shard_map/experts/pallas_call | solution.py:196
  79.8 10.3 %collective-permute-done.7.refs_3_ = bf16[128,2176]{1,0:T(8,128)(2,1)S(1)} collective-permute-done((bf16[128,2176]{1,0:T(8,128)(2,1)S(1)}, bf16[128,2176]{1,0:T(8,128)(2,1)S(1)}, u32[]{:S(2)}, u32[]{:S(2)}) %collective-permute-start.7) | collective-permute-done | bytes 557088 | tf_op jit(solution)/shard_map/ppermute | solution.py:42
  90.1 1.2 collective-permute-done.8.refs_5_
  91.8 1.5 collective-permute-start.10
  94.1 5.1 %experts.6 = (bf16[128,2048]{1,0:T(8,128)(2,1)S(1)}, bf16[128,2048]{1,0:T(8,128)(2,1)S(1)}, bf16[128,2048]{1,0:T(8,128)(2,1)S(1)}, bf16[128,2048]{1,0:T(8,128)(2,1)S(1)}) custom-call(s32[1]{0:T(128)} %bitcast.9.expert_ref, bf16[2048,768]{1,0:T(8,128)(2,1)S(1)} %bitcast.24, bf16[2048,768]{1,0:T(8,128)(2,1)S(1)} %bitcast.29, bf16[768,2048]{1,0:T(8,128)(2,1)S(1)} %bitcast.34, ...), custom_call_target="tpu_custom_call" | custom-call | flops 4831838208 | bytes 13631488 | tf_op jit(solution)/shard_map/experts/pallas_call | solution.py:196
  99.2 7.1 %collective-permute-done.10.refs_3_ = bf16[128,2176]{1,0:T(8,128)(2,1)S(1)} collective-permute-done((bf16[128,2176]{1,0:T(8,128)(2,1)S(1)}, bf16[128,2176]{1,0:T(8,128)(2,1)S(1)}, u32[]{:S(2)}, u32[]{:S(2)}) %collective-permute-start.10) | collective-permute-done | bytes 557088 | tf_op jit(solution)/shard_map/ppermute | solution.py:42
  106.3 1.2 collective-permute-done.11.refs_5_
  108.0 1.5 collective-permute-start.15
  110.8 5.1 %experts.7 = (bf16[128,2048]{1,0:T(8,128)(2,1)S(1)}, bf16[128,2048]{1,0:T(8,128)(2,1)S(1)}, bf16[128,2048]{1,0:T(8,128)(2,1)S(1)}, bf16[128,2048]{1,0:T(8,128)(2,1)S(1)}) custom-call(s32[1]{0:T(128)} %bitcast.9.expert_ref, bf16[2048,768]{1,0:T(8,128)(2,1)S(1)} %bitcast.25, bf16[2048,768]{1,0:T(8,128)(2,1)S(1)} %bitcast.30, bf16[768,2048]{1,0:T(8,128)(2,1)S(1)} %bitcast.35, ...), custom_call_target="tpu_custom_call" | custom-call | flops 4831838208 | bytes 13631488 | tf_op jit(solution)/shard_map/experts/pallas_call | solution.py:196
  115.8 6.7 %collective-permute-done.15.refs_3_ = bf16[128,2176]{1,0:T(8,128)(2,1)S(1)} collective-permute-done((bf16[128,2176]{1,0:T(8,128)(2,1)S(1)}, bf16[128,2176]{1,0:T(8,128)(2,1)S(1)}, u32[]{:S(2)}, u32[]{:S(2)}) %collective-permute-start.15) | collective-permute-done | bytes 557088 | tf_op jit(solution)/shard_map/ppermute | solution.py:42
  122.6 1.2 collective-permute-done.16.refs_5_
  125.7 1.2 collective-permute-start.22
  126.9 5.1 %experts.8 = (bf16[128,2048]{1,0:T(8,128)(2,1)S(1)}, bf16[128,2048]{1,0:T(8,128)(2,1)S(1)}, bf16[128,2048]{1,0:T(8,128)(2,1)S(1)}, bf16[128,2048]{1,0:T(8,128)(2,1)S(1)}) custom-call(s32[1]{0:T(128)} %bitcast.9.expert_ref, bf16[2048,768]{1,0:T(8,128)(2,1)S(1)} %bitcast.26, bf16[2048,768]{1,0:T(8,128)(2,1)S(1)} %bitcast.31, bf16[768,2048]{1,0:T(8,128)(2,1)S(1)} %bitcast.36, ...), custom_call_target="tpu_custom_call" | custom-call | flops 4831838208 | bytes 13631488 | tf_op jit(solution)/shard_map/experts/pallas_call | solution.py:196
  132.0 1.5 collective-permute-done.21.refs_3_
  134.9 1.0 collective-permute-done.27.refs_5_
  136.9 2.6 %experts.9 = (bf16[128,2048]{1,0:T(8,128)(2,1)S(1)}, bf16[128,2048]{1,0:T(8,128)(2,1)S(1)}) custom-call(s32[1]{0:T(128)} %bitcast.9.expert_ref, bf16[2048,768]{1,0:T(8,128)(2,1)S(1)} %bitcast.27, bf16[2048,768]{1,0:T(8,128)(2,1)S(1)} %bitcast.32, bf16[768,2048]{1,0:T(8,128)(2,1)S(1)} %bitcast.37, bf16[64,2176]{1,0:T(8,128)(2,1)S(1)} %collective-permute-done.21.refs_3_, ...), custom_call_target="tpu_custom_call" | custom-call | flops 2415919104 | bytes 11534336 | tf_op jit(solution)/shard_map/experts/pallas_call | solution.py:196
  139.7 1.8 collective-permute-done.31
  141.7 0.9 collective-permute-start.42
  142.6 1.2 collective-permute-start.32
  143.7 6.3 %collective-permute-done.42 = bf16[64,2048]{1,0:T(8,128)(2,1)S(1)} collective-permute-done((bf16[64,2048]{1,0:T(8,128)(2,1)S(1)}, bf16[64,2048]{1,0:T(8,128)(2,1)S(1)}, u32[]{:S(2)}, u32[]{:S(2)}) %collective-permute-start.42) | collective-permute-done | bytes 262176 | tf_op jit(solution)/shard_map/ppermute | solution.py:42
  151.9 1.5 collective-permute-start.33
  153.4 1.2 collective-permute-start.39
  154.6 4.9 %collective-permute-done.36 = bf16[64,2048]{1,0:T(8,128)(2,1)S(1)} collective-permute-done((bf16[64,2048]{1,0:T(8,128)(2,1)S(1)}, bf16[64,2048]{1,0:T(8,128)(2,1)S(1)}, u32[]{:S(2)}, u32[]{:S(2)}) %collective-permute-start.36) | collective-permute-done | bytes 262176 | tf_op jit(solution)/shard_map/ppermute | solution.py:42
  159.5 3.9 %collective-permute-done.43 = bf16[64,2048]{1,0:T(8,128)(2,1)S(1)} collective-permute-done((bf16[64,2048]{1,0:T(8,128)(2,1)S(1)}, bf16[64,2048]{1,0:T(8,128)(2,1)S(1)}, u32[]{:S(2)}, u32[]{:S(2)}) %collective-permute-start.43) | collective-permute-done | bytes 262176 | tf_op jit(solution)/shard_map/ppermute | solution.py:42
  165.4 1.5 collective-permute-start.34
  166.9 1.2 collective-permute-start.40
  168.1 4.9 %collective-permute-done.37 = bf16[64,2048]{1,0:T(8,128)(2,1)S(1)} collective-permute-done((bf16[64,2048]{1,0:T(8,128)(2,1)S(1)}, bf16[64,2048]{1,0:T(8,128)(2,1)S(1)}, u32[]{:S(2)}, u32[]{:S(2)}) %collective-permute-start.37) | collective-permute-done | bytes 262176 | tf_op jit(solution)/shard_map/ppermute | solution.py:42
  173.0 3.0 %collective-permute-done.44 = bf16[64,2048]{1,0:T(8,128)(2,1)S(1)} collective-permute-done((bf16[64,2048]{1,0:T(8,128)(2,1)S(1)}, bf16[64,2048]{1,0:T(8,128)(2,1)S(1)}, u32[]{:S(2)}, u32[]{:S(2)}) %collective-permute-start.44) | collective-permute-done | bytes 262176 | tf_op jit(solution)/shard_map/ppermute | solution.py:42
  177.9 1.5 collective-permute-start.35
  179.4 1.2 collective-permute-start.41
  180.6 4.1 %collective-permute-done.38.refs_1_ = bf16[64,2048]{1,0:T(8,128)(2,1)S(1)} collective-permute-done((bf16[64,2048]{1,0:T(8,128)(2,1)S(1)}, bf16[64,2048]{1,0:T(8,128)(2,1)S(1)}, u32[]{:S(2)}, u32[]{:S(2)}) %collective-permute-start.38) | collective-permute-done | bytes 262176 | tf_op jit(solution)/shard_map/ppermute | solution.py:42
  184.7 2.8 %collective-permute-done.45.refs_3_ = bf16[64,2048]{1,0:T(8,128)(2,1)S(1)} collective-permute-done((bf16[64,2048]{1,0:T(8,128)(2,1)S(1)}, bf16[64,2048]{1,0:T(8,128)(2,1)S(1)}, u32[]{:S(2)}, u32[]{:S(2)}) %collective-permute-start.45) | collective-permute-done | bytes 262176 | tf_op jit(solution)/shard_map/ppermute | solution.py:42
  187.5 1.2 collective-permute-done.41.refs_2_
  188.7 1.1 final.1
  (94 shorter events, 18.6 us)
Async XLA Ops:
  6.5 18.7 %copy-start.9 = (bf16[2048]{0:T(1024)(128)(2,1)S(1)}, bf16[2048]{0:T(1024)(128)(2,1)}, u32[]{:S(2)}) copy-start(bf16[2048]{0:T(1024)(128)(2,1)} %param.14) | copy-start | bytes 12292
  6.5 54.0 %all-gather.2.cloned.1.call-start = ((), (), s32[]{:S(2)}) async-start(), calls=%async_computation | async-start | bytes 4718592 | tf_op jit(solution)/shard_map/all_gather | solution.py:220
  9.8 6.7 %collective-permute-start = (bf16[128,512]{1,0:T(8,128)(2,1)}, bf16[128,512]{1,0:T(8,128)(2,1)S(1)}, u32[]{:S(2)}, u32[]{:S(2)}) collective-permute-start(bf16[128,512]{1,0:T(8,128)(2,1)} %bitcast.42), channel_id=1, source_target_pairs={{0,16},{16,0},{1,17},{17,1},{2,18},{18,2},{3,19},{19,3},{4,20},{20... | collective-permute-start | bytes 393224 | tf_op jit(solution)/shard_map/ppermute | solution.py:49
  21.4 2.0 %collective-permute-start.1 = (bf16[128,2048]{1,0:T(8,128)(2,1)S(1)}, bf16[128,2048]{1,0:T(8,128)(2,1)S(1)}, u32[]{:S(2)}, u32[]{:S(2)}) collective-permute-start(bf16[128,2048]{1,0:T(8,128)(2,1)S(1)} %get-tuple-element.200), channel_id=1, source_target_pairs={{0,1},{1,0},{2,3},{3,2},{4,5},{5,4},{6,7},{7,6},{8,9},{9,8},{10,11... | collective-permute-start | bytes 1572872 | tf_op jit(solution)/shard_map/ppermute | solution.py:34
  23.3 14.8 %collective-permute-start.4 = (bf16[128,2048]{1,0:T(8,128)(2,1)S(1)}, bf16[128,2048]{1,0:T(8,128)(2,1)S(1)}, u32[]{:S(2)}, u32[]{:S(2)}) collective-permute-start(bf16[128,2048]{1,0:T(8,128)(2,1)S(1)} %collective-permute-done.1), channel_id=1, source_target_pairs={{0,16},{16,0},{1,17},{17,1},{2,18},{18,2},{3,19},{19,3},{4,20},{20... | collective-permute-start | bytes 1572872 | tf_op jit(solution)/shard_map/ppermute | solution.py:49
  25.3 39.7 %collective-permute-start.3 = (bf16[128,2048]{1,0:T(8,128)(2,1)S(1)}, bf16[128,2048]{1,0:T(8,128)(2,1)S(1)}, u32[]{:S(2)}, u32[]{:S(2)}) collective-permute-start(bf16[128,2048]{1,0:T(8,128)(2,1)S(1)} %get-tuple-element.199), channel_id=1, source_target_pairs={{0,16},{16,0},{1,17},{17,1},{2,18},{18,2},{3,19},{19,3},{4,20},{20... | collective-permute-start | bytes 1572872 | tf_op jit(solution)/shard_map/ppermute | solution.py:49
  63.6 1.6 collective-permute-start.5
  64.7 2.8 %collective-permute-start.2 = (bf16[128,1024]{1,0:T(8,128)(2,1)S(1)}, bf16[128,1024]{1,0:T(8,128)(2,1)S(1)}, u32[]{:S(2)}, u32[]{:S(2)}) collective-permute-start(bf16[128,1024]{1,0:T(8,128)(2,1)S(1)} %convolution_convert_fusion.1), channel_id=1, source_target_pairs={{0,1},{1,0},{2,3},{3,2},{4,5},{5,4},{6,7},{7,6},{8,9},{9,8},{10,11... | collective-permute-start | bytes 786440 | tf_op jit(solution)/shard_map/ppermute | solution.py:34
  66.0 8.4 %collective-permute-start.6 = (bf16[128,1024]{1,0:T(8,128)(2,1)S(1)}, bf16[128,1024]{1,0:T(8,128)(2,1)S(1)}, u32[]{:S(2)}, u32[]{:S(2)}) collective-permute-start(bf16[128,1024]{1,0:T(8,128)(2,1)S(1)} %fusion), channel_id=1, source_target_pairs={{0,16},{16,0},{1,17},{17,1},{2,18},{18,2},{3,19},{19,3},{4,20},{20... | collective-permute-start | bytes 786440 | tf_op jit(solution)/shard_map/ppermute | solution.py:49
  75.0 2.2 %collective-permute-start.9 = (bf16[128,2176]{1,0:T(8,128)(2,1)S(1)}, bf16[128,2176]{1,0:T(8,128)(2,1)S(1)}, u32[]{:S(2)}, u32[]{:S(2)}) collective-permute-start(bf16[128,2176]{1,0:T(8,128)(2,1)S(1)} %get-tuple-element.96.refs_3_), channel_id=1, source_target_pairs={{0,1},{1,0},{2,3},{3,2},{4,5},{5,4},{6,7},{7,6},{8,9},{9,8},{10,11... | collective-permute-start | bytes 1671176 | tf_op jit(solution)/shard_map/ppermute | solution.py:34
  75.0 15.0 %collective-permute-start.7 = (bf16[128,2176]{1,0:T(8,128)(2,1)S(1)}, bf16[128,2176]{1,0:T(8,128)(2,1)S(1)}, u32[]{:S(2)}, u32[]{:S(2)}) collective-permute-start(bf16[128,2176]{1,0:T(8,128)(2,1)S(1)} %get-tuple-element.96.refs_3_), channel_id=1, source_target_pairs={{0,4},{4,8},{8,12},{12,14},{14,10},{10,6},{6,2},{2,0},{1,5},{5,9},... | collective-permute-start | bytes 1671176 | tf_op jit(solution)/shard_map/ppermute | solution.py:42
  76.6 14.7 %collective-permute-start.8 = (bf16[128,2176]{1,0:T(8,128)(2,1)S(1)}, bf16[128,2176]{1,0:T(8,128)(2,1)S(1)}, u32[]{:S(2)}, u32[]{:S(2)}) collective-permute-start(bf16[128,2176]{1,0:T(8,128)(2,1)S(1)} %get-tuple-element.96.refs_3_), channel_id=1, source_target_pairs={{0,2},{4,0},{8,4},{12,8},{14,12},{10,14},{6,10},{2,6},{1,3},{5,1},... | collective-permute-start | bytes 1671176 | tf_op jit(solution)/shard_map/ppermute | solution.py:42
  91.3 2.5 %collective-permute-start.12 = (bf16[128,2176]{1,0:T(8,128)(2,1)S(1)}, bf16[128,2176]{1,0:T(8,128)(2,1)S(1)}, u32[]{:S(2)}, u32[]{:S(2)}) collective-permute-start(bf16[128,2176]{1,0:T(8,128)(2,1)S(1)} %collective-permute-done.7.refs_3_), channel_id=1, source_target_pairs={{0,1},{1,0},{2,3},{3,2},{4,5},{5,4},{6,7},{7,6},{8,9},{9,8},{10,11... | collective-permute-start | bytes 1671176 | tf_op jit(solution)/shard_map/ppermute | solution.py:34
  91.3 2.8 %collective-permute-start.13 = (bf16[128,2176]{1,0:T(8,128)(2,1)S(1)}, bf16[128,2176]{1,0:T(8,128)(2,1)S(1)}, u32[]{:S(2)}, u32[]{:S(2)}) collective-permute-start(bf16[128,2176]{1,0:T(8,128)(2,1)S(1)} %collective-permute-done.8.refs_5_), channel_id=1, source_target_pairs={{0,1},{1,0},{2,3},{3,2},{4,5},{5,4},{6,7},{7,6},{8,9},{9,8},{10,11... | collective-permute-start | bytes 1671176 | tf_op jit(solution)/shard_map/ppermute | solution.py:34
  91.8 14.5 %collective-permute-start.10 = (bf16[128,2176]{1,0:T(8,128)(2,1)S(1)}, bf16[128,2176]{1,0:T(8,128)(2,1)S(1)}, u32[]{:S(2)}, u32[]{:S(2)}) collective-permute-start(bf16[128,2176]{1,0:T(8,128)(2,1)S(1)} %collective-permute-done.7.refs_3_), channel_id=1, source_target_pairs={{0,4},{4,8},{8,12},{12,14},{14,10},{10,6},{6,2},{2,0},{1,5},{5,9},... | collective-permute-start | bytes 1671176 | tf_op jit(solution)/shard_map/ppermute | solution.py:42
  93.2 14.3 %collective-permute-start.11 = (bf16[128,2176]{1,0:T(8,128)(2,1)S(1)}, bf16[128,2176]{1,0:T(8,128)(2,1)S(1)}, u32[]{:S(2)}, u32[]{:S(2)}) collective-permute-start(bf16[128,2176]{1,0:T(8,128)(2,1)S(1)} %collective-permute-done.8.refs_5_), channel_id=1, source_target_pairs={{0,2},{4,0},{8,4},{12,8},{14,12},{10,14},{6,10},{2,6},{1,3},{5,1},... | collective-permute-start | bytes 1671176 | tf_op jit(solution)/shard_map/ppermute | solution.py:42
  94.0 13.5 %collective-permute-start.14 = (bf16[128,2048]{1,0:T(8,128)(2,1)S(1)}, bf16[128,2048]{1,0:T(8,128)(2,1)S(1)}, u32[]{:S(2)}, u32[]{:S(2)}) collective-permute-start(bf16[128,2048]{1,0:T(8,128)(2,1)S(1)} %get-tuple-element.110), channel_id=1, source_target_pairs={{0,1},{1,0},{2,3},{3,2},{4,5},{5,4},{6,7},{7,6},{8,9},{9,8},{10,11... | collective-permute-start | bytes 1572872 | tf_op jit(solution)/shard_map/ppermute | solution.py:34
  107.5 2.5 %collective-permute-start.17 = (bf16[128,2176]{1,0:T(8,128)(2,1)S(1)}, bf16[128,2176]{1,0:T(8,128)(2,1)S(1)}, u32[]{:S(2)}, u32[]{:S(2)}) collective-permute-start(bf16[128,2176]{1,0:T(8,128)(2,1)S(1)} %collective-permute-done.10.refs_3_), channel_id=1, source_target_pairs={{0,1},{1,0},{2,3},{3,2},{4,5},{5,4},{6,7},{7,6},{8,9},{9,8},{10,11... | collective-permute-start | bytes 1671176 | tf_op jit(solution)/shard_map/ppermute | solution.py:34
  107.5 2.8 %collective-permute-start.18 = (bf16[128,2176]{1,0:T(8,128)(2,1)S(1)}, bf16[128,2176]{1,0:T(8,128)(2,1)S(1)}, u32[]{:S(2)}, u32[]{:S(2)}) collective-permute-start(bf16[128,2176]{1,0:T(8,128)(2,1)S(1)} %collective-permute-done.11.refs_5_), channel_id=1, source_target_pairs={{0,1},{1,0},{2,3},{3,2},{4,5},{5,4},{6,7},{7,6},{8,9},{9,8},{10,11... | collective-permute-start | bytes 1671176 | tf_op jit(solution)/shard_map/ppermute | solution.py:34
  108.0 14.5 %collective-permute-start.15 = (bf16[128,2176]{1,0:T(8,128)(2,1)S(1)}, bf16[128,2176]{1,0:T(8,128)(2,1)S(1)}, u32[]{:S(2)}, u32[]{:S(2)}) collective-permute-start(bf16[128,2176]{1,0:T(8,128)(2,1)S(1)} %collective-permute-done.10.refs_3_), channel_id=1, source_target_pairs={{0,4},{4,8},{8,12},{12,14},{14,10},{10,6},{6,2},{2,0},{1,5},{5,9},... | collective-permute-start | bytes 1671176 | tf_op jit(solution)/shard_map/ppermute | solution.py:42
  109.5 14.3 %collective-permute-start.16 = (bf16[128,2176]{1,0:T(8,128)(2,1)S(1)}, bf16[128,2176]{1,0:T(8,128)(2,1)S(1)}, u32[]{:S(2)}, u32[]{:S(2)}) collective-permute-start(bf16[128,2176]{1,0:T(8,128)(2,1)S(1)} %collective-permute-done.11.refs_5_), channel_id=1, source_target_pairs={{0,2},{4,0},{8,4},{12,8},{14,12},{10,14},{6,10},{2,6},{1,3},{5,1},... | collective-permute-start | bytes 1671176 | tf_op jit(solution)/shard_map/ppermute | solution.py:42
  110.3 13.5 %collective-permute-start.19 = (bf16[128,2048]{1,0:T(8,128)(2,1)S(1)}, bf16[128,2048]{1,0:T(8,128)(2,1)S(1)}, u32[]{:S(2)}, u32[]{:S(2)}) collective-permute-start(bf16[128,2048]{1,0:T(8,128)(2,1)S(1)} %get-tuple-element.126), channel_id=1, source_target_pairs={{0,1},{1,0},{2,3},{3,2},{4,5},{5,4},{6,7},{7,6},{8,9},{9,8},{10,11... | collective-permute-start | bytes 1572872 | tf_op jit(solution)/shard_map/ppermute | solution.py:34
  110.4 13.3 %collective-permute-start.20 = (bf16[128,2048]{1,0:T(8,128)(2,1)S(1)}, bf16[128,2048]{1,0:T(8,128)(2,1)S(1)}, u32[]{:S(2)}, u32[]{:S(2)}) collective-permute-start(bf16[128,2048]{1,0:T(8,128)(2,1)S(1)} %get-tuple-element.128), channel_id=1, source_target_pairs={{0,1},{1,0},{2,3},{3,2},{4,5},{5,4},{6,7},{7,6},{8,9},{9,8},{10,11... | collective-permute-start | bytes 1572872 | tf_op jit(solution)/shard_map/ppermute | solution.py:34
  123.7 2.0 collective-permute-start.23
  123.8 3.2 %collective-permute-start.24 = (bf16[128,2176]{1,0:T(8,128)(2,1)S(1)}, bf16[128,2176]{1,0:T(8,128)(2,1)S(1)}, u32[]{:S(2)}, u32[]{:S(2)}) collective-permute-start(bf16[128,2176]{1,0:T(8,128)(2,1)S(1)} %collective-permute-done.16.refs_5_), channel_id=1, source_target_pairs={{0,1},{1,0},{2,3},{3,2},{4,5},{5,4},{6,7},{7,6},{8,9},{9,8},{10,11... | collective-permute-start | bytes 1671176 | tf_op jit(solution)/shard_map/ppermute | solution.py:34
  124.3 10.1 %collective-permute-start.25 = (bf16[128,2048]{1,0:T(8,128)(2,1)S(1)}, bf16[128,2048]{1,0:T(8,128)(2,1)S(1)}, u32[]{:S(2)}, u32[]{:S(2)}) collective-permute-start(bf16[128,2048]{1,0:T(8,128)(2,1)S(1)} %get-tuple-element.140), channel_id=1, source_target_pairs={{0,1},{1,0},{2,3},{3,2},{4,5},{5,4},{6,7},{7,6},{8,9},{9,8},{10,11... | collective-permute-start | bytes 1572872 | tf_op jit(solution)/shard_map/ppermute | solution.py:34
  124.3 10.1 %collective-permute-start.26 = (bf16[128,2048]{1,0:T(8,128)(2,1)S(1)}, bf16[128,2048]{1,0:T(8,128)(2,1)S(1)}, u32[]{:S(2)}, u32[]{:S(2)}) collective-permute-start(bf16[128,2048]{1,0:T(8,128)(2,1)S(1)} %get-tuple-element.142), channel_id=1, source_target_pairs={{0,1},{1,0},{2,3},{3,2},{4,5},{5,4},{6,7},{7,6},{8,9},{9,8},{10,11... | collective-permute-start | bytes 1572872 | tf_op jit(solution)/shard_map/ppermute | solution.py:34
  124.8 8.7 %collective-permute-start.21 = (bf16[64,2176]{1,0:T(8,128)(2,1)S(1)}, bf16[64,2176]{1,0:T(8,128)(2,1)S(1)}, u32[]{:S(2)}, u32[]{:S(2)}) collective-permute-start(bf16[64,2176]{1,0:T(8,128)(2,1)S(1)} %slice.98), channel_id=1, source_target_pairs={{0,4},{4,8},{8,12},{12,14},{14,10},{10,6},{6,2},{2,0},{1,5},{5,9},... | collective-permute-start | bytes 835592 | tf_op jit(solution)/shard_map/ppermute | solution.py:42
  125.7 8.7 %collective-permute-start.22 = (bf16[64,2176]{1,0:T(8,128)(2,1)S(1)}, bf16[64,2176]{1,0:T(8,128)(2,1)S(1)}, u32[]{:S(2)}, u32[]{:S(2)}) collective-permute-start(bf16[64,2176]{1,0:T(8,128)(2,1)S(1)} %slice.99), channel_id=1, source_target_pairs={{0,2},{4,0},{8,4},{12,8},{14,12},{10,14},{6,10},{2,6},{1,3},{5,1},... | collective-permute-start | bytes 835592 | tf_op jit(solution)/shard_map/ppermute | solution.py:42
  134.4 1.6 collective-permute-start.27
  134.4 1.9 collective-permute-start.28
  136.4 3.1 %collective-permute-start.29 = (bf16[128,2048]{1,0:T(8,128)(2,1)S(1)}, bf16[128,2048]{1,0:T(8,128)(2,1)S(1)}, u32[]{:S(2)}, u32[]{:S(2)}) collective-permute-start(bf16[128,2048]{1,0:T(8,128)(2,1)S(1)} %get-tuple-element.162), channel_id=1, source_target_pairs={{0,1},{1,0},{2,3},{3,2},{4,5},{5,4},{6,7},{7,6},{8,9},{9,8},{10,11... | collective-permute-start | bytes 1572872 | tf_op jit(solution)/shard_map/ppermute | solution.py:34
  136.5 3.0 %collective-permute-start.30 = (bf16[128,2048]{1,0:T(8,128)(2,1)S(1)}, bf16[128,2048]{1,0:T(8,128)(2,1)S(1)}, u32[]{:S(2)}, u32[]{:S(2)}) collective-permute-start(bf16[128,2048]{1,0:T(8,128)(2,1)S(1)} %get-tuple-element.164), channel_id=1, source_target_pairs={{0,1},{1,0},{2,3},{3,2},{4,5},{5,4},{6,7},{7,6},{8,9},{9,8},{10,11... | collective-permute-start | bytes 1572872 | tf_op jit(solution)/shard_map/ppermute | solution.py:34
  139.5 2.0 %collective-permute-start.31 = (bf16[128,2048]{1,0:T(8,128)(2,1)S(1)}, bf16[128,2048]{1,0:T(8,128)(2,1)S(1)}, u32[]{:S(2)}, u32[]{:S(2)}) collective-permute-start(bf16[128,2048]{1,0:T(8,128)(2,1)S(1)} %get-tuple-element.178), channel_id=1, source_target_pairs={{0,1},{1,0},{2,3},{3,2},{4,5},{5,4},{6,7},{7,6},{8,9},{9,8},{10,11... | collective-permute-start | bytes 1572872 | tf_op jit(solution)/shard_map/ppermute | solution.py:34
  141.7 8.4 %collective-permute-start.42 = (bf16[64,2048]{1,0:T(8,128)(2,1)S(1)}, bf16[64,2048]{1,0:T(8,128)(2,1)S(1)}, u32[]{:S(2)}, u32[]{:S(2)}) collective-permute-start(bf16[64,2048]{1,0:T(8,128)(2,1)S(1)} %get-tuple-element.191), channel_id=1, source_target_pairs={{0,2},{4,0},{8,4},{12,8},{14,12},{10,14},{6,10},{2,6},{1,3},{5,1},... | collective-permute-start | bytes 786440 | tf_op jit(solution)/shard_map/ppermute | solution.py:42
  142.6 9.1 %collective-permute-start.32 = (bf16[64,2048]{1,0:T(8,128)(2,1)S(1)}, bf16[64,2048]{1,0:T(8,128)(2,1)S(1)}, u32[]{:S(2)}, u32[]{:S(2)}) collective-permute-start(bf16[64,2048]{1,0:T(8,128)(2,1)S(1)} %get-tuple-element.192), channel_id=1, source_target_pairs={{0,4},{4,8},{8,12},{12,14},{14,10},{10,6},{6,2},{2,0},{1,5},{5,9},... | collective-permute-start | bytes 786440 | tf_op jit(solution)/shard_map/ppermute | solution.py:42
  150.2 9.3 %collective-permute-start.36 = (bf16[64,2048]{1,0:T(8,128)(2,1)S(1)}, bf16[64,2048]{1,0:T(8,128)(2,1)S(1)}, u32[]{:S(2)}, u32[]{:S(2)}) collective-permute-start(bf16[64,2048]{1,0:T(8,128)(2,1)S(1)} %get-tuple-element.190), channel_id=1, source_target_pairs={{0,2},{4,0},{8,4},{12,8},{14,12},{10,14},{6,10},{2,6},{1,3},{5,1},... | collective-permute-start | bytes 786440 | tf_op jit(solution)/shard_map/ppermute | solution.py:42
  151.1 12.3 %collective-permute-start.43 = (bf16[64,2048]{1,0:T(8,128)(2,1)S(1)}, bf16[64,2048]{1,0:T(8,128)(2,1)S(1)}, u32[]{:S(2)}, u32[]{:S(2)}) collective-permute-start(bf16[64,2048]{1,0:T(8,128)(2,1)S(1)} %get-tuple-element.189), channel_id=1, source_target_pairs={{0,2},{4,0},{8,4},{12,8},{14,12},{10,14},{6,10},{2,6},{1,3},{5,1},... | collective-permute-start | bytes 786440 | tf_op jit(solution)/shard_map/ppermute | solution.py:42
  151.9 13.2 %collective-permute-start.33 = (bf16[64,2048]{1,0:T(8,128)(2,1)S(1)}, bf16[64,2048]{1,0:T(8,128)(2,1)S(1)}, u32[]{:S(2)}, u32[]{:S(2)}) collective-permute-start(bf16[64,2048]{1,0:T(8,128)(2,1)S(1)} %get-tuple-element.198), channel_id=1, source_target_pairs={{0,4},{4,8},{8,12},{12,14},{14,10},{10,6},{6,2},{2,0},{1,5},{5,9},... | collective-permute-start | bytes 786440 | tf_op jit(solution)/shard_map/ppermute | solution.py:42
  153.4 11.7 %collective-permute-start.39 = (bf16[64,2048]{1,0:T(8,128)(2,1)S(1)}, bf16[64,2048]{1,0:T(8,128)(2,1)S(1)}, u32[]{:S(2)}, u32[]{:S(2)}) collective-permute-start(bf16[64,2048]{1,0:T(8,128)(2,1)S(1)} %get-tuple-element.197), channel_id=1, source_target_pairs={{0,4},{4,8},{8,12},{12,14},{14,10},{10,6},{6,2},{2,0},{1,5},{5,9},... | collective-permute-start | bytes 786440 | tf_op jit(solution)/shard_map/ppermute | solution.py:42
  163.7 9.3 %collective-permute-start.37 = (bf16[64,2048]{1,0:T(8,128)(2,1)S(1)}, bf16[64,2048]{1,0:T(8,128)(2,1)S(1)}, u32[]{:S(2)}, u32[]{:S(2)}) collective-permute-start(bf16[64,2048]{1,0:T(8,128)(2,1)S(1)} %get-tuple-element.188), channel_id=1, source_target_pairs={{0,2},{4,0},{8,4},{12,8},{14,12},{10,14},{6,10},{2,6},{1,3},{5,1},... | collective-permute-start | bytes 786440 | tf_op jit(solution)/shard_map/ppermute | solution.py:42
  164.6 11.4 %collective-permute-start.44 = (bf16[64,2048]{1,0:T(8,128)(2,1)S(1)}, bf16[64,2048]{1,0:T(8,128)(2,1)S(1)}, u32[]{:S(2)}, u32[]{:S(2)}) collective-permute-start(bf16[64,2048]{1,0:T(8,128)(2,1)S(1)} %get-tuple-element.187), channel_id=1, source_target_pairs={{0,2},{4,0},{8,4},{12,8},{14,12},{10,14},{6,10},{2,6},{1,3},{5,1},... | collective-permute-start | bytes 786440 | tf_op jit(solution)/shard_map/ppermute | solution.py:42
  165.4 12.3 %collective-permute-start.34 = (bf16[64,2048]{1,0:T(8,128)(2,1)S(1)}, bf16[64,2048]{1,0:T(8,128)(2,1)S(1)}, u32[]{:S(2)}, u32[]{:S(2)}) collective-permute-start(bf16[64,2048]{1,0:T(8,128)(2,1)S(1)} %get-tuple-element.196), channel_id=1, source_target_pairs={{0,4},{4,8},{8,12},{12,14},{14,10},{10,6},{6,2},{2,0},{1,5},{5,9},... | collective-permute-start | bytes 786440 | tf_op jit(solution)/shard_map/ppermute | solution.py:42
  166.9 10.7 %collective-permute-start.40 = (bf16[64,2048]{1,0:T(8,128)(2,1)S(1)}, bf16[64,2048]{1,0:T(8,128)(2,1)S(1)}, u32[]{:S(2)}, u32[]{:S(2)}) collective-permute-start(bf16[64,2048]{1,0:T(8,128)(2,1)S(1)} %get-tuple-element.195), channel_id=1, source_target_pairs={{0,4},{4,8},{8,12},{12,14},{14,10},{10,6},{6,2},{2,0},{1,5},{5,9},... | collective-permute-start | bytes 786440 | tf_op jit(solution)/shard_map/ppermute | solution.py:42
  176.2 8.5 %collective-permute-start.38 = (bf16[64,2048]{1,0:T(8,128)(2,1)S(1)}, bf16[64,2048]{1,0:T(8,128)(2,1)S(1)}, u32[]{:S(2)}, u32[]{:S(2)}) collective-permute-start(bf16[64,2048]{1,0:T(8,128)(2,1)S(1)} %get-tuple-element.186), channel_id=1, source_target_pairs={{0,2},{4,0},{8,4},{12,8},{14,12},{10,14},{6,10},{2,6},{1,3},{5,1},... | collective-permute-start | bytes 786440 | tf_op jit(solution)/shard_map/ppermute | solution.py:42
  177.1 10.4 %collective-permute-start.45 = (bf16[64,2048]{1,0:T(8,128)(2,1)S(1)}, bf16[64,2048]{1,0:T(8,128)(2,1)S(1)}, u32[]{:S(2)}, u32[]{:S(2)}) collective-permute-start(bf16[64,2048]{1,0:T(8,128)(2,1)S(1)} %get-tuple-element.185), channel_id=1, source_target_pairs={{0,2},{4,0},{8,4},{12,8},{14,12},{10,14},{6,10},{2,6},{1,3},{5,1},... | collective-permute-start | bytes 786440 | tf_op jit(solution)/shard_map/ppermute | solution.py:42
  177.9 9.6 %collective-permute-start.35 = (bf16[64,2048]{1,0:T(8,128)(2,1)S(1)}, bf16[64,2048]{1,0:T(8,128)(2,1)S(1)}, u32[]{:S(2)}, u32[]{:S(2)}) collective-permute-start(bf16[64,2048]{1,0:T(8,128)(2,1)S(1)} %get-tuple-element.194), channel_id=1, source_target_pairs={{0,4},{4,8},{8,12},{12,14},{14,10},{10,6},{6,2},{2,0},{1,5},{5,9},... | collective-permute-start | bytes 786440 | tf_op jit(solution)/shard_map/ppermute | solution.py:42
  179.4 9.3 %collective-permute-start.41 = (bf16[64,2048]{1,0:T(8,128)(2,1)S(1)}, bf16[64,2048]{1,0:T(8,128)(2,1)S(1)}, u32[]{:S(2)}, u32[]{:S(2)}) collective-permute-start(bf16[64,2048]{1,0:T(8,128)(2,1)S(1)} %get-tuple-element.193), channel_id=1, source_target_pairs={{0,4},{4,8},{8,12},{12,14},{14,10},{10,6},{6,2},{2,0},{1,5},{5,9},... | collective-permute-start | bytes 786440 | tf_op jit(solution)/shard_map/ppermute | solution.py:42
  (9 other events, 86.7 us)
Sparse Core Ops, SparseCore 0:
  9.9 50.5 all-gather.1

commit v6 on v4

--- a/solution.py
+++ b/solution.py
@@ -214,15 +214,13 @@
     own_heads, other_heads = attended[0], attended[1]
     sibling_heads = swap_cores(other_heads)
     projected = []
-    for back in list(range(1, n_ctx)) + [0]:
+    for back in range(n_ctx):
         heads = [rotate(own_heads, "ctx", back), rotate(sibling_heads, "ctx", back)]
         from_sibling = swap_cores(times_columns(heads[1]).astype(jnp.bfloat16))
-        part = lax.optimization_barrier(times_columns(heads[0]))
-        part = part + from_sibling.astype(jnp.float32)
+        part = times_columns(heads[0]) + from_sibling.astype(jnp.float32)
         if back:
             part = rotate(part.astype(jnp.bfloat16), "ctx", -back)
         projected.append(part)
-    projected = projected[-1:] + projected[:-1]
 
     local_experts = w_gate.shape[0]
     experts_all = n_exp * local_experts
@@ -298,19 +296,18 @@
     results, sums = barrier((results, sums))
     sums |= swap_results(results)
 
-    def total_at(direction, half, hop, carried):
-        offset = hop if direction > 0 else n_chip - hop
-        return total_of(sums[offset] + carried, half).astype(jnp.bfloat16)
-
-    def running_sum(direction, half, hops):
+    def running_sum(direction, half, hops, parts):
         carried = []
         for hop in range(hops, 0, -1):
-            carried = [round_ring(total_at(direction, half, hop, carried), direction)]
+            offset = hop if direction > 0 else n_chip - hop
+            total = total_of(parts[offset] + carried, half).astype(jnp.bfloat16)
+            carried = [round_ring(total, direction)]
         return carried
 
+    apart = barrier(sums)
     arrived = [
-        running_sum(1, 0, far) + running_sum(-1, 0, far - 1),
-        running_sum(1, 1, far - 1) + running_sum(-1, 1, far),
+        running_sum(1, 0, far, sums) + running_sum(-1, 0, far - 1, apart),
+        running_sum(1, 1, far - 1, apart) + running_sum(-1, 1, far, sums),
     ]
     return pl.pallas_call(
         final_kernel,

time: 197 us -> 195 us (0.990)
  waiting for transfers between devices: 111 us -> 109 us
    ppermute x22, waiting for transfers between devices: 61.2 us -> 58.6 us  [round_ring(): return lax.ppermute(block, 'exp', route)]
  transfers between devices with their start and end apart: 47 -> 47, of which waited for: 27 -> 28; matrix products, arithmetic and copies ran while one was open for 5% -> 5% of each run, Pallas kernels for 12% -> 12%
where the time goes in v6:
time: 195 us; the launch traced here: 194 us
  waiting for transfers between devices  109 us (56%)
  starting transfers between devices  33.8 us (17%)
  Pallas kernels  24.6 us (13%)
  between operations  13.7 us (7%)
  matrix products  6.57 us (3%)
  local copies, waits for them, and re-layouts  5.66 us (3%)
    ppermute x22, waiting for transfers between devices, round_ring(): return lax.ppermute(block, 'exp', route)  58.6 us
    ppermute x22, starting transfers between devices, round_ring(): return lax.ppermute(block, 'exp', route)  22.8 us
    ppermute x4, waiting for transfers between devices, rotate(): lax.ppermute(block, axis, [(i, (i + distance) % n) for i in range(n)])  22.3 us
    all_gather x1, waiting for transfers between devices, body(): lax.all_gather(lax.dynamic_slice_in_dim(out_proj, position * wide, wide,...  21.7 us
    pallas_call x5, Pallas kernels, run_expert(): pl.pallas_call(functools.partial(expert_kernel, experts_all, groups, part...  20.4 us
    ppermute x4, starting transfers between devices, rotate(): lax.ppermute(block, axis, [(i, (i + distance) % n) for i in range(n)])  6.66 us
    dot_general x4, matrix products, times_columns(): return jnp.dot(block, columns, preferred_element_type=jnp.float32)  6.57 us
    ppermute x20, waiting for transfers between devices, swap_cores(): return lax.ppermute(block, 'exp', [(i, i ^ 1) for i in range(n)])  6.04 us
  transfers between devices with their start and end apart: 47, of which 28 were waited for; matrix products, arithmetic and copies ran while one was open for 5% of the time, Pallas kernels for 12%

profile of v6, /device:TPU:0, one launch (start us, length us, event | category | flops | bytes accessed | tf_op | source)
XLA Modules:
  0.0 194.4 jit_solution(4157635198059459150)
XLA Ops:
  6.6 1.2 copy-done
  8.6 3.0 %collective-permute-start = (bf16[128,512]{1,0:T(8,128)(2,1)}, bf16[128,512]{1,0:T(8,128)(2,1)S(1)}, u32[]{:S(2)}, u32[]{:S(2)}) collective-permute-start(bf16[128,512]{1,0:T(8,128)(2,1)} %bitcast.42), channel_id=1, source_target_pairs={{0,16},{16,0},{1,17},{17,1},{2,18},{18,2},{3,19},{19,3},{4,20},{20... | collective-permute-start | bytes 393224 | tf_op jit(solution)/shard_map/ppermute | solution.py:49
  11.7 3.6 %collective-permute-done.refs_1_ = bf16[128,512]{1,0:T(8,128)(2,1)S(1)} collective-permute-done((bf16[128,512]{1,0:T(8,128)(2,1)}, bf16[128,512]{1,0:T(8,128)(2,1)S(1)}, u32[]{:S(2)}, u32[]{:S(2)}) %collective-permute-start) | collective-permute-done | bytes 131104 | tf_op jit(solution)/shard_map/ppermute | solution.py:49
  15.4 1.2 copy-done.4
  17.5 2.6 %attention.1 = bf16[2,128,2048]{2,1,0:T(8,128)(2,1)S(1)} custom-call(s32[2]{0:T(128)S(1)} %pad_add_fusion.pos_ref, bf16[128,4096]{1,0:T(8,128)(2,1)S(1)} %bitcast.38, bf16[128,512]{1,0:T(8,128)(2,1)S(1)} %bitcast.43, bf16[128,512]{1,0:T(8,128)(2,1)S(1)} %collective-permute-done.refs_1_), custom_call_target="tpu_custom_call" | custom-call | tf_op jit(solution)/shard_map/attention/pallas_call | solution.py:160
  20.1 0.9 slice_bitcast_fusion.1
  21.1 1.9 collective-permute-done.1
  23.0 1.7 collective-permute-start.4
  25.3 12.6 %collective-permute-done.4 = bf16[128,2048]{1,0:T(8,128)(2,1)} collective-permute-done((bf16[128,2048]{1,0:T(8,128)(2,1)S(1)}, bf16[128,2048]{1,0:T(8,128)(2,1)}, u32[]{:S(2)}, u32[]{:S(2)}) %collective-permute-start.4) | collective-permute-done | bytes 524320 | tf_op jit(solution)/shard_map/ppermute | solution.py:49
  37.8 21.7 %all-gather.2.cloned.1.call-done = bf16[2048,1024]{1,0:T(8,128)(2,1)} async-done(((bf16[256,1024]{1,0:T(8,128)(2,1)}), bf16[2048,1024]{1,0:T(8,128)(2,1)}) %all-gather.2.cloned.1.call-update) | async-done | bytes 4194320 | tf_op jit(solution)/shard_map/all_gather | solution.py:200
  59.5 3.2 %convolution_convert_fusion = bf16[128,1024]{1,0:T(8,128)(2,1)S(1)} fusion(bf16[128,2048]{1,0:T(8,128)(2,1)} %collective-permute-done.4, bf16[2048,1024]{1,0:T(8,128)(2,1)} %all-gather.2.cloned.1.call-done), kind=kOutput, calls=%fused_computation.3 | convolution fusion | flops 537001984 | bytes 4980736 | tf_op jit(solution)/shard_map/dot_general | solution.py:209
  64.4 1.9 fusion
  66.3 1.5 collective-permute-start.6
  68.6 6.1 %collective-permute-done.6.refs_1_ = bf16[128,1024]{1,0:T(8,128)(2,1)S(1)} collective-permute-done((bf16[128,1024]{1,0:T(8,128)(2,1)S(1)}, bf16[128,1024]{1,0:T(8,128)(2,1)S(1)}, u32[]{:S(2)}, u32[]{:S(2)}) %collective-permute-start.6) | collective-permute-done | bytes 262176 | tf_op jit(solution)/shard_map/ppermute | solution.py:49
  75.4 1.5 collective-permute-start.7
  77.5 2.6 %experts.5 = (bf16[128,2048]{1,0:T(8,128)(2,1)S(1)}, bf16[128,2048]{1,0:T(8,128)(2,1)S(1)}) custom-call(s32[1]{0:T(128)} %bitcast.9.expert_ref, bf16[2048,768]{1,0:T(8,128)(2,1)S(1)} %bitcast.23, bf16[2048,768]{1,0:T(8,128)(2,1)S(1)} %bitcast.28, bf16[768,2048]{1,0:T(8,128)(2,1)S(1)} %bitcast.33, bf16[128,2176]{1,0:T(8,128)(2,1)S(1)} %get-tuple-element.108.refs_3_, ...), custom_call_target="tpu_custom_call" | custom-call | flops 2415919104 | bytes 11534336 | tf_op jit(solution)/shard_map/experts/pallas_call | solution.py:175
  80.1 10.3 %collective-permute-done.7.refs_3_ = bf16[128,2176]{1,0:T(8,128)(2,1)S(1)} collective-permute-done((bf16[128,2176]{1,0:T(8,128)(2,1)S(1)}, bf16[128,2176]{1,0:T(8,128)(2,1)S(1)}, u32[]{:S(2)}, u32[]{:S(2)}) %collective-permute-start.7) | collective-permute-done | bytes 557088 | tf_op jit(solution)/shard_map/ppermute | solution.py:42
  90.4 1.2 collective-permute-done.8.refs_5_
  92.1 1.5 collective-permute-start.10
  94.5 5.1 %experts.6 = (bf16[128,2048]{1,0:T(8,128)(2,1)S(1)}, bf16[128,2048]{1,0:T(8,128)(2,1)S(1)}, bf16[128,2048]{1,0:T(8,128)(2,1)S(1)}, bf16[128,2048]{1,0:T(8,128)(2,1)S(1)}) custom-call(s32[1]{0:T(128)} %bitcast.9.expert_ref, bf16[2048,768]{1,0:T(8,128)(2,1)S(1)} %bitcast.24, bf16[2048,768]{1,0:T(8,128)(2,1)S(1)} %bitcast.29, bf16[768,2048]{1,0:T(8,128)(2,1)S(1)} %bitcast.34, ...), custom_call_target="tpu_custom_call" | custom-call | flops 4831838208 | bytes 13631488 | tf_op jit(solution)/shard_map/experts/pallas_call | solution.py:175
  99.5 7.1 %collective-permute-done.10.refs_3_ = bf16[128,2176]{1,0:T(8,128)(2,1)S(1)} collective-permute-done((bf16[128,2176]{1,0:T(8,128)(2,1)S(1)}, bf16[128,2176]{1,0:T(8,128)(2,1)S(1)}, u32[]{:S(2)}, u32[]{:S(2)}) %collective-permute-start.10) | collective-permute-done | bytes 557088 | tf_op jit(solution)/shard_map/ppermute | solution.py:42
  106.6 1.2 collective-permute-done.11.refs_5_
  108.3 1.5 collective-permute-start.15
  111.1 5.1 %experts.7 = (bf16[128,2048]{1,0:T(8,128)(2,1)S(1)}, bf16[128,2048]{1,0:T(8,128)(2,1)S(1)}, bf16[128,2048]{1,0:T(8,128)(2,1)S(1)}, bf16[128,2048]{1,0:T(8,128)(2,1)S(1)}) custom-call(s32[1]{0:T(128)} %bitcast.9.expert_ref, bf16[2048,768]{1,0:T(8,128)(2,1)S(1)} %bitcast.25, bf16[2048,768]{1,0:T(8,128)(2,1)S(1)} %bitcast.30, bf16[768,2048]{1,0:T(8,128)(2,1)S(1)} %bitcast.35, ...), custom_call_target="tpu_custom_call" | custom-call | flops 4831838208 | bytes 13631488 | tf_op jit(solution)/shard_map/experts/pallas_call | solution.py:175
  116.2 6.7 %collective-permute-done.15.refs_3_ = bf16[128,2176]{1,0:T(8,128)(2,1)S(1)} collective-permute-done((bf16[128,2176]{1,0:T(8,128)(2,1)S(1)}, bf16[128,2176]{1,0:T(8,128)(2,1)S(1)}, u32[]{:S(2)}, u32[]{:S(2)}) %collective-permute-start.15) | collective-permute-done | bytes 557088 | tf_op jit(solution)/shard_map/ppermute | solution.py:42
  122.9 1.2 collective-permute-done.16.refs_5_
  126.0 1.2 collective-permute-start.22
  127.2 5.1 %experts.8 = (bf16[128,2048]{1,0:T(8,128)(2,1)S(1)}, bf16[128,2048]{1,0:T(8,128)(2,1)S(1)}, bf16[128,2048]{1,0:T(8,128)(2,1)S(1)}, bf16[128,2048]{1,0:T(8,128)(2,1)S(1)}) custom-call(s32[1]{0:T(128)} %bitcast.9.expert_ref, bf16[2048,768]{1,0:T(8,128)(2,1)S(1)} %bitcast.26, bf16[2048,768]{1,0:T(8,128)(2,1)S(1)} %bitcast.31, bf16[768,2048]{1,0:T(8,128)(2,1)S(1)} %bitcast.36, ...), custom_call_target="tpu_custom_call" | custom-call | flops 4831838208 | bytes 13631488 | tf_op jit(solution)/shard_map/experts/pallas_call | solution.py:175
  132.3 1.5 collective-permute-done.21.refs_3_
  135.3 1.0 collective-permute-done.27.refs_5_
  137.2 2.6 %experts.9 = (bf16[128,2048]{1,0:T(8,128)(2,1)S(1)}, bf16[128,2048]{1,0:T(8,128)(2,1)S(1)}) custom-call(s32[1]{0:T(128)} %bitcast.9.expert_ref, bf16[2048,768]{1,0:T(8,128)(2,1)S(1)} %bitcast.27, bf16[2048,768]{1,0:T(8,128)(2,1)S(1)} %bitcast.32, bf16[768,2048]{1,0:T(8,128)(2,1)S(1)} %bitcast.37, bf16[64,2176]{1,0:T(8,128)(2,1)S(1)} %collective-permute-done.21.refs_3_, ...), custom_call_target="tpu_custom_call" | custom-call | flops 2415919104 | bytes 11534336 | tf_op jit(solution)/shard_map/experts/pallas_call | solution.py:175
  140.1 1.8 collective-permute-done.31
  142.9 1.2 collective-permute-start.39
  145.1 1.2 collective-permute-start.32
  146.3 4.9 %collective-permute-done.42 = bf16[64,2048]{1,0:T(8,128)(2,1)S(1)} collective-permute-done((bf16[64,2048]{1,0:T(8,128)(2,1)S(1)}, bf16[64,2048]{1,0:T(8,128)(2,1)S(1)}, u32[]{:S(2)}, u32[]{:S(2)}) %collective-permute-start.42) | collective-permute-done | bytes 262176 | tf_op jit(solution)/shard_map/ppermute | solution.py:42
  152.3 1.2 collective-permute-start.40
  153.5 3.3 %collective-permute-done.36 = bf16[64,2048]{1,0:T(8,128)(2,1)S(1)} collective-permute-done((bf16[64,2048]{1,0:T(8,128)(2,1)S(1)}, bf16[64,2048]{1,0:T(8,128)(2,1)S(1)}, u32[]{:S(2)}, u32[]{:S(2)}) %collective-permute-start.36) | collective-permute-done | bytes 262176 | tf_op jit(solution)/shard_map/ppermute | solution.py:42
  157.9 1.2 collective-permute-start.33
  159.1 3.3 %collective-permute-done.43 = bf16[64,2048]{1,0:T(8,128)(2,1)S(1)} collective-permute-done((bf16[64,2048]{1,0:T(8,128)(2,1)S(1)}, bf16[64,2048]{1,0:T(8,128)(2,1)S(1)}, u32[]{:S(2)}, u32[]{:S(2)}) %collective-permute-start.43) | collective-permute-done | bytes 262176 | tf_op jit(solution)/shard_map/ppermute | solution.py:42
  163.5 1.2 collective-permute-start.41
  164.7 3.3 %collective-permute-done.37 = bf16[64,2048]{1,0:T(8,128)(2,1)S(1)} collective-permute-done((bf16[64,2048]{1,0:T(8,128)(2,1)S(1)}, bf16[64,2048]{1,0:T(8,128)(2,1)S(1)}, u32[]{:S(2)}, u32[]{:S(2)}) %collective-permute-start.37) | collective-permute-done | bytes 262176 | tf_op jit(solution)/shard_map/ppermute | solution.py:42
  169.1 1.2 collective-permute-start.34
  170.4 3.3 %collective-permute-done.44 = bf16[64,2048]{1,0:T(8,128)(2,1)S(1)} collective-permute-done((bf16[64,2048]{1,0:T(8,128)(2,1)S(1)}, bf16[64,2048]{1,0:T(8,128)(2,1)S(1)}, u32[]{:S(2)}, u32[]{:S(2)}) %collective-permute-start.44) | collective-permute-done | bytes 262176 | tf_op jit(solution)/shard_map/ppermute | solution.py:42
  174.6 4.5 %collective-permute-done.34 = bf16[64,2048]{1,0:T(8,128)(2,1)S(1)} collective-permute-done((bf16[64,2048]{1,0:T(8,128)(2,1)S(1)}, bf16[64,2048]{1,0:T(8,128)(2,1)S(1)}, u32[]{:S(2)}, u32[]{:S(2)}) %collective-permute-start.34) | collective-permute-done | bytes 262176 | tf_op jit(solution)/shard_map/ppermute | solution.py:42
  179.2 1.2 collective-permute-start.35
  180.5 3.6 %collective-permute-done.45.refs_3_ = bf16[64,2048]{1,0:T(8,128)(2,1)S(1)} collective-permute-done((bf16[64,2048]{1,0:T(8,128)(2,1)S(1)}, bf16[64,2048]{1,0:T(8,128)(2,1)S(1)}, u32[]{:S(2)}, u32[]{:S(2)}) %collective-permute-start.45) | collective-permute-done | bytes 262176 | tf_op jit(solution)/shard_map/ppermute | solution.py:42
  184.1 2.4 %collective-permute-done.35.refs_0_ = bf16[64,2048]{1,0:T(8,128)(2,1)S(1)} collective-permute-done((bf16[64,2048]{1,0:T(8,128)(2,1)S(1)}, bf16[64,2048]{1,0:T(8,128)(2,1)S(1)}, u32[]{:S(2)}, u32[]{:S(2)}) %collective-permute-start.35) | collective-permute-done | bytes 262176 | tf_op jit(solution)/shard_map/ppermute | solution.py:42
  186.5 1.1 final.1
  (102 shorter events, 21.2 us)
Async XLA Ops:
  6.5 18.4 %copy-start.10 = (bf16[2048]{0:T(1024)(128)(2,1)S(1)}, bf16[2048]{0:T(1024)(128)(2,1)}, u32[]{:S(2)}) copy-start(bf16[2048]{0:T(1024)(128)(2,1)} %param.14) | copy-start | bytes 12292
  6.5 53.0 %all-gather.2.cloned.1.call-start = ((), (), s32[]{:S(2)}) async-start(), calls=%async_computation | async-start | bytes 4718592 | tf_op jit(solution)/shard_map/all_gather | solution.py:200
  8.6 6.7 %collective-permute-start = (bf16[128,512]{1,0:T(8,128)(2,1)}, bf16[128,512]{1,0:T(8,128)(2,1)S(1)}, u32[]{:S(2)}, u32[]{:S(2)}) collective-permute-start(bf16[128,512]{1,0:T(8,128)(2,1)} %bitcast.42), channel_id=1, source_target_pairs={{0,16},{16,0},{1,17},{17,1},{2,18},{18,2},{3,19},{19,3},{4,20},{20... | collective-permute-start | bytes 393224 | tf_op jit(solution)/shard_map/ppermute | solution.py:49
  21.0 1.9 collective-permute-start.1
  23.0 14.9 %collective-permute-start.4 = (bf16[128,2048]{1,0:T(8,128)(2,1)S(1)}, bf16[128,2048]{1,0:T(8,128)(2,1)}, u32[]{:S(2)}, u32[]{:S(2)}) collective-permute-start(bf16[128,2048]{1,0:T(8,128)(2,1)S(1)} %collective-permute-done.1), channel_id=1, source_target_pairs={{0,16},{16,0},{1,17},{17,1},{2,18},{18,2},{3,19},{19,3},{4,20},{20... | collective-permute-start | bytes 1572872 | tf_op jit(solution)/shard_map/ppermute | solution.py:49
  24.9 39.2 %collective-permute-start.3 = (bf16[128,2048]{1,0:T(8,128)(2,1)}, bf16[128,2048]{1,0:T(8,128)(2,1)}, u32[]{:S(2)}, u32[]{:S(2)}) collective-permute-start(bf16[128,2048]{1,0:T(8,128)(2,1)} %get-tuple-element.211), channel_id=1, source_target_pairs={{0,16},{16,0},{1,17},{17,1},{2,18},{18,2},{3,19},{19,3},{4,20},{20... | collective-permute-start | bytes 1572872 | tf_op jit(solution)/shard_map/ppermute | solution.py:49
  62.8 1.6 collective-permute-start.5
  63.9 4.0 %collective-permute-start.2 = (bf16[128,1024]{1,0:T(8,128)(2,1)S(1)}, bf16[128,1024]{1,0:T(8,128)(2,1)S(1)}, u32[]{:S(2)}, u32[]{:S(2)}) collective-permute-start(bf16[128,1024]{1,0:T(8,128)(2,1)S(1)} %convolution_convert_fusion.1), channel_id=1, source_target_pairs={{0,1},{1,0},{2,3},{3,2},{4,5},{5,4},{6,7},{7,6},{8,9},{9,8},{10,11... | collective-permute-start | bytes 786440 | tf_op jit(solution)/shard_map/ppermute | solution.py:34
  66.3 8.4 %collective-permute-start.6 = (bf16[128,1024]{1,0:T(8,128)(2,1)S(1)}, bf16[128,1024]{1,0:T(8,128)(2,1)S(1)}, u32[]{:S(2)}, u32[]{:S(2)}) collective-permute-start(bf16[128,1024]{1,0:T(8,128)(2,1)S(1)} %fusion), channel_id=1, source_target_pairs={{0,16},{16,0},{1,17},{17,1},{2,18},{18,2},{3,19},{19,3},{4,20},{20... | collective-permute-start | bytes 786440 | tf_op jit(solution)/shard_map/ppermute | solution.py:49
  75.3 2.2 %collective-permute-start.9 = (bf16[128,2176]{1,0:T(8,128)(2,1)S(1)}, bf16[128,2176]{1,0:T(8,128)(2,1)S(1)}, u32[]{:S(2)}, u32[]{:S(2)}) collective-permute-start(bf16[128,2176]{1,0:T(8,128)(2,1)S(1)} %get-tuple-element.108.refs_3_), channel_id=1, source_target_pairs={{0,1},{1,0},{2,3},{3,2},{4,5},{5,4},{6,7},{7,6},{8,9},{9,8},{10,11... | collective-permute-start | bytes 1671176 | tf_op jit(solution)/shard_map/ppermute | solution.py:34
  75.4 15.0 %collective-permute-start.7 = (bf16[128,2176]{1,0:T(8,128)(2,1)S(1)}, bf16[128,2176]{1,0:T(8,128)(2,1)S(1)}, u32[]{:S(2)}, u32[]{:S(2)}) collective-permute-start(bf16[128,2176]{1,0:T(8,128)(2,1)S(1)} %get-tuple-element.108.refs_3_), channel_id=1, source_target_pairs={{0,4},{4,8},{8,12},{12,14},{14,10},{10,6},{6,2},{2,0},{1,5},{5,9},... | collective-permute-start | bytes 1671176 | tf_op jit(solution)/shard_map/ppermute | solution.py:42
  76.9 14.7 %collective-permute-start.8 = (bf16[128,2176]{1,0:T(8,128)(2,1)S(1)}, bf16[128,2176]{1,0:T(8,128)(2,1)S(1)}, u32[]{:S(2)}, u32[]{:S(2)}) collective-permute-start(bf16[128,2176]{1,0:T(8,128)(2,1)S(1)} %get-tuple-element.108.refs_3_), channel_id=1, source_target_pairs={{0,2},{4,0},{8,4},{12,8},{14,12},{10,14},{6,10},{2,6},{1,3},{5,1},... | collective-permute-start | bytes 1671176 | tf_op jit(solution)/shard_map/ppermute | solution.py:42
  91.6 2.5 %collective-permute-start.12 = (bf16[128,2176]{1,0:T(8,128)(2,1)S(1)}, bf16[128,2176]{1,0:T(8,128)(2,1)S(1)}, u32[]{:S(2)}, u32[]{:S(2)}) collective-permute-start(bf16[128,2176]{1,0:T(8,128)(2,1)S(1)} %collective-permute-done.7.refs_3_), channel_id=1, source_target_pairs={{0,1},{1,0},{2,3},{3,2},{4,5},{5,4},{6,7},{7,6},{8,9},{9,8},{10,11... | collective-permute-start | bytes 1671176 | tf_op jit(solution)/shard_map/ppermute | solution.py:34
  91.6 2.8 %collective-permute-start.13 = (bf16[128,2176]{1,0:T(8,128)(2,1)S(1)}, bf16[128,2176]{1,0:T(8,128)(2,1)S(1)}, u32[]{:S(2)}, u32[]{:S(2)}) collective-permute-start(bf16[128,2176]{1,0:T(8,128)(2,1)S(1)} %collective-permute-done.8.refs_5_), channel_id=1, source_target_pairs={{0,1},{1,0},{2,3},{3,2},{4,5},{5,4},{6,7},{7,6},{8,9},{9,8},{10,11... | collective-permute-start | bytes 1671176 | tf_op jit(solution)/shard_map/ppermute | solution.py:34
  92.1 14.5 %collective-permute-start.10 = (bf16[128,2176]{1,0:T(8,128)(2,1)S(1)}, bf16[128,2176]{1,0:T(8,128)(2,1)S(1)}, u32[]{:S(2)}, u32[]{:S(2)}) collective-permute-start(bf16[128,2176]{1,0:T(8,128)(2,1)S(1)} %collective-permute-done.7.refs_3_), channel_id=1, source_target_pairs={{0,4},{4,8},{8,12},{12,14},{14,10},{10,6},{6,2},{2,0},{1,5},{5,9},... | collective-permute-start | bytes 1671176 | tf_op jit(solution)/shard_map/ppermute | solution.py:42
  93.6 14.3 %collective-permute-start.11 = (bf16[128,2176]{1,0:T(8,128)(2,1)S(1)}, bf16[128,2176]{1,0:T(8,128)(2,1)S(1)}, u32[]{:S(2)}, u32[]{:S(2)}) collective-permute-start(bf16[128,2176]{1,0:T(8,128)(2,1)S(1)} %collective-permute-done.8.refs_5_), channel_id=1, source_target_pairs={{0,2},{4,0},{8,4},{12,8},{14,12},{10,14},{6,10},{2,6},{1,3},{5,1},... | collective-permute-start | bytes 1671176 | tf_op jit(solution)/shard_map/ppermute | solution.py:42
  94.3 13.5 %collective-permute-start.14 = (bf16[128,2048]{1,0:T(8,128)(2,1)S(1)}, bf16[128,2048]{1,0:T(8,128)(2,1)S(1)}, u32[]{:S(2)}, u32[]{:S(2)}) collective-permute-start(bf16[128,2048]{1,0:T(8,128)(2,1)S(1)} %get-tuple-element.122), channel_id=1, source_target_pairs={{0,1},{1,0},{2,3},{3,2},{4,5},{5,4},{6,7},{7,6},{8,9},{9,8},{10,11... | collective-permute-start | bytes 1572872 | tf_op jit(solution)/shard_map/ppermute | solution.py:34
  107.8 2.5 %collective-permute-start.17 = (bf16[128,2176]{1,0:T(8,128)(2,1)S(1)}, bf16[128,2176]{1,0:T(8,128)(2,1)S(1)}, u32[]{:S(2)}, u32[]{:S(2)}) collective-permute-start(bf16[128,2176]{1,0:T(8,128)(2,1)S(1)} %collective-permute-done.10.refs_3_), channel_id=1, source_target_pairs={{0,1},{1,0},{2,3},{3,2},{4,5},{5,4},{6,7},{7,6},{8,9},{9,8},{10,11... | collective-permute-start | bytes 1671176 | tf_op jit(solution)/shard_map/ppermute | solution.py:34
  107.8 2.8 %collective-permute-start.18 = (bf16[128,2176]{1,0:T(8,128)(2,1)S(1)}, bf16[128,2176]{1,0:T(8,128)(2,1)S(1)}, u32[]{:S(2)}, u32[]{:S(2)}) collective-permute-start(bf16[128,2176]{1,0:T(8,128)(2,1)S(1)} %collective-permute-done.11.refs_5_), channel_id=1, source_target_pairs={{0,1},{1,0},{2,3},{3,2},{4,5},{5,4},{6,7},{7,6},{8,9},{9,8},{10,11... | collective-permute-start | bytes 1671176 | tf_op jit(solution)/shard_map/ppermute | solution.py:34
  108.3 14.5 %collective-permute-start.15 = (bf16[128,2176]{1,0:T(8,128)(2,1)S(1)}, bf16[128,2176]{1,0:T(8,128)(2,1)S(1)}, u32[]{:S(2)}, u32[]{:S(2)}) collective-permute-start(bf16[128,2176]{1,0:T(8,128)(2,1)S(1)} %collective-permute-done.10.refs_3_), channel_id=1, source_target_pairs={{0,4},{4,8},{8,12},{12,14},{14,10},{10,6},{6,2},{2,0},{1,5},{5,9},... | collective-permute-start | bytes 1671176 | tf_op jit(solution)/shard_map/ppermute | solution.py:42
  109.8 14.3 %collective-permute-start.16 = (bf16[128,2176]{1,0:T(8,128)(2,1)S(1)}, bf16[128,2176]{1,0:T(8,128)(2,1)S(1)}, u32[]{:S(2)}, u32[]{:S(2)}) collective-permute-start(bf16[128,2176]{1,0:T(8,128)(2,1)S(1)} %collective-permute-done.11.refs_5_), channel_id=1, source_target_pairs={{0,2},{4,0},{8,4},{12,8},{14,12},{10,14},{6,10},{2,6},{1,3},{5,1},... | collective-permute-start | bytes 1671176 | tf_op jit(solution)/shard_map/ppermute | solution.py:42
  110.6 13.5 %collective-permute-start.19 = (bf16[128,2048]{1,0:T(8,128)(2,1)S(1)}, bf16[128,2048]{1,0:T(8,128)(2,1)S(1)}, u32[]{:S(2)}, u32[]{:S(2)}) collective-permute-start(bf16[128,2048]{1,0:T(8,128)(2,1)S(1)} %get-tuple-element.138), channel_id=1, source_target_pairs={{0,1},{1,0},{2,3},{3,2},{4,5},{5,4},{6,7},{7,6},{8,9},{9,8},{10,11... | collective-permute-start | bytes 1572872 | tf_op jit(solution)/shard_map/ppermute | solution.py:34
  110.7 13.3 %collective-permute-start.20 = (bf16[128,2048]{1,0:T(8,128)(2,1)S(1)}, bf16[128,2048]{1,0:T(8,128)(2,1)S(1)}, u32[]{:S(2)}, u32[]{:S(2)}) collective-permute-start(bf16[128,2048]{1,0:T(8,128)(2,1)S(1)} %get-tuple-element.140), channel_id=1, source_target_pairs={{0,1},{1,0},{2,3},{3,2},{4,5},{5,4},{6,7},{7,6},{8,9},{9,8},{10,11... | collective-permute-start | bytes 1572872 | tf_op jit(solution)/shard_map/ppermute | solution.py:34
  124.1 2.0 %collective-permute-start.23 = (bf16[128,2176]{1,0:T(8,128)(2,1)S(1)}, bf16[128,2176]{1,0:T(8,128)(2,1)S(1)}, u32[]{:S(2)}, u32[]{:S(2)}) collective-permute-start(bf16[128,2176]{1,0:T(8,128)(2,1)S(1)} %collective-permute-done.15.refs_3_), channel_id=1, source_target_pairs={{0,1},{1,0},{2,3},{3,2},{4,5},{5,4},{6,7},{7,6},{8,9},{9,8},{10,11... | collective-permute-start | bytes 1671176 | tf_op jit(solution)/shard_map/ppermute | solution.py:34
  124.1 3.2 %collective-permute-start.24 = (bf16[128,2176]{1,0:T(8,128)(2,1)S(1)}, bf16[128,2176]{1,0:T(8,128)(2,1)S(1)}, u32[]{:S(2)}, u32[]{:S(2)}) collective-permute-start(bf16[128,2176]{1,0:T(8,128)(2,1)S(1)} %collective-permute-done.16.refs_5_), channel_id=1, source_target_pairs={{0,1},{1,0},{2,3},{3,2},{4,5},{5,4},{6,7},{7,6},{8,9},{9,8},{10,11... | collective-permute-start | bytes 1671176 | tf_op jit(solution)/shard_map/ppermute | solution.py:34
  124.6 10.1 %collective-permute-start.25 = (bf16[128,2048]{1,0:T(8,128)(2,1)S(1)}, bf16[128,2048]{1,0:T(8,128)(2,1)S(1)}, u32[]{:S(2)}, u32[]{:S(2)}) collective-permute-start(bf16[128,2048]{1,0:T(8,128)(2,1)S(1)} %get-tuple-element.152), channel_id=1, source_target_pairs={{0,1},{1,0},{2,3},{3,2},{4,5},{5,4},{6,7},{7,6},{8,9},{9,8},{10,11... | collective-permute-start | bytes 1572872 | tf_op jit(solution)/shard_map/ppermute | solution.py:34
  124.7 10.1 %collective-permute-start.26 = (bf16[128,2048]{1,0:T(8,128)(2,1)S(1)}, bf16[128,2048]{1,0:T(8,128)(2,1)S(1)}, u32[]{:S(2)}, u32[]{:S(2)}) collective-permute-start(bf16[128,2048]{1,0:T(8,128)(2,1)S(1)} %get-tuple-element.154), channel_id=1, source_target_pairs={{0,1},{1,0},{2,3},{3,2},{4,5},{5,4},{6,7},{7,6},{8,9},{9,8},{10,11... | collective-permute-start | bytes 1572872 | tf_op jit(solution)/shard_map/ppermute | solution.py:34
  125.2 8.7 %collective-permute-start.21 = (bf16[64,2176]{1,0:T(8,128)(2,1)S(1)}, bf16[64,2176]{1,0:T(8,128)(2,1)S(1)}, u32[]{:S(2)}, u32[]{:S(2)}) collective-permute-start(bf16[64,2176]{1,0:T(8,128)(2,1)S(1)} %slice.98), channel_id=1, source_target_pairs={{0,4},{4,8},{8,12},{12,14},{14,10},{10,6},{6,2},{2,0},{1,5},{5,9},... | collective-permute-start | bytes 835592 | tf_op jit(solution)/shard_map/ppermute | solution.py:42
  126.0 8.7 %collective-permute-start.22 = (bf16[64,2176]{1,0:T(8,128)(2,1)S(1)}, bf16[64,2176]{1,0:T(8,128)(2,1)S(1)}, u32[]{:S(2)}, u32[]{:S(2)}) collective-permute-start(bf16[64,2176]{1,0:T(8,128)(2,1)S(1)} %slice.99), channel_id=1, source_target_pairs={{0,2},{4,0},{8,4},{12,8},{14,12},{10,14},{6,10},{2,6},{1,3},{5,1},... | collective-permute-start | bytes 835592 | tf_op jit(solution)/shard_map/ppermute | solution.py:42
  134.7 1.6 collective-permute-start.27
  134.8 1.9 %collective-permute-start.28 = (bf16[64,2176]{1,0:T(8,128)(2,1)S(1)}, bf16[64,2176]{1,0:T(8,128)(2,1)S(1)}, u32[]{:S(2)}, u32[]{:S(2)}) collective-permute-start(bf16[64,2176]{1,0:T(8,128)(2,1)S(1)} %collective-permute-done.22.refs_4_), channel_id=1, source_target_pairs={{0,1},{1,0},{2,3},{3,2},{4,5},{5,4},{6,7},{7,6},{8,9},{9,8},{10,11... | collective-permute-start | bytes 835592 | tf_op jit(solution)/shard_map/ppermute | solution.py:34
  136.7 3.1 %collective-permute-start.29 = (bf16[128,2048]{1,0:T(8,128)(2,1)S(1)}, bf16[128,2048]{1,0:T(8,128)(2,1)S(1)}, u32[]{:S(2)}, u32[]{:S(2)}) collective-permute-start(bf16[128,2048]{1,0:T(8,128)(2,1)S(1)} %get-tuple-element.174), channel_id=1, source_target_pairs={{0,1},{1,0},{2,3},{3,2},{4,5},{5,4},{6,7},{7,6},{8,9},{9,8},{10,11... | collective-permute-start | bytes 1572872 | tf_op jit(solution)/shard_map/ppermute | solution.py:34
  136.8 3.0 %collective-permute-start.30 = (bf16[128,2048]{1,0:T(8,128)(2,1)S(1)}, bf16[128,2048]{1,0:T(8,128)(2,1)S(1)}, u32[]{:S(2)}, u32[]{:S(2)}) collective-permute-start(bf16[128,2048]{1,0:T(8,128)(2,1)S(1)} %get-tuple-element.176), channel_id=1, source_target_pairs={{0,1},{1,0},{2,3},{3,2},{4,5},{5,4},{6,7},{7,6},{8,9},{9,8},{10,11... | collective-permute-start | bytes 1572872 | tf_op jit(solution)/shard_map/ppermute | solution.py:34
  139.9 2.0 %collective-permute-start.31 = (bf16[128,2048]{1,0:T(8,128)(2,1)S(1)}, bf16[128,2048]{1,0:T(8,128)(2,1)S(1)}, u32[]{:S(2)}, u32[]{:S(2)}) collective-permute-start(bf16[128,2048]{1,0:T(8,128)(2,1)S(1)} %get-tuple-element.190), channel_id=1, source_target_pairs={{0,1},{1,0},{2,3},{3,2},{4,5},{5,4},{6,7},{7,6},{8,9},{9,8},{10,11... | collective-permute-start | bytes 1572872 | tf_op jit(solution)/shard_map/ppermute | solution.py:34
  142.0 9.2 %collective-permute-start.42 = (bf16[64,2048]{1,0:T(8,128)(2,1)S(1)}, bf16[64,2048]{1,0:T(8,128)(2,1)S(1)}, u32[]{:S(2)}, u32[]{:S(2)}) collective-permute-start(bf16[64,2048]{1,0:T(8,128)(2,1)S(1)} %get-tuple-element.209), channel_id=1, source_target_pairs={{0,2},{4,0},{8,4},{12,8},{14,12},{10,14},{6,10},{2,6},{1,3},{5,1},... | collective-permute-start | bytes 786440 | tf_op jit(solution)/shard_map/ppermute | solution.py:42
  142.9 9.2 %collective-permute-start.39 = (bf16[64,2048]{1,0:T(8,128)(2,1)S(1)}, bf16[64,2048]{1,0:T(8,128)(2,1)S(1)}, u32[]{:S(2)}, u32[]{:S(2)}) collective-permute-start(bf16[64,2048]{1,0:T(8,128)(2,1)S(1)} %add_convert_fusion.6), channel_id=1, source_target_pairs={{0,4},{4,8},{8,12},{12,14},{14,10},{10,6},{6,2},{2,0},{1,5},{5,9},... | collective-permute-start | bytes 786440 | tf_op jit(solution)/shard_map/ppermute | solution.py:42
  144.2 12.6 %collective-permute-start.36 = (bf16[64,2048]{1,0:T(8,128)(2,1)S(1)}, bf16[64,2048]{1,0:T(8,128)(2,1)S(1)}, u32[]{:S(2)}, u32[]{:S(2)}) collective-permute-start(bf16[64,2048]{1,0:T(8,128)(2,1)S(1)} %add_convert_fusion.9), channel_id=1, source_target_pairs={{0,2},{4,0},{8,4},{12,8},{14,12},{10,14},{6,10},{2,6},{1,3},{5,1},... | collective-permute-start | bytes 786440 | tf_op jit(solution)/shard_map/ppermute | solution.py:42
  145.1 12.7 %collective-permute-start.32 = (bf16[64,2048]{1,0:T(8,128)(2,1)S(1)}, bf16[64,2048]{1,0:T(8,128)(2,1)S(1)}, u32[]{:S(2)}, u32[]{:S(2)}) collective-permute-start(bf16[64,2048]{1,0:T(8,128)(2,1)S(1)} %get-tuple-element.210), channel_id=1, source_target_pairs={{0,4},{4,8},{8,12},{12,14},{14,10},{10,6},{6,2},{2,0},{1,5},{5,9},... | collective-permute-start | bytes 786440 | tf_op jit(solution)/shard_map/ppermute | solution.py:42
  151.3 11.1 %collective-permute-start.43 = (bf16[64,2048]{1,0:T(8,128)(2,1)S(1)}, bf16[64,2048]{1,0:T(8,128)(2,1)S(1)}, u32[]{:S(2)}, u32[]{:S(2)}) collective-permute-start(bf16[64,2048]{1,0:T(8,128)(2,1)S(1)} %add_convert_fusion.2), channel_id=1, source_target_pairs={{0,2},{4,0},{8,4},{12,8},{14,12},{10,14},{6,10},{2,6},{1,3},{5,1},... | collective-permute-start | bytes 786440 | tf_op jit(solution)/shard_map/ppermute | solution.py:42
  152.3 11.1 %collective-permute-start.40 = (bf16[64,2048]{1,0:T(8,128)(2,1)S(1)}, bf16[64,2048]{1,0:T(8,128)(2,1)S(1)}, u32[]{:S(2)}, u32[]{:S(2)}) collective-permute-start(bf16[64,2048]{1,0:T(8,128)(2,1)S(1)} %add_convert_fusion.5), channel_id=1, source_target_pairs={{0,4},{4,8},{8,12},{12,14},{14,10},{10,6},{6,2},{2,0},{1,5},{5,9},... | collective-permute-start | bytes 786440 | tf_op jit(solution)/shard_map/ppermute | solution.py:42
  156.9 11.1 %collective-permute-start.37 = (bf16[64,2048]{1,0:T(8,128)(2,1)S(1)}, bf16[64,2048]{1,0:T(8,128)(2,1)S(1)}, u32[]{:S(2)}, u32[]{:S(2)}) collective-permute-start(bf16[64,2048]{1,0:T(8,128)(2,1)S(1)} %add_convert_fusion.8), channel_id=1, source_target_pairs={{0,2},{4,0},{8,4},{12,8},{14,12},{10,14},{6,10},{2,6},{1,3},{5,1},... | collective-permute-start | bytes 786440 | tf_op jit(solution)/shard_map/ppermute | solution.py:42
  157.9 11.1 %collective-permute-start.33 = (bf16[64,2048]{1,0:T(8,128)(2,1)S(1)}, bf16[64,2048]{1,0:T(8,128)(2,1)S(1)}, u32[]{:S(2)}, u32[]{:S(2)}) collective-permute-start(bf16[64,2048]{1,0:T(8,128)(2,1)S(1)} %add_convert_fusion.12), channel_id=1, source_target_pairs={{0,4},{4,8},{8,12},{12,14},{14,10},{10,6},{6,2},{2,0},{1,5},{5,9},... | collective-permute-start | bytes 786440 | tf_op jit(solution)/shard_map/ppermute | solution.py:42
  162.5 11.1 %collective-permute-start.44 = (bf16[64,2048]{1,0:T(8,128)(2,1)S(1)}, bf16[64,2048]{1,0:T(8,128)(2,1)S(1)}, u32[]{:S(2)}, u32[]{:S(2)}) collective-permute-start(bf16[64,2048]{1,0:T(8,128)(2,1)S(1)} %add_convert_fusion.1), channel_id=1, source_target_pairs={{0,2},{4,0},{8,4},{12,8},{14,12},{10,14},{6,10},{2,6},{1,3},{5,1},... | collective-permute-start | bytes 786440 | tf_op jit(solution)/shard_map/ppermute | solution.py:42
  163.5 17.0 %collective-permute-start.41 = (bf16[64,2048]{1,0:T(8,128)(2,1)S(1)}, bf16[64,2048]{1,0:T(8,128)(2,1)S(1)}, u32[]{:S(2)}, u32[]{:S(2)}) collective-permute-start(bf16[64,2048]{1,0:T(8,128)(2,1)S(1)} %add_convert_fusion.4), channel_id=1, source_target_pairs={{0,4},{4,8},{8,12},{12,14},{14,10},{10,6},{6,2},{2,0},{1,5},{5,9},... | collective-permute-start | bytes 786440 | tf_op jit(solution)/shard_map/ppermute | solution.py:42
  168.1 12.4 %collective-permute-start.38 = (bf16[64,2048]{1,0:T(8,128)(2,1)S(1)}, bf16[64,2048]{1,0:T(8,128)(2,1)S(1)}, u32[]{:S(2)}, u32[]{:S(2)}) collective-permute-start(bf16[64,2048]{1,0:T(8,128)(2,1)S(1)} %add_convert_fusion.7), channel_id=1, source_target_pairs={{0,2},{4,0},{8,4},{12,8},{14,12},{10,14},{6,10},{2,6},{1,3},{5,1},... | collective-permute-start | bytes 786440 | tf_op jit(solution)/shard_map/ppermute | solution.py:42
  169.1 10.0 %collective-permute-start.34 = (bf16[64,2048]{1,0:T(8,128)(2,1)S(1)}, bf16[64,2048]{1,0:T(8,128)(2,1)S(1)}, u32[]{:S(2)}, u32[]{:S(2)}) collective-permute-start(bf16[64,2048]{1,0:T(8,128)(2,1)S(1)} %add_convert_fusion.11), channel_id=1, source_target_pairs={{0,4},{4,8},{8,12},{12,14},{14,10},{10,6},{6,2},{2,0},{1,5},{5,9},... | collective-permute-start | bytes 786440 | tf_op jit(solution)/shard_map/ppermute | solution.py:42
  173.7 10.3 %collective-permute-start.45 = (bf16[64,2048]{1,0:T(8,128)(2,1)S(1)}, bf16[64,2048]{1,0:T(8,128)(2,1)S(1)}, u32[]{:S(2)}, u32[]{:S(2)}) collective-permute-start(bf16[64,2048]{1,0:T(8,128)(2,1)S(1)} %add_convert_fusion), channel_id=1, source_target_pairs={{0,2},{4,0},{8,4},{12,8},{14,12},{10,14},{6,10},{2,6},{1,3},{5,1},... | collective-permute-start | bytes 786440 | tf_op jit(solution)/shard_map/ppermute | solution.py:42
  179.2 7.3 %collective-permute-start.35 = (bf16[64,2048]{1,0:T(8,128)(2,1)S(1)}, bf16[64,2048]{1,0:T(8,128)(2,1)S(1)}, u32[]{:S(2)}, u32[]{:S(2)}) collective-permute-start(bf16[64,2048]{1,0:T(8,128)(2,1)S(1)} %add_convert_fusion.10), channel_id=1, source_target_pairs={{0,4},{4,8},{8,12},{12,14},{14,10},{10,6},{6,2},{2,0},{1,5},{5,9},... | collective-permute-start | bytes 786440 | tf_op jit(solution)/shard_map/ppermute | solution.py:42
  (10 other events, 89.7 us)
Sparse Core Ops, SparseCore 0:
  8.9 50.5 all-gather.1

commit v7 on v6

--- a/solution.py
+++ b/solution.py
@@ -84,6 +84,28 @@
             out_ref[slot, :, at : at + HD] = (mixed / row_sum).astype(jnp.bfloat16)
 
 
+def sent_kernel(kept_ref, given_ref, weight_hbm, keep_ref, give_ref, weight_ref, sems):
+    pieces = sems.shape[0]
+    deep = weight_ref.shape[0] // pieces
+    copies = []
+    for i in range(pieces):
+        at = pl.ds(i * deep, deep)
+        copies.append(
+            pltpu.make_async_copy(weight_hbm.at[at], weight_ref.at[at], sems.at[i])
+        )
+        copies[-1].start()
+    total = None
+    for i in range(pieces):
+        copies[i].wait()
+        at = pl.ds(i * deep, deep)
+        left = jnp.concatenate([kept_ref[:, at], given_ref[:, at]], axis=0)
+        part = jnp.dot(left, weight_ref[at, :], preferred_element_type=jnp.float32)
+        total = part if total is None else total + part
+    rows = kept_ref.shape[0]
+    keep_ref[...] = total[:rows]
+    give_ref[...] = total[rows:].astype(jnp.bfloat16)
+
+
 def norm_kernel(experts_all, pos_ref, hidden_ref, *refs):
     *projected_refs, gain_ref, ids_ref, gates_ref, residual_ref, tokens_ref = refs
     n_ctx = len(projected_refs)
@@ -167,6 +189,25 @@
     )(jnp.stack([position, core]), queries, *blocks)
 
 
+def sent_products(kept, given, columns):
+    shape = (kept.shape[0], columns.shape[1])
+    return pl.pallas_call(
+        sent_kernel,
+        out_shape=(
+            jax.ShapeDtypeStruct(shape, jnp.float32),
+            jax.ShapeDtypeStruct(shape, jnp.bfloat16),
+        ),
+        in_specs=[vmem(), vmem(), pl.BlockSpec(memory_space=pl.ANY)],
+        out_specs=(vmem(), vmem()),
+        scratch_shapes=[
+            pltpu.VMEM(columns.shape, columns.dtype),
+            pltpu.SemaphoreType.DMA((4,)),
+        ],
+        compiler_params=pltpu.CompilerParams(vmem_limit_bytes=56 * 1024 * 1024),
+        name="sent",
+    )(kept, given, columns)
+
+
 def run_expert(experts_all, expert, chips, weights):
     groups, parts = len(chips), len(chips[0][0])
     blocks = [block for own, other in chips for block in own + other]
@@ -214,13 +255,14 @@
     own_heads, other_heads = attended[0], attended[1]
     sibling_heads = swap_cores(other_heads)
     projected = []
-    for back in range(n_ctx):
+    for back in range(1, n_ctx):
         heads = [rotate(own_heads, "ctx", back), rotate(sibling_heads, "ctx", back)]
-        from_sibling = swap_cores(times_columns(heads[1]).astype(jnp.bfloat16))
-        part = times_columns(heads[0]) + from_sibling.astype(jnp.float32)
-        if back:
-            part = rotate(part.astype(jnp.bfloat16), "ctx", -back)
-        projected.append(part)
+        keep, give = sent_products(heads[0], heads[1], columns)
+        part = (keep + swap_cores(give).astype(jnp.float32)).astype(jnp.bfloat16)
+        own_heads, sibling_heads, part = lax.optimization_barrier((own_heads, sibling_heads, part))
+        projected.append(rotate(part, "ctx", -back))
+    from_sibling = swap_cores(times_columns(sibling_heads).astype(jnp.bfloat16))
+    projected = [times_columns(own_heads) + from_sibling.astype(jnp.float32)] + projected
 
     local_experts = w_gate.shape[0]
     experts_all = n_exp * local_experts

time: 195 us -> 198 us (1.015)
  Pallas kernels: 24.6 us -> 30 us
  waiting for transfers between devices: 109 us -> 106 us
  matrix products: 6.57 us -> 3.87 us
    all_gather x1, waiting for transfers between devices: 21.7 us -> 13.7 us  [body(): lax.all_gather(lax.dynamic_slice_in_dim(out_proj, position * wide, wide,...]
    ppermute x4, waiting for transfers between devices: 22.3 us -> 29.5 us  [rotate(): lax.ppermute(block, axis, [(i, (i + distance) % n) for i in range(n)])]
    pallas_call x0 -> x1, Pallas kernels: none -> 5.34 us  [sent_products(): pl.pallas_call(sent_kernel, out_shape=(jax.ShapeDtypeStruct(shape, jnp.fl...]
    dot_general x4 -> x2, matrix products: 6.57 us -> 3.87 us  [times_columns(): return jnp.dot(block, columns, preferred_element_type=jnp.float32)]
    unnamed x24 -> x28, local copies, waits for them, and re-layouts: 3.84 us -> 5.49 us
  transfers between devices with their start and end apart: 47 -> 47, of which waited for: 28 -> 29; matrix products, arithmetic and copies ran while one was open for 5% -> 2% of each run, Pallas kernels for 12% -> 12%
where the time goes in v7:
time: 198 us; the launch traced here: 197 us
  waiting for transfers between devices  106 us (54%)
  starting transfers between devices  35.3 us (18%)
  Pallas kernels  30 us (15%)
  between operations  13.7 us (7%)
  local copies, waits for them, and re-layouts  6.44 us (3%)
  matrix products  3.87 us (2%)
  other arithmetic  2.45 us (1%)
    ppermute x22, waiting for transfers between devices, round_ring(): return lax.ppermute(block, 'exp', route)  56.7 us
    ppermute x4, waiting for transfers between devices, rotate(): lax.ppermute(block, axis, [(i, (i + distance) % n) for i in range(n)])  29.5 us
    ppermute x22, starting transfers between devices, round_ring(): return lax.ppermute(block, 'exp', route)  22.9 us
    pallas_call x5, Pallas kernels, run_expert(): pl.pallas_call(functools.partial(expert_kernel, experts_all, groups, part...  20.4 us
    all_gather x1, waiting for transfers between devices, body(): lax.all_gather(lax.dynamic_slice_in_dim(out_proj, position * wide, wide,...  13.7 us
    ppermute x4, starting transfers between devices, rotate(): lax.ppermute(block, axis, [(i, (i + distance) % n) for i in range(n)])  8.13 us
    ppermute x20, waiting for transfers between devices, swap_cores(): return lax.ppermute(block, 'exp', [(i, i ^ 1) for i in range(n)])  5.74 us
    unnamed x28, local copies, waits for them, and re-layouts  5.49 us
  transfers between devices with their start and end apart: 47, of which 29 were waited for; matrix products, arithmetic and copies ran while one was open for 2% of the time, Pallas kernels for 12%

profile of v7, /device:TPU:0, one launch (start us, length us, event | category | flops | bytes accessed | tf_op | source)
XLA Modules:
  0.0 197.4 jit_solution(14565630774810468344)
XLA Ops:
  6.5 1.2 copy-done
  8.6 3.0 %collective-permute-start = (bf16[128,512]{1,0:T(8,128)(2,1)}, bf16[128,512]{1,0:T(8,128)(2,1)S(1)}, u32[]{:S(2)}, u32[]{:S(2)}) collective-permute-start(bf16[128,512]{1,0:T(8,128)(2,1)} %bitcast.38), channel_id=1, source_target_pairs={{0,16},{16,0},{1,17},{17,1},{2,18},{18,2},{3,19},{19,3},{4,20},{20... | collective-permute-start | bytes 393224 | tf_op jit(solution)/shard_map/ppermute | solution.py:49
  11.7 3.6 %collective-permute-done.refs_1_ = bf16[128,512]{1,0:T(8,128)(2,1)S(1)} collective-permute-done((bf16[128,512]{1,0:T(8,128)(2,1)}, bf16[128,512]{1,0:T(8,128)(2,1)S(1)}, u32[]{:S(2)}, u32[]{:S(2)}) %collective-permute-start) | collective-permute-done | bytes 131104 | tf_op jit(solution)/shard_map/ppermute | solution.py:49
  15.4 1.2 copy-done.4
  17.5 2.6 %attention.1 = bf16[2,128,2048]{2,1,0:T(8,128)(2,1)S(1)} custom-call(s32[2]{0:T(128)S(1)} %pad_add_fusion.pos_ref, bf16[128,4096]{1,0:T(8,128)(2,1)S(1)} %bitcast.34, bf16[128,512]{1,0:T(8,128)(2,1)S(1)} %bitcast.39, bf16[128,512]{1,0:T(8,128)(2,1)S(1)} %collective-permute-done.refs_1_), custom_call_target="tpu_custom_call" | custom-call | tf_op jit(solution)/shard_map/attention/pallas_call | solution.py:182
  20.3 1.8 collective-permute-start.2
  22.2 1.7 collective-permute-start.3
  23.9 11.2 %collective-permute-done.2.kept_ref = bf16[128,2048]{1,0:T(8,128)(2,1)S(1)} collective-permute-done((bf16[128,2048]{1,0:T(8,128)(2,1)S(1)}, bf16[128,2048]{1,0:T(8,128)(2,1)S(1)}, u32[]{:S(2)}, u32[]{:S(2)}) %collective-permute-start.2) | collective-permute-done | bytes 524320 | tf_op jit(solution)/shard_map/ppermute | solution.py:49
  35.1 10.8 %collective-permute-done.3.given_ref = bf16[128,2048]{1,0:T(8,128)(2,1)S(1)} collective-permute-done((bf16[128,2048]{1,0:T(8,128)(2,1)S(1)}, bf16[128,2048]{1,0:T(8,128)(2,1)S(1)}, u32[]{:S(2)}, u32[]{:S(2)}) %collective-permute-start.3) | collective-permute-done | bytes 524320 | tf_op jit(solution)/shard_map/ppermute | solution.py:49
  45.9 13.7 %all-gather.2.cloned.1.call-done.weight_hbm = bf16[2048,1024]{1,0:T(8,128)(2,1)} async-done(((bf16[256,1024]{1,0:T(8,128)(2,1)}), bf16[2048,1024]{1,0:T(8,128)(2,1)}) %all-gather.2.cloned.1.call-update) | async-done | bytes 4194320 | tf_op jit(solution)/shard_map/all_gather | solution.py:241
  59.5 5.3 %sent.1 = (f32[128,1024]{1,0:T(8,128)}, bf16[128,1024]{1,0:T(8,128)(2,1)}) custom-call(bf16[128,2048]{1,0:T(8,128)(2,1)} %copy-done.8, bf16[128,2048]{1,0:T(8,128)(2,1)} %copy-done.9, bf16[2048,1024]{1,0:T(8,128)(2,1)} %all-gather.2.cloned.1.call-done.weight_hbm), custom_call_target="tpu_custom_call" | custom-call | tf_op jit(solution)/shard_map/sent/pallas_call | solution.py:194
  65.0 1.7 collective-permute-done.4
  69.0 1.6 collective-permute-start.6
  70.6 3.2 %convolution_add_fusion.refs_0_ = f32[128,1024]{1,0:T(8,128)S(1)} fusion(bf16[128,2048]{1,0:T(8,128)(2,1)S(1)} %get-tuple-element.114, bf16[2048,1024]{1,0:T(8,128)(2,1)} %all-gather.2.cloned.1.call-done.weight_hbm, bf16[128,1024]{1,0:T(8,128)(2,1)S(1)} %collective-permute-done.5), kind=kOutput, calls=%fused_computation | convolution fusion | flops 537133056 | bytes 5505024 | tf_op jit(solution)/shard_map/dot_general | solution.py:250
  73.8 3.9 %collective-permute-done.6.refs_1_ = bf16[128,1024]{1,0:T(8,128)(2,1)S(1)} collective-permute-done((bf16[128,1024]{1,0:T(8,128)(2,1)S(1)}, bf16[128,1024]{1,0:T(8,128)(2,1)S(1)}, u32[]{:S(2)}, u32[]{:S(2)}) %collective-permute-start.6) | collective-permute-done | bytes 262176 | tf_op jit(solution)/shard_map/ppermute | solution.py:49
  78.3 1.5 collective-permute-start.7
  80.4 1.9 copy-done.3
  82.3 2.6 %experts.5 = (bf16[128,2048]{1,0:T(8,128)(2,1)S(1)}, bf16[128,2048]{1,0:T(8,128)(2,1)S(1)}) custom-call(s32[1]{0:T(128)} %bitcast.9.expert_ref, bf16[2048,768]{1,0:T(8,128)(2,1)S(1)} %bitcast.19, bf16[2048,768]{1,0:T(8,128)(2,1)S(1)} %bitcast.24, bf16[768,2048]{1,0:T(8,128)(2,1)S(1)} %bitcast.29, bf16[128,2176]{1,0:T(8,128)(2,1)S(1)} %get-tuple-element.118.refs_3_, ...), custom_call_target="tpu_custom_call" | custom-call | flops 2415919104 | bytes 11534336 | tf_op jit(solution)/shard_map/experts/pallas_call | solution.py:216
  84.9 8.4 %collective-permute-done.7.refs_3_ = bf16[128,2176]{1,0:T(8,128)(2,1)S(1)} collective-permute-done((bf16[128,2176]{1,0:T(8,128)(2,1)S(1)}, bf16[128,2176]{1,0:T(8,128)(2,1)S(1)}, u32[]{:S(2)}, u32[]{:S(2)}) %collective-permute-start.7) | collective-permute-done | bytes 557088 | tf_op jit(solution)/shard_map/ppermute | solution.py:42
  93.3 1.2 collective-permute-done.8.refs_5_
  95.0 1.5 collective-permute-start.10
  97.4 5.1 %experts.6 = (bf16[128,2048]{1,0:T(8,128)(2,1)S(1)}, bf16[128,2048]{1,0:T(8,128)(2,1)S(1)}, bf16[128,2048]{1,0:T(8,128)(2,1)S(1)}, bf16[128,2048]{1,0:T(8,128)(2,1)S(1)}) custom-call(s32[1]{0:T(128)} %bitcast.9.expert_ref, bf16[2048,768]{1,0:T(8,128)(2,1)S(1)} %bitcast.20, bf16[2048,768]{1,0:T(8,128)(2,1)S(1)} %bitcast.25, bf16[768,2048]{1,0:T(8,128)(2,1)S(1)} %bitcast.30, ...), custom_call_target="tpu_custom_call" | custom-call | flops 4831838208 | bytes 13631488 | tf_op jit(solution)/shard_map/experts/pallas_call | solution.py:216
  102.5 7.1 %collective-permute-done.10.refs_3_ = bf16[128,2176]{1,0:T(8,128)(2,1)S(1)} collective-permute-done((bf16[128,2176]{1,0:T(8,128)(2,1)S(1)}, bf16[128,2176]{1,0:T(8,128)(2,1)S(1)}, u32[]{:S(2)}, u32[]{:S(2)}) %collective-permute-start.10) | collective-permute-done | bytes 557088 | tf_op jit(solution)/shard_map/ppermute | solution.py:42
  109.6 1.2 collective-permute-done.11.refs_5_
  111.3 1.5 collective-permute-start.15
  114.1 5.1 %experts.7 = (bf16[128,2048]{1,0:T(8,128)(2,1)S(1)}, bf16[128,2048]{1,0:T(8,128)(2,1)S(1)}, bf16[128,2048]{1,0:T(8,128)(2,1)S(1)}, bf16[128,2048]{1,0:T(8,128)(2,1)S(1)}) custom-call(s32[1]{0:T(128)} %bitcast.9.expert_ref, bf16[2048,768]{1,0:T(8,128)(2,1)S(1)} %bitcast.21, bf16[2048,768]{1,0:T(8,128)(2,1)S(1)} %bitcast.26, bf16[768,2048]{1,0:T(8,128)(2,1)S(1)} %bitcast.31, ...), custom_call_target="tpu_custom_call" | custom-call | flops 4831838208 | bytes 13631488 | tf_op jit(solution)/shard_map/experts/pallas_call | solution.py:216
  119.1 6.7 %collective-permute-done.15.refs_3_ = bf16[128,2176]{1,0:T(8,128)(2,1)S(1)} collective-permute-done((bf16[128,2176]{1,0:T(8,128)(2,1)S(1)}, bf16[128,2176]{1,0:T(8,128)(2,1)S(1)}, u32[]{:S(2)}, u32[]{:S(2)}) %collective-permute-start.15) | collective-permute-done | bytes 557088 | tf_op jit(solution)/shard_map/ppermute | solution.py:42
  125.8 1.2 collective-permute-done.16.refs_5_
  129.0 1.2 collective-permute-start.22
  130.2 5.1 %experts.8 = (bf16[128,2048]{1,0:T(8,128)(2,1)S(1)}, bf16[128,2048]{1,0:T(8,128)(2,1)S(1)}, bf16[128,2048]{1,0:T(8,128)(2,1)S(1)}, bf16[128,2048]{1,0:T(8,128)(2,1)S(1)}) custom-call(s32[1]{0:T(128)} %bitcast.9.expert_ref, bf16[2048,768]{1,0:T(8,128)(2,1)S(1)} %bitcast.22, bf16[2048,768]{1,0:T(8,128)(2,1)S(1)} %bitcast.27, bf16[768,2048]{1,0:T(8,128)(2,1)S(1)} %bitcast.32, ...), custom_call_target="tpu_custom_call" | custom-call | flops 4831838208 | bytes 13631488 | tf_op jit(solution)/shard_map/experts/pallas_call | solution.py:216
  135.3 1.5 collective-permute-done.21.refs_3_
  140.2 2.6 %experts.9 = (bf16[128,2048]{1,0:T(8,128)(2,1)S(1)}, bf16[128,2048]{1,0:T(8,128)(2,1)S(1)}) custom-call(s32[1]{0:T(128)} %bitcast.9.expert_ref, bf16[2048,768]{1,0:T(8,128)(2,1)S(1)} %bitcast.23, bf16[2048,768]{1,0:T(8,128)(2,1)S(1)} %bitcast.28, bf16[768,2048]{1,0:T(8,128)(2,1)S(1)} %bitcast.33, bf16[64,2176]{1,0:T(8,128)(2,1)S(1)} %collective-permute-done.21.refs_3_, ...), custom_call_target="tpu_custom_call" | custom-call | flops 2415919104 | bytes 11534336 | tf_op jit(solution)/shard_map/experts/pallas_call | solution.py:216
  143.0 1.8 collective-permute-done.31
  145.9 1.2 collective-permute-start.39
  148.1 1.2 collective-permute-start.32
  149.3 4.9 %collective-permute-done.42 = bf16[64,2048]{1,0:T(8,128)(2,1)S(1)} collective-permute-done((bf16[64,2048]{1,0:T(8,128)(2,1)S(1)}, bf16[64,2048]{1,0:T(8,128)(2,1)S(1)}, u32[]{:S(2)}, u32[]{:S(2)}) %collective-permute-start.42) | collective-permute-done | bytes 262176 | tf_op jit(solution)/shard_map/ppermute | solution.py:42
  155.2 1.2 collective-permute-start.40
  156.5 3.3 %collective-permute-done.36 = bf16[64,2048]{1,0:T(8,128)(2,1)S(1)} collective-permute-done((bf16[64,2048]{1,0:T(8,128)(2,1)S(1)}, bf16[64,2048]{1,0:T(8,128)(2,1)S(1)}, u32[]{:S(2)}, u32[]{:S(2)}) %collective-permute-start.36) | collective-permute-done | bytes 262176 | tf_op jit(solution)/shard_map/ppermute | solution.py:42
  160.9 1.2 collective-permute-start.33
  162.1 3.3 %collective-permute-done.43 = bf16[64,2048]{1,0:T(8,128)(2,1)S(1)} collective-permute-done((bf16[64,2048]{1,0:T(8,128)(2,1)S(1)}, bf16[64,2048]{1,0:T(8,128)(2,1)S(1)}, u32[]{:S(2)}, u32[]{:S(2)}) %collective-permute-start.43) | collective-permute-done | bytes 262176 | tf_op jit(solution)/shard_map/ppermute | solution.py:42
  166.5 1.2 collective-permute-start.41
  167.7 3.3 %collective-permute-done.37 = bf16[64,2048]{1,0:T(8,128)(2,1)S(1)} collective-permute-done((bf16[64,2048]{1,0:T(8,128)(2,1)S(1)}, bf16[64,2048]{1,0:T(8,128)(2,1)S(1)}, u32[]{:S(2)}, u32[]{:S(2)}) %collective-permute-start.37) | collective-permute-done | bytes 262176 | tf_op jit(solution)/shard_map/ppermute | solution.py:42
  172.1 1.2 collective-permute-start.34
  173.3 3.3 %collective-permute-done.44 = bf16[64,2048]{1,0:T(8,128)(2,1)S(1)} collective-permute-done((bf16[64,2048]{1,0:T(8,128)(2,1)S(1)}, bf16[64,2048]{1,0:T(8,128)(2,1)S(1)}, u32[]{:S(2)}, u32[]{:S(2)}) %collective-permute-start.44) | collective-permute-done | bytes 262176 | tf_op jit(solution)/shard_map/ppermute | solution.py:42
  177.6 4.5 %collective-permute-done.34 = bf16[64,2048]{1,0:T(8,128)(2,1)S(1)} collective-permute-done((bf16[64,2048]{1,0:T(8,128)(2,1)S(1)}, bf16[64,2048]{1,0:T(8,128)(2,1)S(1)}, u32[]{:S(2)}, u32[]{:S(2)}) %collective-permute-start.34) | collective-permute-done | bytes 262176 | tf_op jit(solution)/shard_map/ppermute | solution.py:42
  182.2 1.2 collective-permute-start.35
  183.4 3.6 %collective-permute-done.45.refs_3_ = bf16[64,2048]{1,0:T(8,128)(2,1)S(1)} collective-permute-done((bf16[64,2048]{1,0:T(8,128)(2,1)S(1)}, bf16[64,2048]{1,0:T(8,128)(2,1)S(1)}, u32[]{:S(2)}, u32[]{:S(2)}) %collective-permute-start.45) | collective-permute-done | bytes 262176 | tf_op jit(solution)/shard_map/ppermute | solution.py:42
  187.0 2.4 %collective-permute-done.35.refs_0_ = bf16[64,2048]{1,0:T(8,128)(2,1)S(1)} collective-permute-done((bf16[64,2048]{1,0:T(8,128)(2,1)S(1)}, bf16[64,2048]{1,0:T(8,128)(2,1)S(1)}, u32[]{:S(2)}, u32[]{:S(2)}) %collective-permute-start.35) | collective-permute-done | bytes 262176 | tf_op jit(solution)/shard_map/ppermute | solution.py:42
  (106 shorter events, 23.1 us)
Async XLA Ops:
  6.5 53.0 %all-gather.2.cloned.1.call-start = ((), (), s32[]{:S(2)}) async-start(), calls=%async_computation | async-start | bytes 4718592 | tf_op jit(solution)/shard_map/all_gather | solution.py:241
  8.6 6.7 %collective-permute-start = (bf16[128,512]{1,0:T(8,128)(2,1)}, bf16[128,512]{1,0:T(8,128)(2,1)S(1)}, u32[]{:S(2)}, u32[]{:S(2)}) collective-permute-start(bf16[128,512]{1,0:T(8,128)(2,1)} %bitcast.38), channel_id=1, source_target_pairs={{0,16},{16,0},{1,17},{17,1},{2,18},{18,2},{3,19},{19,3},{4,20},{20... | collective-permute-start | bytes 393224 | tf_op jit(solution)/shard_map/ppermute | solution.py:49
  20.2 2.0 %collective-permute-start.1 = (bf16[128,2048]{1,0:T(8,128)(2,1)S(1)}, bf16[128,2048]{1,0:T(8,128)(2,1)S(1)}, u32[]{:S(2)}, u32[]{:S(2)}) collective-permute-start(bf16[128,2048]{1,0:T(8,128)(2,1)S(1)} %get-tuple-element.221), channel_id=1, source_target_pairs={{0,1},{1,0},{2,3},{3,2},{4,5},{5,4},{6,7},{7,6},{8,9},{9,8},{10,11... | collective-permute-start | bytes 1572872 | tf_op jit(solution)/shard_map/ppermute | solution.py:34
  20.3 14.8 %collective-permute-start.2 = (bf16[128,2048]{1,0:T(8,128)(2,1)S(1)}, bf16[128,2048]{1,0:T(8,128)(2,1)S(1)}, u32[]{:S(2)}, u32[]{:S(2)}) collective-permute-start(bf16[128,2048]{1,0:T(8,128)(2,1)S(1)} %get-tuple-element.114), channel_id=1, source_target_pairs={{0,16},{16,0},{1,17},{17,1},{2,18},{18,2},{3,19},{19,3},{4,20},{20... | collective-permute-start | bytes 1572872 | tf_op jit(solution)/shard_map/ppermute | solution.py:49
  22.2 23.7 %collective-permute-start.3 = (bf16[128,2048]{1,0:T(8,128)(2,1)S(1)}, bf16[128,2048]{1,0:T(8,128)(2,1)S(1)}, u32[]{:S(2)}, u32[]{:S(2)}) collective-permute-start(bf16[128,2048]{1,0:T(8,128)(2,1)S(1)} %collective-permute-done.1), channel_id=1, source_target_pairs={{0,16},{16,0},{1,17},{17,1},{2,18},{18,2},{3,19},{19,3},{4,20},{20... | collective-permute-start | bytes 1572872 | tf_op jit(solution)/shard_map/ppermute | solution.py:49
  35.1 24.5 %copy-start.8 = (bf16[128,2048]{1,0:T(8,128)(2,1)}, bf16[128,2048]{1,0:T(8,128)(2,1)S(1)}, u32[]{:S(2)}) copy-start(bf16[128,2048]{1,0:T(8,128)(2,1)S(1)} %collective-permute-done.2.kept_ref) | copy-start | bytes 1572868
  64.9 1.8 collective-permute-start.4
  68.6 2.0 %collective-permute-start.5 = (bf16[128,1024]{1,0:T(8,128)(2,1)S(1)}, bf16[128,1024]{1,0:T(8,128)(2,1)S(1)}, u32[]{:S(2)}, u32[]{:S(2)}) collective-permute-start(bf16[128,1024]{1,0:T(8,128)(2,1)S(1)} %convolution_convert_fusion), channel_id=1, source_target_pairs={{0,1},{1,0},{2,3},{3,2},{4,5},{5,4},{6,7},{7,6},{8,9},{9,8},{10,11... | collective-permute-start | bytes 786440 | tf_op jit(solution)/shard_map/ppermute | solution.py:34
  69.0 8.6 %collective-permute-start.6 = (bf16[128,1024]{1,0:T(8,128)(2,1)S(1)}, bf16[128,1024]{1,0:T(8,128)(2,1)S(1)}, u32[]{:S(2)}, u32[]{:S(2)}) collective-permute-start(bf16[128,1024]{1,0:T(8,128)(2,1)S(1)} %add_convert_fusion.14), channel_id=1, source_target_pairs={{0,16},{16,0},{1,17},{17,1},{2,18},{18,2},{3,19},{19,3},{4,20},{20... | collective-permute-start | bytes 786440 | tf_op jit(solution)/shard_map/ppermute | solution.py:49
  78.2 2.2 %collective-permute-start.9 = (bf16[128,2176]{1,0:T(8,128)(2,1)S(1)}, bf16[128,2176]{1,0:T(8,128)(2,1)S(1)}, u32[]{:S(2)}, u32[]{:S(2)}) collective-permute-start(bf16[128,2176]{1,0:T(8,128)(2,1)S(1)} %get-tuple-element.118.refs_3_), channel_id=1, source_target_pairs={{0,1},{1,0},{2,3},{3,2},{4,5},{5,4},{6,7},{7,6},{8,9},{9,8},{10,11... | collective-permute-start | bytes 1671176 | tf_op jit(solution)/shard_map/ppermute | solution.py:34
  78.3 15.0 %collective-permute-start.7 = (bf16[128,2176]{1,0:T(8,128)(2,1)S(1)}, bf16[128,2176]{1,0:T(8,128)(2,1)S(1)}, u32[]{:S(2)}, u32[]{:S(2)}) collective-permute-start(bf16[128,2176]{1,0:T(8,128)(2,1)S(1)} %get-tuple-element.118.refs_3_), channel_id=1, source_target_pairs={{0,4},{4,8},{8,12},{12,14},{14,10},{10,6},{6,2},{2,0},{1,5},{5,9},... | collective-permute-start | bytes 1671176 | tf_op jit(solution)/shard_map/ppermute | solution.py:42
  79.8 14.7 %collective-permute-start.8 = (bf16[128,2176]{1,0:T(8,128)(2,1)S(1)}, bf16[128,2176]{1,0:T(8,128)(2,1)S(1)}, u32[]{:S(2)}, u32[]{:S(2)}) collective-permute-start(bf16[128,2176]{1,0:T(8,128)(2,1)S(1)} %get-tuple-element.118.refs_3_), channel_id=1, source_target_pairs={{0,2},{4,0},{8,4},{12,8},{14,12},{10,14},{6,10},{2,6},{1,3},{5,1},... | collective-permute-start | bytes 1671176 | tf_op jit(solution)/shard_map/ppermute | solution.py:42
  94.5 2.5 %collective-permute-start.12 = (bf16[128,2176]{1,0:T(8,128)(2,1)S(1)}, bf16[128,2176]{1,0:T(8,128)(2,1)S(1)}, u32[]{:S(2)}, u32[]{:S(2)}) collective-permute-start(bf16[128,2176]{1,0:T(8,128)(2,1)S(1)} %collective-permute-done.7.refs_3_), channel_id=1, source_target_pairs={{0,1},{1,0},{2,3},{3,2},{4,5},{5,4},{6,7},{7,6},{8,9},{9,8},{10,11... | collective-permute-start | bytes 1671176 | tf_op jit(solution)/shard_map/ppermute | solution.py:34
  94.5 2.8 %collective-permute-start.13 = (bf16[128,2176]{1,0:T(8,128)(2,1)S(1)}, bf16[128,2176]{1,0:T(8,128)(2,1)S(1)}, u32[]{:S(2)}, u32[]{:S(2)}) collective-permute-start(bf16[128,2176]{1,0:T(8,128)(2,1)S(1)} %collective-permute-done.8.refs_5_), channel_id=1, source_target_pairs={{0,1},{1,0},{2,3},{3,2},{4,5},{5,4},{6,7},{7,6},{8,9},{9,8},{10,11... | collective-permute-start | bytes 1671176 | tf_op jit(solution)/shard_map/ppermute | solution.py:34
  95.0 14.5 %collective-permute-start.10 = (bf16[128,2176]{1,0:T(8,128)(2,1)S(1)}, bf16[128,2176]{1,0:T(8,128)(2,1)S(1)}, u32[]{:S(2)}, u32[]{:S(2)}) collective-permute-start(bf16[128,2176]{1,0:T(8,128)(2,1)S(1)} %collective-permute-done.7.refs_3_), channel_id=1, source_target_pairs={{0,4},{4,8},{8,12},{12,14},{14,10},{10,6},{6,2},{2,0},{1,5},{5,9},... | collective-permute-start | bytes 1671176 | tf_op jit(solution)/shard_map/ppermute | solution.py:42
  96.5 14.3 %collective-permute-start.11 = (bf16[128,2176]{1,0:T(8,128)(2,1)S(1)}, bf16[128,2176]{1,0:T(8,128)(2,1)S(1)}, u32[]{:S(2)}, u32[]{:S(2)}) collective-permute-start(bf16[128,2176]{1,0:T(8,128)(2,1)S(1)} %collective-permute-done.8.refs_5_), channel_id=1, source_target_pairs={{0,2},{4,0},{8,4},{12,8},{14,12},{10,14},{6,10},{2,6},{1,3},{5,1},... | collective-permute-start | bytes 1671176 | tf_op jit(solution)/shard_map/ppermute | solution.py:42
  97.3 13.5 %collective-permute-start.14 = (bf16[128,2048]{1,0:T(8,128)(2,1)S(1)}, bf16[128,2048]{1,0:T(8,128)(2,1)S(1)}, u32[]{:S(2)}, u32[]{:S(2)}) collective-permute-start(bf16[128,2048]{1,0:T(8,128)(2,1)S(1)} %get-tuple-element.132), channel_id=1, source_target_pairs={{0,1},{1,0},{2,3},{3,2},{4,5},{5,4},{6,7},{7,6},{8,9},{9,8},{10,11... | collective-permute-start | bytes 1572872 | tf_op jit(solution)/shard_map/ppermute | solution.py:34
  110.8 2.5 %collective-permute-start.17 = (bf16[128,2176]{1,0:T(8,128)(2,1)S(1)}, bf16[128,2176]{1,0:T(8,128)(2,1)S(1)}, u32[]{:S(2)}, u32[]{:S(2)}) collective-permute-start(bf16[128,2176]{1,0:T(8,128)(2,1)S(1)} %collective-permute-done.10.refs_3_), channel_id=1, source_target_pairs={{0,1},{1,0},{2,3},{3,2},{4,5},{5,4},{6,7},{7,6},{8,9},{9,8},{10,11... | collective-permute-start | bytes 1671176 | tf_op jit(solution)/shard_map/ppermute | solution.py:34
  110.8 2.8 %collective-permute-start.18 = (bf16[128,2176]{1,0:T(8,128)(2,1)S(1)}, bf16[128,2176]{1,0:T(8,128)(2,1)S(1)}, u32[]{:S(2)}, u32[]{:S(2)}) collective-permute-start(bf16[128,2176]{1,0:T(8,128)(2,1)S(1)} %collective-permute-done.11.refs_5_), channel_id=1, source_target_pairs={{0,1},{1,0},{2,3},{3,2},{4,5},{5,4},{6,7},{7,6},{8,9},{9,8},{10,11... | collective-permute-start | bytes 1671176 | tf_op jit(solution)/shard_map/ppermute | solution.py:34
  111.3 14.5 %collective-permute-start.15 = (bf16[128,2176]{1,0:T(8,128)(2,1)S(1)}, bf16[128,2176]{1,0:T(8,128)(2,1)S(1)}, u32[]{:S(2)}, u32[]{:S(2)}) collective-permute-start(bf16[128,2176]{1,0:T(8,128)(2,1)S(1)} %collective-permute-done.10.refs_3_), channel_id=1, source_target_pairs={{0,4},{4,8},{8,12},{12,14},{14,10},{10,6},{6,2},{2,0},{1,5},{5,9},... | collective-permute-start | bytes 1671176 | tf_op jit(solution)/shard_map/ppermute | solution.py:42
  112.8 14.3 %collective-permute-start.16 = (bf16[128,2176]{1,0:T(8,128)(2,1)S(1)}, bf16[128,2176]{1,0:T(8,128)(2,1)S(1)}, u32[]{:S(2)}, u32[]{:S(2)}) collective-permute-start(bf16[128,2176]{1,0:T(8,128)(2,1)S(1)} %collective-permute-done.11.refs_5_), channel_id=1, source_target_pairs={{0,2},{4,0},{8,4},{12,8},{14,12},{10,14},{6,10},{2,6},{1,3},{5,1},... | collective-permute-start | bytes 1671176 | tf_op jit(solution)/shard_map/ppermute | solution.py:42
  113.6 13.5 %collective-permute-start.19 = (bf16[128,2048]{1,0:T(8,128)(2,1)S(1)}, bf16[128,2048]{1,0:T(8,128)(2,1)S(1)}, u32[]{:S(2)}, u32[]{:S(2)}) collective-permute-start(bf16[128,2048]{1,0:T(8,128)(2,1)S(1)} %get-tuple-element.148), channel_id=1, source_target_pairs={{0,1},{1,0},{2,3},{3,2},{4,5},{5,4},{6,7},{7,6},{8,9},{9,8},{10,11... | collective-permute-start | bytes 1572872 | tf_op jit(solution)/shard_map/ppermute | solution.py:34
  113.7 13.3 %collective-permute-start.20 = (bf16[128,2048]{1,0:T(8,128)(2,1)S(1)}, bf16[128,2048]{1,0:T(8,128)(2,1)S(1)}, u32[]{:S(2)}, u32[]{:S(2)}) collective-permute-start(bf16[128,2048]{1,0:T(8,128)(2,1)S(1)} %get-tuple-element.150), channel_id=1, source_target_pairs={{0,1},{1,0},{2,3},{3,2},{4,5},{5,4},{6,7},{7,6},{8,9},{9,8},{10,11... | collective-permute-start | bytes 1572872 | tf_op jit(solution)/shard_map/ppermute | solution.py:34
  127.0 2.0 collective-permute-start.23
  127.0 3.2 %collective-permute-start.24 = (bf16[128,2176]{1,0:T(8,128)(2,1)S(1)}, bf16[128,2176]{1,0:T(8,128)(2,1)S(1)}, u32[]{:S(2)}, u32[]{:S(2)}) collective-permute-start(bf16[128,2176]{1,0:T(8,128)(2,1)S(1)} %collective-permute-done.16.refs_5_), channel_id=1, source_target_pairs={{0,1},{1,0},{2,3},{3,2},{4,5},{5,4},{6,7},{7,6},{8,9},{9,8},{10,11... | collective-permute-start | bytes 1671176 | tf_op jit(solution)/shard_map/ppermute | solution.py:34
  127.6 10.1 %collective-permute-start.25 = (bf16[128,2048]{1,0:T(8,128)(2,1)S(1)}, bf16[128,2048]{1,0:T(8,128)(2,1)S(1)}, u32[]{:S(2)}, u32[]{:S(2)}) collective-permute-start(bf16[128,2048]{1,0:T(8,128)(2,1)S(1)} %get-tuple-element.162), channel_id=1, source_target_pairs={{0,1},{1,0},{2,3},{3,2},{4,5},{5,4},{6,7},{7,6},{8,9},{9,8},{10,11... | collective-permute-start | bytes 1572872 | tf_op jit(solution)/shard_map/ppermute | solution.py:34
  127.6 10.1 %collective-permute-start.26 = (bf16[128,2048]{1,0:T(8,128)(2,1)S(1)}, bf16[128,2048]{1,0:T(8,128)(2,1)S(1)}, u32[]{:S(2)}, u32[]{:S(2)}) collective-permute-start(bf16[128,2048]{1,0:T(8,128)(2,1)S(1)} %get-tuple-element.164), channel_id=1, source_target_pairs={{0,1},{1,0},{2,3},{3,2},{4,5},{5,4},{6,7},{7,6},{8,9},{9,8},{10,11... | collective-permute-start | bytes 1572872 | tf_op jit(solution)/shard_map/ppermute | solution.py:34
  128.1 8.7 %collective-permute-start.21 = (bf16[64,2176]{1,0:T(8,128)(2,1)S(1)}, bf16[64,2176]{1,0:T(8,128)(2,1)S(1)}, u32[]{:S(2)}, u32[]{:S(2)}) collective-permute-start(bf16[64,2176]{1,0:T(8,128)(2,1)S(1)} %slice.98), channel_id=1, source_target_pairs={{0,4},{4,8},{8,12},{12,14},{14,10},{10,6},{6,2},{2,0},{1,5},{5,9},... | collective-permute-start | bytes 835592 | tf_op jit(solution)/shard_map/ppermute | solution.py:42
  129.0 8.7 %collective-permute-start.22 = (bf16[64,2176]{1,0:T(8,128)(2,1)S(1)}, bf16[64,2176]{1,0:T(8,128)(2,1)S(1)}, u32[]{:S(2)}, u32[]{:S(2)}) collective-permute-start(bf16[64,2176]{1,0:T(8,128)(2,1)S(1)} %slice.99), channel_id=1, source_target_pairs={{0,2},{4,0},{8,4},{12,8},{14,12},{10,14},{6,10},{2,6},{1,3},{5,1},... | collective-permute-start | bytes 835592 | tf_op jit(solution)/shard_map/ppermute | solution.py:42
  137.7 1.6 collective-permute-start.27
  137.7 1.9 collective-permute-start.28
  139.7 3.1 %collective-permute-start.29 = (bf16[128,2048]{1,0:T(8,128)(2,1)S(1)}, bf16[128,2048]{1,0:T(8,128)(2,1)S(1)}, u32[]{:S(2)}, u32[]{:S(2)}) collective-permute-start(bf16[128,2048]{1,0:T(8,128)(2,1)S(1)} %get-tuple-element.184), channel_id=1, source_target_pairs={{0,1},{1,0},{2,3},{3,2},{4,5},{5,4},{6,7},{7,6},{8,9},{9,8},{10,11... | collective-permute-start | bytes 1572872 | tf_op jit(solution)/shard_map/ppermute | solution.py:34
  139.8 3.0 %collective-permute-start.30 = (bf16[128,2048]{1,0:T(8,128)(2,1)S(1)}, bf16[128,2048]{1,0:T(8,128)(2,1)S(1)}, u32[]{:S(2)}, u32[]{:S(2)}) collective-permute-start(bf16[128,2048]{1,0:T(8,128)(2,1)S(1)} %get-tuple-element.186), channel_id=1, source_target_pairs={{0,1},{1,0},{2,3},{3,2},{4,5},{5,4},{6,7},{7,6},{8,9},{9,8},{10,11... | collective-permute-start | bytes 1572872 | tf_op jit(solution)/shard_map/ppermute | solution.py:34
  142.8 2.0 %collective-permute-start.31 = (bf16[128,2048]{1,0:T(8,128)(2,1)S(1)}, bf16[128,2048]{1,0:T(8,128)(2,1)S(1)}, u32[]{:S(2)}, u32[]{:S(2)}) collective-permute-start(bf16[128,2048]{1,0:T(8,128)(2,1)S(1)} %get-tuple-element.200), channel_id=1, source_target_pairs={{0,1},{1,0},{2,3},{3,2},{4,5},{5,4},{6,7},{7,6},{8,9},{9,8},{10,11... | collective-permute-start | bytes 1572872 | tf_op jit(solution)/shard_map/ppermute | solution.py:34
  144.9 9.2 %collective-permute-start.42 = (bf16[64,2048]{1,0:T(8,128)(2,1)S(1)}, bf16[64,2048]{1,0:T(8,128)(2,1)S(1)}, u32[]{:S(2)}, u32[]{:S(2)}) collective-permute-start(bf16[64,2048]{1,0:T(8,128)(2,1)S(1)} %get-tuple-element.219), channel_id=1, source_target_pairs={{0,2},{4,0},{8,4},{12,8},{14,12},{10,14},{6,10},{2,6},{1,3},{5,1},... | collective-permute-start | bytes 786440 | tf_op jit(solution)/shard_map/ppermute | solution.py:42
  145.9 9.2 %collective-permute-start.39 = (bf16[64,2048]{1,0:T(8,128)(2,1)S(1)}, bf16[64,2048]{1,0:T(8,128)(2,1)S(1)}, u32[]{:S(2)}, u32[]{:S(2)}) collective-permute-start(bf16[64,2048]{1,0:T(8,128)(2,1)S(1)} %add_convert_fusion.6), channel_id=1, source_target_pairs={{0,4},{4,8},{8,12},{12,14},{14,10},{10,6},{6,2},{2,0},{1,5},{5,9},... | collective-permute-start | bytes 786440 | tf_op jit(solution)/shard_map/ppermute | solution.py:42
  147.2 12.5 %collective-permute-start.36 = (bf16[64,2048]{1,0:T(8,128)(2,1)S(1)}, bf16[64,2048]{1,0:T(8,128)(2,1)S(1)}, u32[]{:S(2)}, u32[]{:S(2)}) collective-permute-start(bf16[64,2048]{1,0:T(8,128)(2,1)S(1)} %add_convert_fusion.9), channel_id=1, source_target_pairs={{0,2},{4,0},{8,4},{12,8},{14,12},{10,14},{6,10},{2,6},{1,3},{5,1},... | collective-permute-start | bytes 786440 | tf_op jit(solution)/shard_map/ppermute | solution.py:42
  148.1 12.7 %collective-permute-start.32 = (bf16[64,2048]{1,0:T(8,128)(2,1)S(1)}, bf16[64,2048]{1,0:T(8,128)(2,1)S(1)}, u32[]{:S(2)}, u32[]{:S(2)}) collective-permute-start(bf16[64,2048]{1,0:T(8,128)(2,1)S(1)} %get-tuple-element.220), channel_id=1, source_target_pairs={{0,4},{4,8},{8,12},{12,14},{14,10},{10,6},{6,2},{2,0},{1,5},{5,9},... | collective-permute-start | bytes 786440 | tf_op jit(solution)/shard_map/ppermute | solution.py:42
  154.2 11.1 %collective-permute-start.43 = (bf16[64,2048]{1,0:T(8,128)(2,1)S(1)}, bf16[64,2048]{1,0:T(8,128)(2,1)S(1)}, u32[]{:S(2)}, u32[]{:S(2)}) collective-permute-start(bf16[64,2048]{1,0:T(8,128)(2,1)S(1)} %add_convert_fusion.2), channel_id=1, source_target_pairs={{0,2},{4,0},{8,4},{12,8},{14,12},{10,14},{6,10},{2,6},{1,3},{5,1},... | collective-permute-start | bytes 786440 | tf_op jit(solution)/shard_map/ppermute | solution.py:42
  155.2 11.1 %collective-permute-start.40 = (bf16[64,2048]{1,0:T(8,128)(2,1)S(1)}, bf16[64,2048]{1,0:T(8,128)(2,1)S(1)}, u32[]{:S(2)}, u32[]{:S(2)}) collective-permute-start(bf16[64,2048]{1,0:T(8,128)(2,1)S(1)} %add_convert_fusion.5), channel_id=1, source_target_pairs={{0,4},{4,8},{8,12},{12,14},{14,10},{10,6},{6,2},{2,0},{1,5},{5,9},... | collective-permute-start | bytes 786440 | tf_op jit(solution)/shard_map/ppermute | solution.py:42
  159.8 11.1 %collective-permute-start.37 = (bf16[64,2048]{1,0:T(8,128)(2,1)S(1)}, bf16[64,2048]{1,0:T(8,128)(2,1)S(1)}, u32[]{:S(2)}, u32[]{:S(2)}) collective-permute-start(bf16[64,2048]{1,0:T(8,128)(2,1)S(1)} %add_convert_fusion.8), channel_id=1, source_target_pairs={{0,2},{4,0},{8,4},{12,8},{14,12},{10,14},{6,10},{2,6},{1,3},{5,1},... | collective-permute-start | bytes 786440 | tf_op jit(solution)/shard_map/ppermute | solution.py:42
  160.9 11.1 %collective-permute-start.33 = (bf16[64,2048]{1,0:T(8,128)(2,1)S(1)}, bf16[64,2048]{1,0:T(8,128)(2,1)S(1)}, u32[]{:S(2)}, u32[]{:S(2)}) collective-permute-start(bf16[64,2048]{1,0:T(8,128)(2,1)S(1)} %add_convert_fusion.12), channel_id=1, source_target_pairs={{0,4},{4,8},{8,12},{12,14},{14,10},{10,6},{6,2},{2,0},{1,5},{5,9},... | collective-permute-start | bytes 786440 | tf_op jit(solution)/shard_map/ppermute | solution.py:42
  165.5 11.1 %collective-permute-start.44 = (bf16[64,2048]{1,0:T(8,128)(2,1)S(1)}, bf16[64,2048]{1,0:T(8,128)(2,1)S(1)}, u32[]{:S(2)}, u32[]{:S(2)}) collective-permute-start(bf16[64,2048]{1,0:T(8,128)(2,1)S(1)} %add_convert_fusion.1), channel_id=1, source_target_pairs={{0,2},{4,0},{8,4},{12,8},{14,12},{10,14},{6,10},{2,6},{1,3},{5,1},... | collective-permute-start | bytes 786440 | tf_op jit(solution)/shard_map/ppermute | solution.py:42
  166.5 17.0 %collective-permute-start.41 = (bf16[64,2048]{1,0:T(8,128)(2,1)S(1)}, bf16[64,2048]{1,0:T(8,128)(2,1)S(1)}, u32[]{:S(2)}, u32[]{:S(2)}) collective-permute-start(bf16[64,2048]{1,0:T(8,128)(2,1)S(1)} %add_convert_fusion.4), channel_id=1, source_target_pairs={{0,4},{4,8},{8,12},{12,14},{14,10},{10,6},{6,2},{2,0},{1,5},{5,9},... | collective-permute-start | bytes 786440 | tf_op jit(solution)/shard_map/ppermute | solution.py:42
  171.1 12.4 %collective-permute-start.38 = (bf16[64,2048]{1,0:T(8,128)(2,1)S(1)}, bf16[64,2048]{1,0:T(8,128)(2,1)S(1)}, u32[]{:S(2)}, u32[]{:S(2)}) collective-permute-start(bf16[64,2048]{1,0:T(8,128)(2,1)S(1)} %add_convert_fusion.7), channel_id=1, source_target_pairs={{0,2},{4,0},{8,4},{12,8},{14,12},{10,14},{6,10},{2,6},{1,3},{5,1},... | collective-permute-start | bytes 786440 | tf_op jit(solution)/shard_map/ppermute | solution.py:42
  172.1 10.0 %collective-permute-start.34 = (bf16[64,2048]{1,0:T(8,128)(2,1)S(1)}, bf16[64,2048]{1,0:T(8,128)(2,1)S(1)}, u32[]{:S(2)}, u32[]{:S(2)}) collective-permute-start(bf16[64,2048]{1,0:T(8,128)(2,1)S(1)} %add_convert_fusion.11), channel_id=1, source_target_pairs={{0,4},{4,8},{8,12},{12,14},{14,10},{10,6},{6,2},{2,0},{1,5},{5,9},... | collective-permute-start | bytes 786440 | tf_op jit(solution)/shard_map/ppermute | solution.py:42
  176.7 10.3 %collective-permute-start.45 = (bf16[64,2048]{1,0:T(8,128)(2,1)S(1)}, bf16[64,2048]{1,0:T(8,128)(2,1)S(1)}, u32[]{:S(2)}, u32[]{:S(2)}) collective-permute-start(bf16[64,2048]{1,0:T(8,128)(2,1)S(1)} %add_convert_fusion), channel_id=1, source_target_pairs={{0,2},{4,0},{8,4},{12,8},{14,12},{10,14},{6,10},{2,6},{1,3},{5,1},... | collective-permute-start | bytes 786440 | tf_op jit(solution)/shard_map/ppermute | solution.py:42
  182.2 7.3 %collective-permute-start.35 = (bf16[64,2048]{1,0:T(8,128)(2,1)S(1)}, bf16[64,2048]{1,0:T(8,128)(2,1)S(1)}, u32[]{:S(2)}, u32[]{:S(2)}) collective-permute-start(bf16[64,2048]{1,0:T(8,128)(2,1)S(1)} %add_convert_fusion.10), channel_id=1, source_target_pairs={{0,4},{4,8},{8,12},{12,14},{14,10},{10,6},{6,2},{2,0},{1,5},{5,9},... | collective-permute-start | bytes 786440 | tf_op jit(solution)/shard_map/ppermute | solution.py:42
  (12 other events, 71.9 us)
Sparse Core Ops, SparseCore 0:
  8.9 50.5 all-gather.1
